TPU v7x, 512 devices: a whole 4x8x8 slice. The times are simulated.
512 devices in a mesh: aux: 128 (over z, y, core), orb: 4 (over x).
Axes of the slice: x: 4, y: 8, z: 8, core: 2. Of those that a mesh axis runs over, the one named last changes fastest.
Arguments:
- half_integrals: bfloat16 [128, 32768, 128], P('orb', 'aux'), may hold values from -1.11488167 to 1.11488167
- domain_map: bfloat16 [128, 128, 128], P('orb'), may hold values from -0.5 to 0.5
- domain_index: int32 [128, 128], replicated, may hold values from -1 to 24999, as said below
- owner_orbitals: int32 [128, 4], replicated, may hold values from 0 to 127, as said below
- pair_slots: int32 [2048, 2], P('aux'), may hold values from 0 to 3, as said below
- pair_weight: int32 [2048], P('aux'), may hold values from 0 to 2, as said below
- virtual_energy: float32 [25000], replicated, may hold values from 0.2 to 3
- occupied_energy: float32 [128], replicated, may hold values from -2 to -0.5
Outputs:
- amplitude: bfloat16 [2048, 128, 128], P(('aux', 'orb'))
- pair_energy: float32 [2048], P(('aux', 'orb'))
- domain_grad: float32 [128, 128], P('orb')
Inputs may be any that keep to these rules, and one draw needn't show every extreme that they name: `domain_index`: each orbital's live slots come first and the rest are -1; some orbital's domain has all 128 slots live. `owner_orbitals`: entry g (g = 0 to 3) of an owner's list is an orbital of group g, that is g * 32 to (g + 1) * 32 - 1; the entries of one owner are distinct. `pair_slots`: the two positions of a row may be equal; no ordered pair of positions stands twice among one owner's rows. `pair_weight`: in each owner's 16 rows the live pairs (weight 1 or 2) come first and the rest have weight 0; every owner has a live pair and some owner has all 16 live.
All inputs are finite; a program needn't handle non-finite values.
Results may differ from a plain program's by a relative error of at most 0.0034.
Values may be sent and summed in bfloat16 or wider, within the bound.
No kernel may reach another device: no remote copies, remote signals or barrier semaphores. Data moves between devices by JAX's collectives and lax.ppermute only.
A program may use at most 64 MiB of HBM per device.

v0:
```python
import jax
import jax.numpy as jnp
from jax import lax
from jax.sharding import PartitionSpec as P


def on_device(
    half_integrals,
    domain_map,
    domain_index,
    owner_orbitals,
    pair_slots,
    pair_weight,
    virtual_energy,
    occupied_energy,
):
    orb_group = lax.axis_index("orb")
    group_count = lax.axis_size("orb")
    occ_local = half_integrals.shape[0]
    width = half_integrals.shape[2]
    total_occ = domain_index.shape[0]
    list_width = owner_orbitals.shape[1]
    per_group = list_width // group_count
    local_index = lax.dynamic_slice_in_dim(domain_index, orb_group * occ_local, occ_local, 0)
    live_mask = (local_index >= 0).astype(jnp.float32)
    product = jnp.einsum(
        "opm,oma->opa", half_integrals, domain_map, preferred_element_type=jnp.float32
    )
    domain_slabs = (product * live_mask[:, None, :]).astype(jnp.bfloat16)
    own_local = (
        lax.dynamic_slice_in_dim(owner_orbitals, orb_group * per_group, per_group, 1)
        - orb_group * occ_local
    )
    outgoing = domain_slabs[own_local.T]
    received = lax.all_to_all(
        lax.all_to_all(outgoing, "aux", split_axis=1, concat_axis=1, tiled=True),
        "orb",
        split_axis=2,
        concat_axis=0,
        tiled=True,
    )
    slot_slabs = received.reshape(list_width, -1, width)

    def one_block(slot_pair):
        left_slab = slot_slabs[slot_pair[0]]
        right_slab = slot_slabs[slot_pair[1]]
        return lax.dot_general(
            left_slab, right_slab, (((0,), (0,)), ((), ())), preferred_element_type=jnp.float32
        )

    share = pair_slots.shape[0] // group_count
    pair_block = lax.psum_scatter(
        lax.map(one_block, pair_slots), "orb", scatter_dimension=0, tiled=True
    )
    owner_rank = lax.axis_index("aux")
    my_orbitals = owner_orbitals[owner_rank]
    my_slots = lax.dynamic_slice_in_dim(pair_slots, orb_group * share, share, 0)
    my_weight = lax.dynamic_slice_in_dim(pair_weight, orb_group * share, share, 0)
    first_orb = my_orbitals[my_slots[:, 0]]
    second_orb = my_orbitals[my_slots[:, 1]]
    first_index = domain_index[first_orb]
    second_index = domain_index[second_orb]
    virt_count = virtual_energy.shape[0]
    first_level = jnp.where(
        first_index >= 0, virtual_energy[jnp.clip(first_index, 0, virt_count - 1)], jnp.float32(1.0)
    )
    second_level = jnp.where(
        second_index >= 0,
        virtual_energy[jnp.clip(second_index, 0, virt_count - 1)],
        jnp.float32(1.0),
    )
    denominator = (
        first_level[:, :, None]
        + second_level[:, None, :]
        - occupied_energy[first_orb][:, None, None]
        - occupied_energy[second_orb][:, None, None]
    )
    amp_ratio = pair_block / denominator
    weight_float = my_weight.astype(jnp.float32)
    live_pair = (my_weight > 0).astype(jnp.float32)
    amplitude = (-amp_ratio * live_pair[:, None, None]).astype(jnp.bfloat16)
    pair_energy = -weight_float * jnp.sum(pair_block * amp_ratio, axis=(1, 2)) / (width * width)
    squares = amp_ratio * amp_ratio
    row_grad = weight_float[:, None] * jnp.sum(squares, axis=2) / width
    col_grad = weight_float[:, None] * jnp.sum(squares, axis=1) / width
    orbital_ids = jnp.arange(total_occ)
    first_onehot = (first_orb[:, None] == orbital_ids[None, :]).astype(jnp.float32)
    second_onehot = (second_orb[:, None] == orbital_ids[None, :]).astype(jnp.float32)
    grad_part = jnp.dot(
        first_onehot.T,
        row_grad,
        preferred_element_type=jnp.float32,
        precision=lax.Precision.HIGHEST,
    )
    grad_part = grad_part + jnp.dot(
        second_onehot.T,
        col_grad,
        preferred_element_type=jnp.float32,
        precision=lax.Precision.HIGHEST,
    )
    summed = lax.psum(grad_part, "aux")
    domain_grad = lax.psum_scatter(summed, "orb", scatter_dimension=0, tiled=True)
    return (amplitude, pair_energy, domain_grad)


def solution(mesh):
    placed = (
        P("orb", "aux", None),
        P("orb", None, None),
        P(),
        P(),
        P("aux", None),
        P("aux"),
        P(),
        P(),
    )
    return jax.shard_map(
        on_device,
        mesh=mesh,
        in_specs=placed,
        out_specs=(P(("aux", "orb"), None, None), P(("aux", "orb")), P("orb", None)),
        check_vma=False,
    )
```

profile of v0, /device:TPU:1, one launch (start us, length us, event | category | flops | bytes accessed | tf_op | source)
XLA Modules:
  0.0 1042.3 jit_solution(16945820670603174913)
XLA Ops:
  12.1 8.1 gather_fusion
  20.2 209.2 %all_to_all.20 = bf16[1,128,256,128]{3,2,0,1:T(8,128)(2,1)} all-to-all(bf16[1,128,256,128]{3,2,0,1:T(8,128)(2,1)} %bitcast.70), channel_id=1, replica_groups=mesh['aux'=128,'orb'=4] {'aux'}, dimensions={1} | all-to-all | bytes 16777216 | tf_op jit(solution)/shard_map/all_to_all | solution.py:36
  229.4 12.0 %copy.14 = bf16[1,128,256,128]{3,1,0,2:T(8,128)(2,1)} copy(bf16[1,128,256,128]{3,2,0,1:T(8,128)(2,1)} %all_to_all.20) | data formatting | bytes 16777216 | tf_op jit(solution)/shard_map/all_to_all | solution.py:36
  241.4 5.8 all-to-all-start.1
  247.8 93.4 %all-to-all-done.1 = bf16[1,128,256,128]{3,1,0,2:T(8,128)(2,1)} async-done(((bf16[1,128,256,128]{3,1,0,2:T(8,128)(2,1)}), bf16[1,128,256,128]{3,1,0,2:T(8,128)(2,1)}, u32[]{:S(2)}, u32[]{:S(2)}) %all-to-all-start.1) | async-done | bytes 8388640 | tf_op jit(solution)/shard_map/all_to_all | solution.py:35
  341.2 12.0 %copy.15 = bf16[4,1,128,64,128]{4,3,2,0,1:T(8,128)(2,1)} copy(bf16[4,1,128,64,128]{4,2,3,0,1:T(8,128)(2,1)} %bitcast.10) | data formatting | bytes 16777216 | tf_op jit(solution)/shard_map/all_to_all | solution.py:35
  353.2 129.3 %while.10 = (s32[]{:T(128)}, f32[16,128,128]{2,1,0:T(8,128)}, s32[16,2]{0,1:T(2,128)S(1)}, bf16[4,8192,128]{2,1,0:T(8,128)(2,1)}, s32[]{:T(128)}, /*index=5*/s32[]{:T(128)}, s32[]{:T(128)}) while((s32[]{:T(128)}, f32[16,128,128]{2,1,0:T(8,128)}, s32[16,2]{0,1:T(2,128)S(1)}, bf16[4,8192,128]{2,1,0:T(8,128)(2,1)}, s32[]{:T(128)}, ...), condition=%wide.region_1.2_spmd, body=%wide.region_0.1_spmd.sunk | while | flops 268435456 | bytes 4260541 | solution.py:53
  357.7 3.6 fusion.49
  365.7 3.6 fusion.49
  373.8 3.6 fusion.49
  381.9 3.6 fusion.49
  390.0 3.6 fusion.49
  398.1 3.6 fusion.49
  422.3 3.6 fusion.49
  430.4 3.6 fusion.49
  438.5 3.6 fusion.49
  446.6 3.6 fusion.49
  454.6 3.6 fusion.49
  462.7 3.6 fusion.49
  470.8 3.6 fusion.49
  478.9 3.6 fusion.49
  492.8 23.1 %reduce-scatter.3.cloned.1.call-done = f32[4,128,128]{2,1,0:T(8,128)} async-done(((f32[16,128,128]{2,1,0:T(8,128)}), f32[4,128,128]{2,1,0:T(8,128)}) %reduce-scatter.3.cloned.1.call-update) | async-done | bytes 262160 | tf_op jit(solution)/shard_map/reduce_scatter | solution.py:52
  519.9 24.0 %reduce-scatter.5.cloned.1.call-done = f32[32,128]{1,0:T(8,128)} async-done(((f32[128,128]{1,0:T(8,128)}), f32[32,128]{1,0:T(8,128)}) %reduce-scatter.5.cloned.1.call-update) | async-done | bytes 16400 | tf_op jit(solution)/shard_map/reduce_scatter | solution.py:102
  543.9 491.5 %psum.8 = f32[32,128]{1,0:T(8,128)} all-reduce(f32[32,128]{1,0:T(8,128)} %reduce-scatter.5.cloned.1.call-done), channel_id=1, replica_groups=mesh['aux'=128,'orb'=4] {'aux'}, use_global_device_ids=true, to_apply=%region_6.7 | all-reduce | flops 4096 | bytes 32768 | tf_op jit(solution)/shard_map/psum | solution.py:101
  (85 shorter events, 36.2 us)
Async XLA Ops:
  7.2 1.6 copy-start
  241.4 6.1 copy-start.5
  241.4 6.3 copy-start.4
  241.4 99.7 %all-to-all-start.1 = ((bf16[1,128,256,128]{3,1,0,2:T(8,128)(2,1)}), bf16[1,128,256,128]{3,1,0,2:T(8,128)(2,1)}, u32[]{:S(2)}, u32[]{:S(2)}) async-start(bf16[1,128,256,128]{3,1,0,2:T(8,128)(2,1)} %copy.14), calls=%async_computation.1 | async-start | bytes 16777216 | tf_op jit(solution)/shard_map/all_to_all | solution.py:35
  247.3 268.7 %reduce-scatter.3.cloned.1.call-start = ((), (), s32[]{:S(2)}) async-start(), calls=%async_computation.4 | async-start | bytes 1310720 | tf_op jit(solution)/shard_map/reduce_scatter | solution.py:52
  353.2 130.7 %copy-start.3 = (s32[128,128]{1,0:T(8,128)S(1)}, s32[128,128]{1,0:T(8,128)}, u32[]{:S(2)}) copy-start(s32[128,128]{1,0:T(8,128)} %param.12) | copy-start | bytes 196612
  353.2 131.9 %copy-start.1 = (f32[128]{0:T(128)S(1)}, f32[128]{0:T(128)}, u32[]{:S(2)}) copy-start(f32[128]{0:T(128)} %param.17) | copy-start | bytes 1540
  482.5 3.9 copy-start.2
  482.5 10.2 copy-start.6
  482.5 61.4 %reduce-scatter.5.cloned.1.call-start = ((), (), s32[]{:S(2)}) async-start(), calls=%async_computation.5 | async-start | bytes 81920 | tf_op jit(solution)/shard_map/reduce_scatter | solution.py:102
Sparse Core Ops, SparseCore 0:
  482.7 33.2 reduce-scatter.2
  519.3 24.6 reduce-scatter.4
where the time goes:
time: 1050 us; the launch traced here: 1040 us
  blocking collectives  701 us (67%)
  waiting for transfers between devices  141 us (13%)
  matrix products  62.3 us (6%)
  loops' own time  62.1 us (6%)
  local copies, waits for them, and re-layouts  51.9 us (5%)
  between operations  14.2 us (1%)
    psum x1, blocking collectives, on_device(): summed = lax.psum(grad_part, 'aux')  491 us
    all_to_all x1, blocking collectives, on_device(): lax.all_to_all(outgoing, 'aux', split_axis=1, concat_axis=1, tiled=True)  209 us
    all_to_all x1, waiting for transfers between devices, on_device(): lax.all_to_all(lax.all_to_all(outgoing, 'aux', split_axis=1, concat_axis=...  93.4 us
    another operation x1, loops' own time, on_device(): lax.map(one_block, pair_slots)  62.1 us
    dot_general x16, matrix products, one_block(): lax.dot_general(left_slab, right_slab, (((0,), (0,)), ((), ())), preferre...  57.7 us
    reduce_scatter x1, waiting for transfers between devices, on_device(): lax.psum_scatter(summed, 'orb', scatter_dimension=0, tiled=True)  24 us
    reduce_scatter x1, waiting for transfers between devices, on_device(): lax.psum_scatter(lax.map(one_block, pair_slots), 'orb', scatter_dimension...  23.1 us
  transfers between devices with their start and end apart: 3, of which 3 were waited for; matrix products, arithmetic and copies ran while one was open for 1% of the time, Pallas kernels for 0%

commit v1 on v0

v1 whole, which is shorter than its diff:
```python
import jax
import jax.numpy as jnp
from jax import lax
from jax.experimental import pallas as pl
from jax.experimental.pallas import tpu as pltpu
from jax.sharding import PartitionSpec as P

F32 = jnp.float32
VMEM_LIMIT = 48 * 1024 * 1024
OWNERS_PER_STEP = 8
AUX_PER_STEP = 16


def slab_kernel(scalars, integral_ref, map_ref, index_ref, out_ref, slab_ref):
    occ_local = integral_ref.shape[0]
    per_step = out_ref.shape[0]
    step = pl.program_id(0)
    group = scalars[0]

    @pl.when(step == 0)
    def _():
        for orb in range(occ_local):
            product = jnp.dot(integral_ref[orb], map_ref[orb], preferred_element_type=F32)
            live = (index_ref[pl.ds(group * occ_local + orb, 1), :] >= 0).astype(F32)
            slab_ref[orb] = (product * live).astype(jnp.bfloat16)

    for k in range(per_step):
        out_ref[k] = slab_ref[scalars[1 + step * per_step + k]]


def make_slabs(half_integrals, domain_map, domain_index, own_local, orb_group):
    occ_local, rows, width = half_integrals.shape
    owners = own_local.shape[0]
    scalars = jnp.concatenate([orb_group[None].astype(jnp.int32), own_local])
    whole = lambda shape: pl.BlockSpec(shape, lambda i, s: (0,) * len(shape))
    return pl.pallas_call(
        slab_kernel,
        out_shape=jax.ShapeDtypeStruct((owners, rows, width), jnp.bfloat16),
        grid_spec=pltpu.PrefetchScalarGridSpec(
            num_scalar_prefetch=1,
            grid=(owners // OWNERS_PER_STEP,),
            in_specs=[
                whole(half_integrals.shape),
                whole(domain_map.shape),
                whole(domain_index.shape),
            ],
            out_specs=pl.BlockSpec((OWNERS_PER_STEP, rows, width), lambda i, s: (i, 0, 0)),
            scratch_shapes=[pltpu.VMEM((occ_local, rows, width), jnp.bfloat16)],
        ),
        compiler_params=pltpu.CompilerParams(vmem_limit_bytes=VMEM_LIMIT),
        name="slabs",
    )(scalars, half_integrals, domain_map, domain_index)


def gram_kernel(slots, slab_ref, out_ref, gram_ref):
    step = pl.program_id(0)
    count, list_width, rows, width = slab_ref.shape
    joined = jnp.concatenate(
        [slab_ref[:, g].reshape(count * rows, width) for g in range(list_width)], axis=1
    )
    part = lax.dot_general(joined, joined, (((0,), (0,)), ((), ())), preferred_element_type=F32)

    @pl.when(step == 0)
    def _():
        gram_ref[...] = part

    @pl.when(step > 0)
    def _():
        gram_ref[...] += part

    @pl.when(step == pl.num_programs(0) - 1)
    def _():
        for pair in range(out_ref.shape[0]):
            left = pl.multiple_of(slots[pair, 0] * width, width)
            right = pl.multiple_of(slots[pair, 1] * width, width)
            out_ref[pair] = gram_ref[pl.ds(left, width), pl.ds(right, width)]


def pair_blocks(slabs, pair_slots):
    aux, list_width, rows, width = slabs.shape
    pairs = pair_slots.shape[0]
    return pl.pallas_call(
        gram_kernel,
        out_shape=jax.ShapeDtypeStruct((pairs, width, width), F32),
        grid_spec=pltpu.PrefetchScalarGridSpec(
            num_scalar_prefetch=1,
            grid=(aux // AUX_PER_STEP,),
            in_specs=[
                pl.BlockSpec((AUX_PER_STEP, list_width, rows, width), lambda i, s: (i, 0, 0, 0))
            ],
            out_specs=pl.BlockSpec((pairs, width, width), lambda i, s: (0, 0, 0)),
            scratch_shapes=[pltpu.VMEM((list_width * width, list_width * width), F32)],
        ),
        compiler_params=pltpu.CompilerParams(vmem_limit_bytes=VMEM_LIMIT),
        name="pair_blocks",
    )(pair_slots, slabs)


def pair_kernel(slots, weights, occupied, first_pair, part_ref, level_ref, amp_ref, energy_ref, grad_ref, acc_ref):
    groups, share, width, _ = part_ref.shape
    list_width = level_ref.shape[0]
    acc_ref[...] = jnp.zeros_like(acc_ref)
    base = first_pair[0]
    for pair in range(share):
        left = slots[base + pair, 0]
        right = slots[base + pair, 1]
        weight_int = weights[base + pair]
        block = part_ref[0, pair]
        for g in range(1, groups):
            block = block + part_ref[g, pair]
        left_level = jnp.broadcast_to(level_ref[pl.ds(left, 1), :], (width, width)).T
        right_level = level_ref[pl.ds(right, 1), :]
        denominator = left_level + right_level - occupied[left] - occupied[right]
        ratio = block / denominator
        live = (weight_int > 0).astype(F32)
        weight = weight_int.astype(F32)
        amp_ref[pair] = (-ratio * live).astype(jnp.bfloat16)
        energy_ref[pair] = -weight * jnp.sum(block * ratio) / (width * width)
        squares = ratio * ratio
        scale = weight / width
        acc_ref[pl.ds(left, 1), :] += scale * jnp.sum(squares.T, axis=0, keepdims=True)
        acc_ref[pl.ds(right, 1), :] += scale * jnp.sum(squares, axis=0, keepdims=True)
    terms = acc_ref[...]
    for k in range(grad_ref.shape[0] // list_width):
        grad_ref[pl.ds(k * list_width, list_width), :] = terms


def pair_terms(parts, levels, pair_slots, pair_weight, occupied, first_pair, copies):
    groups, share, width, _ = parts.shape
    list_width = levels.shape[0]
    whole = pl.BlockSpec(memory_space=pltpu.VMEM)
    scalar = pl.BlockSpec(memory_space=pltpu.SMEM)
    return pl.pallas_call(
        pair_kernel,
        out_shape=(
            jax.ShapeDtypeStruct((share, width, width), jnp.bfloat16),
            jax.ShapeDtypeStruct((share,), F32),
            jax.ShapeDtypeStruct((copies * list_width, width), F32),
        ),
        in_specs=[scalar, scalar, scalar, scalar, whole, whole],
        out_specs=(whole, scalar, whole),
        scratch_shapes=[pltpu.VMEM((list_width, width), F32)],
        compiler_params=pltpu.CompilerParams(vmem_limit_bytes=VMEM_LIMIT),
        name="pair_terms",
    )(pair_slots, pair_weight, occupied, first_pair, parts, levels)


def grad_kernel(group, owner_ref, terms_ref, out_ref):
    occ_local, width = out_ref.shape
    owners = owner_ref.shape[1]
    per_owner = terms_ref.shape[0] // owners
    own = owner_ref[pl.ds(group[0], 1), :] - group[0] * occ_local
    chosen = (lax.broadcasted_iota(jnp.int32, (occ_local, owners), 0) == own).astype(F32)
    summed = jnp.sum(terms_ref[...].reshape(owners, per_owner, width), axis=1)
    out_ref[...] = jnp.dot(
        chosen, summed, preferred_element_type=F32, precision=lax.Precision.HIGHEST
    )


def sum_grads(terms, owner_orbitals, orb_group, occ_local):
    whole = pl.BlockSpec(memory_space=pltpu.VMEM)
    return pl.pallas_call(
        grad_kernel,
        out_shape=jax.ShapeDtypeStruct((occ_local, terms.shape[1]), F32),
        in_specs=[pl.BlockSpec(memory_space=pltpu.SMEM), whole, whole],
        out_specs=whole,
        compiler_params=pltpu.CompilerParams(vmem_limit_bytes=VMEM_LIMIT),
        name="sum_grads",
    )(orb_group[None].astype(jnp.int32), owner_orbitals.T, terms)


def on_device(
    half_integrals,
    domain_map,
    domain_index,
    owner_orbitals,
    pair_slots,
    pair_weight,
    virtual_energy,
    occupied_energy,
):
    orb_group = lax.axis_index("orb")
    owner_rank = lax.axis_index("aux")
    groups = lax.axis_size("orb")
    owners = lax.axis_size("aux")
    occ_local, rows, width = half_integrals.shape
    list_width = owner_orbitals.shape[1]
    share = pair_slots.shape[0] // groups

    own_local = (
        lax.dynamic_slice_in_dim(owner_orbitals, orb_group, 1, 1)[:, 0] - orb_group * occ_local
    )
    my_orbitals = lax.dynamic_slice_in_dim(owner_orbitals, owner_rank, 1, 0)[0]
    my_index = domain_index[my_orbitals]
    virt_count = virtual_energy.shape[0]
    levels = jnp.where(
        my_index >= 0, virtual_energy[jnp.clip(my_index, 0, virt_count - 1)], jnp.float32(1.0)
    )
    occupied = occupied_energy[my_orbitals]

    outgoing = make_slabs(half_integrals, domain_map, domain_index, own_local, orb_group)
    received = lax.all_to_all(
        outgoing.reshape(owners * groups, rows // groups, width),
        ("aux", "orb"),
        split_axis=0,
        concat_axis=0,
        tiled=True,
    )
    blocks = pair_blocks(
        received.reshape(owners, list_width, rows // groups, width), pair_slots
    )
    parts = lax.all_to_all(blocks, "orb", split_axis=0, concat_axis=0, tiled=True)
    amplitude, pair_energy, grad_terms = pair_terms(
        parts.reshape(groups, share, width, width),
        levels,
        pair_slots,
        pair_weight,
        occupied,
        (orb_group * share)[None].astype(jnp.int32),
        owners,
    )
    all_terms = lax.all_to_all(
        grad_terms, ("aux", "orb"), split_axis=0, concat_axis=0, tiled=True
    )
    domain_grad = sum_grads(all_terms, owner_orbitals, orb_group, occ_local)
    return (amplitude, pair_energy, domain_grad)


def solution(mesh):
    placed = (
        P("orb", "aux", None),
        P("orb", None, None),
        P(),
        P(),
        P("aux", None),
        P("aux"),
        P(),
        P(),
    )
    return jax.shard_map(
        on_device,
        mesh=mesh,
        in_specs=placed,
        out_specs=(P(("aux", "orb"), None, None), P(("aux", "orb")), P("orb", None)),
        check_vma=False,
    )
```

time: 1050 us -> 284 us (0.27)
  blocking collectives: 701 us -> 27.5 us
  matrix products: 62.3 us -> 0 us
  loops' own time: 62.1 us -> 0 us
  waiting for transfers between devices: 141 us -> 196 us
  local copies, waits for them, and re-layouts: 51.9 us -> 9.13 us
  Pallas kernels: 0 us -> 22 us
  starting transfers between devices: 6.09 us -> 27.8 us
  between operations: 14.2 us -> 0.75 us
    psum x1 -> x0, blocking collectives: 491 us -> none  [on_device(): summed = lax.psum(grad_part, 'aux')]
    all_to_all x1, blocking collectives: 209 us -> 27.5 us  [on_device(): lax.all_to_all(grad_terms, ('aux', 'orb'), split_axis=0, concat_axis=0, t...]
    all_to_all x1 -> x2, waiting for transfers between devices: 93.4 us -> 196 us  [the longest x1 186 us: on_device(): lax.all_to_all(outgoing.reshape(owners * groups, rows // groups, width),...]
    dot_general x19 -> x0, matrix products: 62.3 us -> none  [the longest x16 57.7 us: one_block(): lax.dot_general(left_slab, right_slab, (((0,), (0,)), ((), ())), preferre...]
    another operation x1 -> x0, loops' own time: 62.1 us -> none  [on_device(): lax.map(one_block, pair_slots)]
    reduce_scatter x2 -> x0, waiting for transfers between devices: 47.2 us -> none  [the longest x1 24 us: on_device(): lax.psum_scatter(summed, 'orb', scatter_dimension=0, tiled=True)]
    all_to_all x2 -> x0, local copies, waits for them, and re-layouts: 24 us -> none  [the longest x1 12 us: on_device(): lax.all_to_all(lax.all_to_all(outgoing, 'aux', split_axis=1, concat_axis=...]
    pallas_call x0 -> x4, Pallas kernels: none -> 22 us  [the longest x1 11.2 us: pair_blocks(): pl.pallas_call(gram_kernel, out_shape=jax.ShapeDtypeStruct((pairs, width,...]
  transfers between devices with their start and end apart: 3 -> 2, of which waited for: 3 -> 2; matrix products, arithmetic and copies ran while one was open for 1% -> 2% of each run, Pallas kernels for 0% -> 0%
where the time goes in v1:
time: 284 us; the launch traced here: 283 us
  waiting for transfers between devices  196 us (69%)
  starting transfers between devices  27.8 us (10%)
  blocking collectives  27.5 us (10%)
  Pallas kernels  22 us (8%)
  local copies, waits for them, and re-layouts  9.13 us (3%)
    all_to_all x1, waiting for transfers between devices, on_device(): lax.all_to_all(outgoing.reshape(owners * groups, rows // groups, width),...  186 us
    all_to_all x1, blocking collectives, on_device(): lax.all_to_all(grad_terms, ('aux', 'orb'), split_axis=0, concat_axis=0, t...  27.5 us
    all_to_all x1, starting transfers between devices, on_device(): lax.all_to_all(outgoing.reshape(owners * groups, rows // groups, width),...  24.2 us
    pallas_call x1, Pallas kernels, pair_blocks(): pl.pallas_call(gram_kernel, out_shape=jax.ShapeDtypeStruct((pairs, width,...  11.2 us
    all_to_all x1, waiting for transfers between devices, on_device(): lax.all_to_all(blocks, 'orb', split_axis=0, concat_axis=0, tiled=True)  9.9 us
    pallas_call x1, Pallas kernels, make_slabs(): pl.pallas_call(slab_kernel, out_shape=jax.ShapeDtypeStruct((owners, rows,...  8.24 us
  transfers between devices with their start and end apart: 2, of which 2 were waited for; matrix products, arithmetic and copies ran while one was open for 2% of the time, Pallas kernels for 0%

profile of v1, /device:TPU:1, one launch (start us, length us, event | category | flops | bytes accessed | tf_op | source)
XLA Modules:
  0.0 283.4 jit_solution(9992774399579061210)
XLA Ops:
  0.6 0.0 copy-start
  0.7 0.7 subtract_bitcast_fusion
  1.4 0.1 pad_add_fusion.scalars
  1.5 1.6 copy-done.1
  3.0 1.2 copy-done.2
  4.3 0.8 copy-done.3
  5.1 8.2 %slabs.1 = bf16[128,256,128]{2,1,0:T(8,128)(2,1)} custom-call(s32[129]{0:T(256)S(1)} %pad_add_fusion.scalars, bf16[32,256,128]{2,1,0:T(8,128)(2,1)S(1)} %copy-done.1, bf16[32,128,128]{2,1,0:T(8,128)(2,1)S(1)} %copy-done.2, s32[128,128]{1,0:T(8,128)S(1)} %copy-done.3), custom_call_target="tpu_custom_call" | custom-call | tf_op jit(solution)/shard_map/slabs/pallas_call | solution.py:36
  13.4 24.2 %all-to-all-start = ((bf16[512,64,128]{2,1,0:T(8,128)(2,1)}), bf16[512,64,128]{2,1,0:T(8,128)(2,1)}, u32[]{:S(2)}, u32[]{:S(2)}) async-start(bf16[512,64,128]{2,1,0:T(8,128)(2,1)} %bitcast.26), calls=%async_computation | async-start | bytes 16777216 | tf_op jit(solution)/shard_map/all_to_all | solution.py:202
  37.6 0.0 copy-start.6
  37.6 0.0 copy-start.5
  37.6 0.0 copy-done.7
  37.6 0.1 copy.16.slots
  37.7 0.2 dynamic-slice_reduce_fusion
  37.9 185.6 %all-to-all-done = bf16[512,64,128]{2,1,0:T(8,128)(2,1)} async-done(((bf16[512,64,128]{2,1,0:T(8,128)(2,1)}), bf16[512,64,128]{2,1,0:T(8,128)(2,1)}, u32[]{:S(2)}, u32[]{:S(2)}) %all-to-all-start) | async-done | bytes 8388640 | tf_op jit(solution)/shard_map/all_to_all | solution.py:202
  223.5 11.2 %pair_blocks.1 = f32[16,128,128]{2,1,0:T(8,128)} custom-call(s32[16,2]{1,0:T(8,128)S(1)} %copy.16.slots, bf16[128,4,64,128]{3,2,1,0:T(8,128)(2,1)} %bitcast.5.slab_ref), custom_call_target="tpu_custom_call" | custom-call | tf_op jit(solution)/shard_map/pair_blocks/pallas_call | solution.py:82
  234.7 3.5 %all-to-all-start.1 = ((f32[16,128,128]{2,1,0:T(8,128)}), f32[16,128,128]{2,1,0:T(8,128)S(1)}, u32[]{:S(2)}, u32[]{:S(2)}) async-start(f32[16,128,128]{2,1,0:T(8,128)} %pair_blocks.1), calls=%async_computation.1 | async-start | bytes 2097152 | tf_op jit(solution)/shard_map/all_to_all | solution.py:212
  238.3 1.4 gather_fusion.1
  239.7 0.0 copy-done.6
  239.7 0.6 gather_fusion
  240.3 3.1 %gather_fusion.2 = f32[512]{0:T(512)S(1)} fusion(f32[25000]{0:T(1024)S(1)} %copy-done, s32[1024]{0:T(1024)S(1)} %pad_clamp_fusion), kind=kCustom, calls=%fused_computation.2 | custom fusion | bytes 6144 | tf_op jit(solution)/shard_map/gather | solution.py:197
  243.5 9.9 %all-to-all-done.1 = f32[16,128,128]{2,1,0:T(8,128)S(1)} async-done(((f32[16,128,128]{2,1,0:T(8,128)}), f32[16,128,128]{2,1,0:T(8,128)S(1)}, u32[]{:S(2)}, u32[]{:S(2)}) %all-to-all-start.1) | async-done | bytes 1048608 | tf_op jit(solution)/shard_map/all_to_all | solution.py:212
  253.4 1.6 pair_terms.1
  255.0 27.5 %all_to_all.21 = f32[512,1,128]{2,1,0:T(1,128)S(1)} all-to-all(f32[512,1,128]{2,1,0:T(1,128)S(1)} %bitcast.24), channel_id=1, replica_groups=mesh['aux'=128,'orb'=4] {'aux','orb'}, dimensions={0} | all-to-all | bytes 524288 | tf_op jit(solution)/shard_map/all_to_all | solution.py:222
  282.5 0.9 sum_grads.1
  (13 shorter events, 0.0 us)
Async XLA Ops:
  0.6 239.7 %copy-start = (f32[25000]{0:T(1024)S(1)}, f32[25000]{0:T(1024)}, u32[]{:S(2)}) copy-start(f32[25000]{0:T(1024)} %param.14) | copy-start | bytes 300004
  1.5 1.6 copy-start.1
  3.0 1.2 copy-start.2
  4.3 0.8 copy-start.3
  13.4 24.3 %copy-start.7 = (s32[16,2]{0,1:T(2,128)S(1)}, s32[16,2]{0,1:T(2,128)}, u32[]{:S(2)}) copy-start(s32[16,2]{0,1:T(2,128)} %param.12) | copy-start | bytes 388
  13.4 24.4 %copy-start.4 = (s32[128,4]{0,1:T(4,128)S(1)}, s32[128,4]{0,1:T(4,128)}, u32[]{:S(2)}) copy-start(s32[128,4]{0,1:T(4,128)} %param.11) | copy-start | bytes 6148
  13.4 210.2 %all-to-all-start = ((bf16[512,64,128]{2,1,0:T(8,128)(2,1)}), bf16[512,64,128]{2,1,0:T(8,128)(2,1)}, u32[]{:S(2)}, u32[]{:S(2)}) async-start(bf16[512,64,128]{2,1,0:T(8,128)(2,1)} %bitcast.26), calls=%async_computation | async-start | bytes 16777216 | tf_op jit(solution)/shard_map/all_to_all | solution.py:202
  37.6 202.1 %copy-start.6 = (f32[128]{0:T(128)S(1)}, f32[128]{0:T(128)}, u32[]{:S(2)}) copy-start(f32[128]{0:T(128)} %param.15) | copy-start | bytes 1540
  37.6 215.8 %copy-start.5 = (s32[16]{0:T(128)S(1)}, s32[16]{0:T(128)}, u32[]{:S(2)}) copy-start(s32[16]{0:T(128)} %weights.1) | copy-start | bytes 196
  234.7 18.7 %all-to-all-start.1 = ((f32[16,128,128]{2,1,0:T(8,128)}), f32[16,128,128]{2,1,0:T(8,128)S(1)}, u32[]{:S(2)}, u32[]{:S(2)}) async-start(f32[16,128,128]{2,1,0:T(8,128)} %pair_blocks.1), calls=%async_computation.1 | async-start | bytes 2097152 | tf_op jit(solution)/shard_map/all_to_all | solution.py:212

commit v2 on v1

v2 whole, which is shorter than its diff:
```python
import functools

import jax
import jax.numpy as jnp
from jax import lax
from jax.experimental import pallas as pl
from jax.experimental.pallas import tpu as pltpu
from jax.sharding import PartitionSpec as P

F32 = jnp.float32
VMEM_LIMIT = 48 * 1024 * 1024
OWNERS_PER_STEP = 8
AXES = ("zh", "zl", "yh", "yl", "c", "x")
BLOCKS = tuple((s, t) for s in range(4) for t in range(s, 4))
TAIL = 16
TOP_POWER = 14.0


def slab_kernel(scalars, integral_ref, map_ref, index_ref, out_ref, slab_ref):
    occ_local = integral_ref.shape[0]
    per_step = out_ref.shape[0]
    step = pl.program_id(0)
    group = scalars[0]

    @pl.when(step == 0)
    def _():
        for orb in range(occ_local):
            product = jnp.dot(integral_ref[orb], map_ref[orb], preferred_element_type=F32)
            live = (index_ref[pl.ds(group * occ_local + orb, 1), :] >= 0).astype(F32)
            slab_ref[orb] = (product * live).astype(jnp.bfloat16)

    for k in range(per_step):
        out_ref[k] = slab_ref[scalars[1 + step * per_step + k]]


def make_slabs(half_integrals, domain_map, domain_index, own_local, orb_group):
    occ_local, rows, width = half_integrals.shape
    owners = own_local.shape[0]
    scalars = jnp.concatenate([orb_group[None].astype(jnp.int32), own_local])
    whole = lambda shape: pl.BlockSpec(shape, lambda i, s: (0,) * len(shape))
    return pl.pallas_call(
        slab_kernel,
        out_shape=jax.ShapeDtypeStruct((owners, rows, width), jnp.bfloat16),
        grid_spec=pltpu.PrefetchScalarGridSpec(
            num_scalar_prefetch=1,
            grid=(owners // OWNERS_PER_STEP,),
            in_specs=[
                whole(half_integrals.shape),
                whole(domain_map.shape),
                whole(domain_index.shape),
            ],
            out_specs=pl.BlockSpec((OWNERS_PER_STEP, rows, width), lambda i, s: (i, 0, 0)),
            scratch_shapes=[pltpu.VMEM((occ_local, rows, width), jnp.bfloat16)],
        ),
        compiler_params=pltpu.CompilerParams(vmem_limit_bytes=VMEM_LIMIT),
        name="slabs",
    )(scalars, half_integrals, domain_map, domain_index)


def gram_kernel(slab_ref, out_ref, gram_ref):
    step = pl.program_id(1)
    count, list_width, _, rows, width = slab_ref.shape
    half = list_width * width // 2
    joined = jnp.concatenate(
        [slab_ref[:, g, 0].reshape(count * rows, width) for g in range(list_width)], axis=1
    )
    low, high = joined[:, :half], joined[:, half:]
    product = functools.partial(
        lax.dot_general,
        dimension_numbers=(((0,), (0,)), ((), ())),
        preferred_element_type=F32,
    )
    parts = (product(low, low), product(low, high), product(high, high))

    @pl.when(step == 0)
    def _():
        for k in range(3):
            gram_ref[k] = parts[k]

    @pl.when(step > 0)
    def _():
        for k in range(3):
            gram_ref[k] += parts[k]

    @pl.when(step == pl.num_programs(1) - 1)
    def _():
        top = jnp.max(jnp.max(jnp.abs(gram_ref[...]), axis=0), axis=0, keepdims=True)
        top = jnp.max(top, axis=1, keepdims=True)
        power = jnp.clip(jnp.ceil(jnp.log2(jnp.maximum(top, 1e-35))), -100.0, 100.0)
        power = jnp.broadcast_to(power, (8, width))
        scale = jnp.exp2(TOP_POWER - power)
        pieces = out_ref.shape[0]
        depth = width // pieces
        for index, (left, right) in enumerate(BLOCKS):
            quadrant = left // 2 + right // 2
            for q in range(pieces):
                row = (left % 2) * width + q * depth
                column = (right % 2) * width
                block = gram_ref[quadrant, row : row + depth, column : column + width]
                out_ref[q, 0, index * depth : (index + 1) * depth, :] = block * scale[0:1]
        for q in range(pieces):
            base = len(BLOCKS) * depth
            out_ref[q, 0, base : base + 8, :] = power
            out_ref[q, 0, base + 8 : base + TAIL, :] = power


def partial_grams(slabs):
    count, list_width, owners, rows, width = slabs.shape
    pieces = 4
    depth = len(BLOCKS) * (width // pieces) + TAIL
    steps = 2
    return pl.pallas_call(
        gram_kernel,
        out_shape=jax.ShapeDtypeStruct((pieces, owners, depth, width), F32),
        grid=(owners, steps),
        in_specs=[
            pl.BlockSpec(
                (count // steps, list_width, 1, rows, width), lambda j, h: (h, 0, j, 0, 0)
            )
        ],
        out_specs=pl.BlockSpec((pieces, 1, depth, width), lambda j, h: (0, j, 0, 0)),
        scratch_shapes=[pltpu.VMEM((3, list_width * width // 2, list_width * width // 2), F32)],
        compiler_params=pltpu.CompilerParams(vmem_limit_bytes=VMEM_LIMIT),
        name="partial_grams",
    )(slabs)


def pair_kernel(
    packed,
    occupied,
    piece_ref,
    block_ref,
    level_ref,
    amp0_ref,
    amp1_ref,
    amp2_ref,
    amp3_ref,
    grad_ref,
    ratio_ref,
    column_ref,
    place_ref,
    acc_ref,
    weight_table,
    energy_table,
):
    list_width, width = level_ref.shape
    depth = block_ref.shape[0] // len(BLOCKS)
    pairs = packed.shape[0]
    piece = piece_ref[0]
    rows = pl.ds(pl.multiple_of(piece * depth, depth), depth)
    for k in range(list_width * list_width):
        weight_table[k] = 0
    for pair in range(pairs):
        weight_table[packed[pair, 0] * list_width + packed[pair, 1]] = packed[pair, 2]
    for s in range(list_width):
        column_ref[s] = jnp.broadcast_to(level_ref[s : s + 1, :], (width, width)).T
    acc_ref[...] = jnp.zeros_like(acc_ref)
    place_ref[...] = jnp.zeros_like(place_ref)
    row_squares = [jnp.zeros((depth, width), F32) for _ in range(list_width)]
    for index, (left, right) in enumerate(BLOCKS):
        block = block_ref[index * depth : (index + 1) * depth, :]
        denominator = (
            column_ref[left, rows, :]
            + level_ref[right : right + 1, :]
            - occupied[left]
            - occupied[right]
        )
        ratio = block / denominator
        ratio_ref[index] = ratio
        energy_table[index] = jnp.sum(block * ratio)
        weight = weight_table[left * list_width + right]
        if left != right:
            weight = weight + weight_table[right * list_width + left]
        squares = (weight.astype(F32) / width) * (ratio * ratio)
        row_squares[left] = row_squares[left] + squares
        acc_ref[right : right + 1, :] += jnp.sum(squares, axis=0, keepdims=True)
    for s in range(list_width):
        place_ref[rows, :] = row_squares[s]
        acc_ref[s : s + 1, :] += jnp.sum(place_ref[...].T, axis=0, keepdims=True)

    def block_of(pair):
        low = jnp.minimum(packed[pair, 0], packed[pair, 1])
        high = jnp.maximum(packed[pair, 0], packed[pair, 1])
        return jnp.where(low == 0, 0, jnp.where(low == 1, 3, jnp.where(low == 2, 5, 6))) + high

    lane = lax.broadcasted_iota(jnp.int32, (1, width), 1)
    energies = jnp.zeros((1, width), F32)
    for pair in range(pairs):
        energy = -packed[pair, 2].astype(F32) * energy_table[block_of(pair)] / (width * width)
        energies = jnp.where(lane == pair, energy, energies)
    lines = []
    for s in range(list_width):
        lines.extend([acc_ref[s : s + 1, :], energies])
    tile = jnp.concatenate(lines, axis=0)
    height = tile.shape[0]
    for k in range(grad_ref.shape[0] // height):
        grad_ref[k * height : (k + 1) * height, :] = tile
    for shift, amp_ref in enumerate((amp0_ref, amp1_ref, amp2_ref, amp3_ref)):
        share = amp_ref.shape[0]
        quarter = jnp.bitwise_and(piece + shift, 3)
        for k in range(share):
            pair = quarter * share + k
            live = (packed[pair, 2] > 0).astype(F32)
            amp_ref[k] = (-ratio_ref[block_of(pair)] * live).astype(jnp.bfloat16)


def pair_terms(blocks, levels, packed, occupied, piece, copies):
    height, width = blocks.shape
    depth = height // len(BLOCKS)
    list_width = levels.shape[0]
    share = packed.shape[0] // 4
    whole = pl.BlockSpec(memory_space=pltpu.VMEM)
    scalar = pl.BlockSpec(memory_space=pltpu.SMEM)
    amp = jax.ShapeDtypeStruct((share, depth, width), jnp.bfloat16)
    return pl.pallas_call(
        pair_kernel,
        out_shape=(amp,) * 4
        + (jax.ShapeDtypeStruct((copies * 2 * list_width, width), F32),),
        in_specs=[scalar, scalar, scalar, whole, whole],
        out_specs=(whole,) * 5,
        scratch_shapes=[
            pltpu.VMEM((len(BLOCKS), depth, width), F32),
            pltpu.VMEM((list_width, width, width), F32),
            pltpu.VMEM((width, width), F32),
            pltpu.VMEM((list_width, width), F32),
            pltpu.SMEM((list_width * list_width,), jnp.int32),
            pltpu.SMEM((len(BLOCKS),), F32),
        ],
        compiler_params=pltpu.CompilerParams(vmem_limit_bytes=VMEM_LIMIT),
        name="pair_terms",
    )(packed, occupied, piece[None].astype(jnp.int32), blocks, levels)


def join_kernel(slots, quarter_ref, part0_ref, part1_ref, part2_ref, part3_ref, out_ref, place_ref):
    share, depth, width = part0_ref.shape
    quarter = quarter_ref[0]
    for k in range(share):
        for shift, part_ref in enumerate((part0_ref, part1_ref, part2_ref, part3_ref)):
            piece = jnp.bitwise_and(quarter + 4 - shift, 3)
            rows = pl.ds(pl.multiple_of(piece * depth, depth), depth)
            place_ref[rows, :] = part_ref[k].astype(F32)
        block = place_ref[...]
        pair = quarter * share + k
        swapped = slots[pair, 0] > slots[pair, 1]
        out_ref[k] = jnp.where(swapped, block.T, block).astype(jnp.bfloat16)


def join_amplitudes(parts, pair_slots, quarter):
    share, depth, width = parts[0].shape
    whole = pl.BlockSpec(memory_space=pltpu.VMEM)
    scalar = pl.BlockSpec(memory_space=pltpu.SMEM)
    return pl.pallas_call(
        join_kernel,
        out_shape=jax.ShapeDtypeStruct((share, width, width), jnp.bfloat16),
        in_specs=[scalar, scalar] + [whole] * 4,
        out_specs=whole,
        scratch_shapes=[pltpu.VMEM((width, width), F32)],
        compiler_params=pltpu.CompilerParams(vmem_limit_bytes=VMEM_LIMIT),
        name="join_amplitudes",
    )(pair_slots, quarter[None].astype(jnp.int32), *parts)


def grad_kernel(scalars, owner_ref, terms_ref, out_ref, energy_ref):
    occ_local, width = out_ref.shape
    lines = owner_ref.shape[1]
    share = energy_ref.shape[0]
    chosen = (
        lax.broadcasted_iota(jnp.int32, (occ_local, lines), 0) == owner_ref[...]
    ).astype(F32)
    out_ref[...] = jnp.dot(
        chosen, terms_ref[...], preferred_element_type=F32, precision=lax.Precision.HIGHEST
    )
    energies = terms_ref[pl.ds(scalars[1], 1), :]
    for k in range(2, scalars.shape[0]):
        energies = energies + terms_ref[pl.ds(scalars[k], 1), :]
    lane = lax.broadcasted_iota(jnp.int32, (1, width), 1)
    for k in range(share):
        energy_ref[k] = jnp.sum(jnp.where(lane == scalars[0] * share + k, energies, 0.0))


def sum_grads(terms, line_owner, scalars, occ_local, share):
    whole = pl.BlockSpec(memory_space=pltpu.VMEM)
    scalar = pl.BlockSpec(memory_space=pltpu.SMEM)
    return pl.pallas_call(
        grad_kernel,
        out_shape=(
            jax.ShapeDtypeStruct((occ_local, terms.shape[1]), F32),
            jax.ShapeDtypeStruct((share,), F32),
        ),
        in_specs=[scalar, whole, whole],
        out_specs=(whole, scalar),
        compiler_params=pltpu.CompilerParams(vmem_limit_bytes=VMEM_LIMIT),
        name="sum_grads",
    )(scalars, line_owner, terms)


def on_device(
    half_integrals,
    domain_map,
    domain_index,
    owner_orbitals,
    pair_slots,
    pair_weight,
    virtual_energy,
    occupied_energy,
):
    position = {name: lax.axis_index(name) for name in AXES}
    size = {name: lax.axis_size(name) for name in AXES}
    x = position["x"]

    def aux_rank(zh):
        rank = zh
        for name in AXES[1:-1]:
            rank = rank * size[name] + position[name]
        return rank

    occ_local, rows, width = half_integrals.shape
    owners, list_width = owner_orbitals.shape
    share = pair_slots.shape[0] // size["x"]
    cross = [(q * 4 + s, s * 4 + q) for q in range(4) for s in range(4)]

    packed = lax.ppermute(
        jnp.concatenate([pair_slots, pair_weight[:, None]], axis=1), ("zh", "x"), cross
    )
    own = lax.dynamic_slice_in_dim(owner_orbitals, x, 1, 1)[:, 0] - x * occ_local
    grid = own.reshape([size[name] for name in AXES[:-1]])
    order = grid.transpose(1, 3, 4, 0, 2).reshape(-1)
    source_own = jnp.broadcast_to(
        grid.transpose(1, 2, 3, 4, 0)[None], (size["zh"],) + grid.shape[1:] + grid.shape[:1]
    ).reshape(-1)
    line_owner = jnp.stack([source_own, jnp.full_like(source_own, -1)], axis=1).reshape(1, -1)

    my_orbitals = lax.dynamic_slice_in_dim(owner_orbitals, aux_rank(x), 1, 0)[0]
    my_index = domain_index[my_orbitals]
    virt_count = virtual_energy.shape[0]
    levels = jnp.where(
        my_index >= 0, virtual_energy[jnp.clip(my_index, 0, virt_count - 1)], jnp.float32(1.0)
    )
    occupied = occupied_energy[my_orbitals]

    outgoing = make_slabs(half_integrals, domain_map, domain_index, order, x)
    inner = ("zl", "yl", "c", "x")
    members = size["zl"] * size["yl"] * size["c"] * size["x"]
    per_member = owners // members
    received = lax.all_to_all(
        outgoing.reshape(members, per_member * rows, width),
        inner,
        split_axis=0,
        concat_axis=0,
        tiled=True,
    )
    scaled = partial_grams(
        received.reshape(members // size["x"], list_width, per_member, rows, width)
    )
    depth = scaled.shape[2]
    sent = scaled.astype(jnp.float16).reshape(-1, depth, width)
    arrived = lax.all_to_all(sent, ("zh", "yh"), split_axis=0, concat_axis=0, tiled=True)
    power = arrived[:, depth - TAIL : depth - TAIL + 1, :].astype(F32) - TOP_POWER
    blocks = jnp.sum(arrived[:, : depth - TAIL, :].astype(F32) * jnp.exp2(power), axis=0)

    *pieces, grad_terms = pair_terms(
        blocks, levels, packed, occupied, position["zh"], owners
    )
    moved = [
        lax.ppermute(
            piece,
            ("zh", "x"),
            [(q * 4 + s, s * 4 + (q + k) % 4) for q in range(4) for s in range(4)],
        )
        for k, piece in enumerate(pieces)
    ]
    all_terms = lax.all_to_all(grad_terms, AXES, split_axis=0, concat_axis=0, tiled=True)
    amplitude = join_amplitudes(moved, pair_slots, x)
    lines = [
        2 * (aux_rank(jnp.int32(q)) * size["x"] + position["zh"]) + 1 for q in range(size["zh"])
    ]
    scalars = jnp.stack([x] + lines).astype(jnp.int32)
    domain_grad, pair_energy = sum_grads(all_terms, line_owner, scalars, occ_local, share)
    return (amplitude, pair_energy, domain_grad)


def solution(mesh):
    fine = jax.sharding.Mesh(mesh.devices.reshape(4, 2, 4, 2, 2, 4), AXES)
    aux, orb = AXES[:-1], "x"
    placed = (
        P(orb, aux, None),
        P(orb, None, None),
        P(),
        P(),
        P(aux, None),
        P(aux),
        P(),
        P(),
    )
    return jax.shard_map(
        on_device,
        mesh=fine,
        in_specs=placed,
        out_specs=(P(AXES, None, None), P(AXES), P(orb, None)),
        check_vma=False,
    )
```

time: 284 us -> 233 us (0.82)
  waiting for transfers between devices: 196 us -> 34.7 us
  blocking collectives: 27.5 us -> 106 us
  starting transfers between devices: 27.8 us -> 53.2 us
    all_to_all x2, waiting for transfers between devices: 196 us -> 31.1 us  [the longest x1 31.1 us: on_device(): lax.all_to_all(sent, ('zh', 'yh'), split_axis=0, concat_axis=0, tiled=True)]
    all_to_all x1, blocking collectives: 27.5 us -> 106 us  [on_device(): lax.all_to_all(outgoing.reshape(members, per_member * rows, width), inner...]
    ppermute x0 -> x5, starting transfers between devices: none -> 19.6 us  [the longest x4 19 us: on_device(): lax.ppermute(piece, ('zh', 'x'), [(q * 4 + s, s * 4 + (q + k) % 4) for q...]
    all_to_all x2, starting transfers between devices: 27.8 us -> 33.6 us  [the longest x1 22.6 us: on_device(): lax.all_to_all(grad_terms, AXES, split_axis=0, concat_axis=0, tiled=True)]
    ppermute x0 -> x5, waiting for transfers between devices: none -> 3.63 us  [the longest x4 3.63 us: on_device(): lax.ppermute(piece, ('zh', 'x'), [(q * 4 + s, s * 4 + (q + k) % 4) for q...]
    pallas_call x3 -> x4, Pallas kernels: 13.7 us -> 14.4 us  [the longest x1 9.43 us: partial_grams(): pl.pallas_call(gram_kernel, out_shape=jax.ShapeDtypeStruct((pieces, owner...]
  transfers between devices with their start and end apart: 2 -> 7, of which waited for: 2 -> 3; matrix products, arithmetic and copies ran while one was open for 2% -> 3% of each run, Pallas kernels for 0% -> 1%
where the time goes in v2:
time: 233 us; the launch traced here: 230 us
  blocking collectives  106 us (45%)
  starting transfers between devices  53.2 us (23%)
  waiting for transfers between devices  34.7 us (15%)
  Pallas kernels  22.6 us (10%)
  local copies, waits for them, and re-layouts  10.4 us (4%)
  other arithmetic  2.43 us (1%)
    all_to_all x1, blocking collectives, on_device(): lax.all_to_all(outgoing.reshape(members, per_member * rows, width), inner...  106 us
    all_to_all x1, waiting for transfers between devices, on_device(): lax.all_to_all(sent, ('zh', 'yh'), split_axis=0, concat_axis=0, tiled=True)  31.1 us
    all_to_all x1, starting transfers between devices, on_device(): lax.all_to_all(grad_terms, AXES, split_axis=0, concat_axis=0, tiled=True)  22.6 us
    ppermute x4, starting transfers between devices, on_device(): lax.ppermute(piece, ('zh', 'x'), [(q * 4 + s, s * 4 + (q + k) % 4) for q...  19 us
    all_to_all x1, starting transfers between devices, on_device(): lax.all_to_all(sent, ('zh', 'yh'), split_axis=0, concat_axis=0, tiled=True)  10.9 us
    pallas_call x1, Pallas kernels, partial_grams(): pl.pallas_call(gram_kernel, out_shape=jax.ShapeDtypeStruct((pieces, owner...  9.43 us
    pallas_call x1, Pallas kernels, make_slabs(): pl.pallas_call(slab_kernel, out_shape=jax.ShapeDtypeStruct((owners, rows,...  8.27 us
  transfers between devices with their start and end apart: 7, of which 3 were waited for; matrix products, arithmetic and copies ran while one was open for 3% of the time, Pallas kernels for 1%

profile of v2, /device:TPU:1, one launch (start us, length us, event | category | flops | bytes accessed | tf_op | source)
XLA Modules:
  0.0 230.4 jit_solution(1804185932437362009)
XLA Ops:
  0.7 0.7 subtract_reduce_fusion
  2.0 1.6 copy-done.1
  3.6 1.2 copy-done.2
  4.8 0.8 copy-done.3
  5.6 8.3 %slabs.1 = bf16[128,256,128]{2,1,0:T(8,128)(2,1)} custom-call(s32[129]{0:T(256)S(1)} %pad_add_fusion.1.scalars, bf16[32,256,128]{2,1,0:T(8,128)(2,1)S(1)} %copy-done.1, bf16[32,128,128]{2,1,0:T(8,128)(2,1)S(1)} %copy-done.2, s32[128,128]{1,0:T(8,128)S(1)} %copy-done.3), custom_call_target="tpu_custom_call" | custom-call | tf_op jit(solution)/shard_map/slabs/pallas_call | solution.py:41
  13.9 106.2 %all_to_all.21 = bf16[32,1024,128]{2,1,0:T(8,128)(2,1)} all-to-all(bf16[32,1024,128]{2,1,0:T(8,128)(2,1)} %bitcast.27), channel_id=1, replica_groups=mesh['zh'=4,'zl'=2,'yh'=4,'yl'=2,'c'=2,'x'=4] {'zl','yl','c','x'}, dimensions={0} | all-to-all | bytes 16777216 | tf_op jit(solution)/shard_map/all_to_all | solution.py:345
  120.1 9.4 %partial_grams.1 = f32[4,4,336,128]{3,2,1,0:T(8,128)S(1)} custom-call(bf16[8,4,4,256,128]{4,3,2,1,0:T(8,128)(2,1)} %bitcast.28), custom_call_target="tpu_custom_call" | custom-call | tf_op jit(solution)/shard_map/partial_grams/pallas_call | solution.py:112
  129.5 1.3 convert_element_type.9
  130.8 10.9 %all-to-all-start.1 = ((f16[16,336,128]{2,1,0:T(8,128)(2,1)}), f16[16,336,128]{2,1,0:T(8,128)(2,1)S(1)}, u32[]{:S(2)}, u32[]{:S(2)}) async-start(f16[16,336,128]{2,1,0:T(8,128)(2,1)} %bitcast.7), calls=%async_computation.1 | async-start | bytes 2752512 | tf_op jit(solution)/shard_map/all_to_all | solution.py:357
  141.9 0.7 collective-permute-start
  142.8 1.4 gather_fusion.1
  144.2 0.6 gather_fusion
  144.8 3.1 %gather_fusion.2 = f32[512]{0:T(512)S(1)} fusion(f32[25000]{0:T(1024)S(1)} %copy-done, s32[1024]{0:T(1024)S(1)} %pad_clamp_fusion), kind=kCustom, calls=%fused_computation.2 | custom fusion | bytes 6144 | tf_op jit(solution)/shard_map/gather | solution.py:337
  148.0 31.1 %all-to-all-done.1 = f16[16,336,128]{2,1,0:T(8,128)(2,1)S(1)} async-done(((f16[16,336,128]{2,1,0:T(8,128)(2,1)}), f16[16,336,128]{2,1,0:T(8,128)(2,1)S(1)}, u32[]{:S(2)}, u32[]{:S(2)}) %all-to-all-start.1) | async-done | bytes 1376288 | tf_op jit(solution)/shard_map/all_to_all | solution.py:357
  179.4 1.9 pair_terms.1
  181.3 22.6 %all-to-all-start.2 = ((f32[512,2,128]{2,1,0:T(2,128)}), f32[512,2,128]{2,1,0:T(2,128)S(1)}, u32[]{:S(2)}, u32[]{:S(2)}) async-start(f32[512,2,128]{2,1,0:T(2,128)} %bitcast.17), calls=%async_computation.2 | async-start | bytes 1048576 | tf_op jit(solution)/shard_map/all_to_all | solution.py:372
  204.0 0.7 collective-permute-start.1
  204.6 7.6 %collective-permute-start.2 = (bf16[4,32,128]{2,1,0:T(8,128)(2,1)S(1)}, bf16[4,32,128]{2,1,0:T(8,128)(2,1)S(1)}, u32[]{:S(2)}, u32[]{:S(2)}) collective-permute-start(bf16[4,32,128]{2,1,0:T(8,128)(2,1)S(1)} %get-tuple-element.11), channel_id=1, source_target_pairs={{0,1},{1,129},{2,257},{3,385},{128,2},{129,130},{130,258},{131,386... | collective-permute-start | bytes 98312 | tf_op jit(solution)/shard_map/ppermute | solution.py:365
  212.2 7.6 %collective-permute-start.3 = (bf16[4,32,128]{2,1,0:T(8,128)(2,1)S(1)}, bf16[4,32,128]{2,1,0:T(8,128)(2,1)S(1)}, u32[]{:S(2)}, u32[]{:S(2)}) collective-permute-start(bf16[4,32,128]{2,1,0:T(8,128)(2,1)S(1)} %get-tuple-element.12), channel_id=1, source_target_pairs={{0,2},{1,130},{2,258},{3,386},{128,3},{129,131},{130,259},{131,387... | collective-permute-start | bytes 98312 | tf_op jit(solution)/shard_map/ppermute | solution.py:365
  219.8 3.1 %collective-permute-start.4 = (bf16[4,32,128]{2,1,0:T(8,128)(2,1)S(1)}, bf16[4,32,128]{2,1,0:T(8,128)(2,1)S(1)}, u32[]{:S(2)}, u32[]{:S(2)}) collective-permute-start(bf16[4,32,128]{2,1,0:T(8,128)(2,1)S(1)} %get-tuple-element.13), channel_id=1, source_target_pairs={{0,3},{1,131},{2,259},{3,387},{128,0},{129,128},{130,256},{131,384... | collective-permute-start | bytes 98312 | tf_op jit(solution)/shard_map/ppermute | solution.py:365
  223.8 1.6 collective-permute-done.3.part2_ref
  225.4 2.0 collective-permute-done.4.part3_ref
  227.4 1.5 join_amplitudes.1
  228.9 1.5 sum_grads.1
  (39 shorter events, 2.0 us)
Async XLA Ops:
  0.6 144.2 %copy-start = (f32[25000]{0:T(1024)S(1)}, f32[25000]{0:T(1024)}, u32[]{:S(2)}) copy-start(f32[25000]{0:T(1024)} %param.14) | copy-start | bytes 300004
  2.0 1.6 copy-start.1
  3.6 1.2 copy-start.2
  4.8 0.8 copy-start.3
  129.5 12.2 %copy-start.5 = (s32[16,2]{0,1:T(2,128)S(1)}, s32[16,2]{0,1:T(2,128)}, u32[]{:S(2)}) copy-start(s32[16,2]{0,1:T(2,128)} %param.12) | copy-start | bytes 388
  129.5 12.2 %copy-start.7 = (s32[16]{0:T(128)S(1)}, s32[16]{0:T(128)}, u32[]{:S(2)}) copy-start(s32[16]{0:T(128)} %param.13) | copy-start | bytes 196
  129.5 13.0 %copy-start.6 = (s32[128,4]{0,1:T(4,128)S(1)}, s32[128,4]{0,1:T(4,128)}, u32[]{:S(2)}) copy-start(s32[128,4]{0,1:T(4,128)} %param.11) | copy-start | bytes 6148
  129.5 14.6 %copy-start.4 = (f32[128]{0:T(128)S(1)}, f32[128]{0:T(128)}, u32[]{:S(2)}) copy-start(f32[128]{0:T(128)} %param.15) | copy-start | bytes 1540
  130.8 48.2 %all-to-all-start.1 = ((f16[16,336,128]{2,1,0:T(8,128)(2,1)}), f16[16,336,128]{2,1,0:T(8,128)(2,1)S(1)}, u32[]{:S(2)}, u32[]{:S(2)}) async-start(f16[16,336,128]{2,1,0:T(8,128)(2,1)} %bitcast.7), calls=%async_computation.1 | async-start | bytes 2752512 | tf_op jit(solution)/shard_map/all_to_all | solution.py:357
  141.9 37.5 %collective-permute-start = (s32[16,3]{1,0:T(8,128)S(1)}, s32[16,3]{1,0:T(8,128)S(1)}, u32[]{:S(2)}, u32[]{:S(2)}) collective-permute-start(s32[16,3]{1,0:T(8,128)S(1)} %copy.33), channel_id=1, source_target_pairs={{0,0},{1,128},{2,256},{3,384},{128,1},{129,129},{130,257},{131,385... | collective-permute-start | bytes 584 | tf_op jit(solution)/shard_map/ppermute | solution.py:322
  181.3 47.6 %all-to-all-start.2 = ((f32[512,2,128]{2,1,0:T(2,128)}), f32[512,2,128]{2,1,0:T(2,128)S(1)}, u32[]{:S(2)}, u32[]{:S(2)}) async-start(f32[512,2,128]{2,1,0:T(2,128)} %bitcast.17), calls=%async_computation.2 | async-start | bytes 1048576 | tf_op jit(solution)/shard_map/all_to_all | solution.py:372
  204.0 19.8 %collective-permute-start.1 = (bf16[4,32,128]{2,1,0:T(8,128)(2,1)S(1)}, bf16[4,32,128]{2,1,0:T(8,128)(2,1)S(1)}, u32[]{:S(2)}, u32[]{:S(2)}) collective-permute-start(bf16[4,32,128]{2,1,0:T(8,128)(2,1)S(1)} %get-tuple-element.10), channel_id=1, source_target_pairs={{0,0},{1,128},{2,256},{3,384},{128,1},{129,129},{130,257},{131,385... | collective-permute-start | bytes 98312 | tf_op jit(solution)/shard_map/ppermute | solution.py:365
  204.6 19.1 %collective-permute-start.2 = (bf16[4,32,128]{2,1,0:T(8,128)(2,1)S(1)}, bf16[4,32,128]{2,1,0:T(8,128)(2,1)S(1)}, u32[]{:S(2)}, u32[]{:S(2)}) collective-permute-start(bf16[4,32,128]{2,1,0:T(8,128)(2,1)S(1)} %get-tuple-element.11), channel_id=1, source_target_pairs={{0,1},{1,129},{2,257},{3,385},{128,2},{129,130},{130,258},{131,386... | collective-permute-start | bytes 98312 | tf_op jit(solution)/shard_map/ppermute | solution.py:365
  212.2 13.2 %collective-permute-start.3 = (bf16[4,32,128]{2,1,0:T(8,128)(2,1)S(1)}, bf16[4,32,128]{2,1,0:T(8,128)(2,1)S(1)}, u32[]{:S(2)}, u32[]{:S(2)}) collective-permute-start(bf16[4,32,128]{2,1,0:T(8,128)(2,1)S(1)} %get-tuple-element.12), channel_id=1, source_target_pairs={{0,2},{1,130},{2,258},{3,386},{128,3},{129,131},{130,259},{131,387... | collective-permute-start | bytes 98312 | tf_op jit(solution)/shard_map/ppermute | solution.py:365
  219.8 7.5 %collective-permute-start.4 = (bf16[4,32,128]{2,1,0:T(8,128)(2,1)S(1)}, bf16[4,32,128]{2,1,0:T(8,128)(2,1)S(1)}, u32[]{:S(2)}, u32[]{:S(2)}) collective-permute-start(bf16[4,32,128]{2,1,0:T(8,128)(2,1)S(1)} %get-tuple-element.13), channel_id=1, source_target_pairs={{0,3},{1,131},{2,259},{3,387},{128,0},{129,128},{130,256},{131,384... | collective-permute-start | bytes 98312 | tf_op jit(solution)/shard_map/ppermute | solution.py:365

commit v3 on v2

v3 whole, which is shorter than its diff:
```python
import functools

import jax
import jax.numpy as jnp
from jax import lax
from jax.experimental import pallas as pl
from jax.experimental.pallas import tpu as pltpu
from jax.sharding import PartitionSpec as P

F32 = jnp.float32
VMEM_LIMIT = 48 * 1024 * 1024
SLAB_VMEM_LIMIT = 62 * 1024 * 1024
OWNERS_PER_STEP = 8
ORBS_PER_STEP = 8
AXES = ("zh", "zl", "yh", "yl", "c", "x")
BLOCKS = tuple((s, t) for s in range(4) for t in range(s, 4))
TAIL = 16
TOP_POWER = 14.0


def slab_kernel(scalars, integral_ref, map_ref, index_ref, out_ref, slab_ref):
    orbs = integral_ref.shape[0]
    per_step = out_ref.shape[0]
    step = pl.program_id(0)
    first_write = slab_ref.shape[0] // orbs

    @pl.when(step < first_write)
    def _():
        for k in range(orbs):
            orb = step * orbs + k
            live = index_ref[pl.ds(scalars[0] * slab_ref.shape[0] + orb, 1), :] >= 0
            masked = map_ref[k] * live.astype(F32).astype(jnp.bfloat16)
            slab_ref[orb] = lax.dot_general(
                masked.T, integral_ref[k], (((1,), (1,)), ((), ())), preferred_element_type=F32
            ).astype(jnp.bfloat16)

    @pl.when(step >= first_write)
    def _():
        for k in range(per_step):
            out_ref[k] = slab_ref[scalars[1 + (step - first_write) * per_step + k]]


def make_slabs(half_integrals, domain_map, domain_index, own_local, orb_group):
    occ_local, rows, width = half_integrals.shape
    owners = own_local.shape[0]
    scalars = jnp.concatenate([orb_group[None].astype(jnp.int32), own_local])
    parts = occ_local // ORBS_PER_STEP
    read = lambda i, s: (jnp.minimum(i, parts - 1), 0, 0)
    return pl.pallas_call(
        slab_kernel,
        out_shape=jax.ShapeDtypeStruct((owners, width, rows), jnp.bfloat16),
        grid_spec=pltpu.PrefetchScalarGridSpec(
            num_scalar_prefetch=1,
            grid=(parts + owners // OWNERS_PER_STEP,),
            in_specs=[
                pl.BlockSpec((ORBS_PER_STEP, rows, width), read),
                pl.BlockSpec((ORBS_PER_STEP, width, width), read),
                pl.BlockSpec(domain_index.shape, lambda i, s: (0, 0)),
            ],
            out_specs=pl.BlockSpec(
                (OWNERS_PER_STEP, width, rows), lambda i, s: (jnp.maximum(i - parts, 0), 0, 0)
            ),
            scratch_shapes=[pltpu.VMEM((occ_local, width, rows), jnp.bfloat16)],
        ),
        compiler_params=pltpu.CompilerParams(vmem_limit_bytes=SLAB_VMEM_LIMIT),
        name="slabs",
    )(scalars, half_integrals, domain_map, domain_index)


def gram_kernel(slab_ref, out_ref, gram_ref):
    step = pl.program_id(1)
    count, list_width, _, width, rows = slab_ref.shape
    half = list_width * width // 2
    middle = list_width // 2
    low = jnp.concatenate(
        [slab_ref[k, :middle, 0].reshape(half, rows) for k in range(count)], axis=1
    )
    high = jnp.concatenate(
        [slab_ref[k, middle:, 0].reshape(half, rows) for k in range(count)], axis=1
    )
    product = functools.partial(
        lax.dot_general,
        dimension_numbers=(((1,), (1,)), ((), ())),
        preferred_element_type=F32,
    )
    parts = (product(low, low), product(low, high), product(high, high))

    @pl.when(step == 0)
    def _():
        for k in range(3):
            gram_ref[k] = parts[k]

    @pl.when(step > 0)
    def _():
        for k in range(3):
            gram_ref[k] += parts[k]

    @pl.when(step == pl.num_programs(1) - 1)
    def _():
        top = jnp.max(jnp.max(jnp.abs(gram_ref[...]), axis=0), axis=0, keepdims=True)
        top = jnp.max(top, axis=1, keepdims=True)
        power = jnp.clip(jnp.ceil(jnp.log2(jnp.maximum(top, 1e-35))), -100.0, 100.0)
        power = jnp.broadcast_to(power, (8, width))
        scale = jnp.exp2(TOP_POWER - power)
        pieces = out_ref.shape[0]
        depth = width // pieces
        for index, (left, right) in enumerate(BLOCKS):
            quadrant = left // 2 + right // 2
            for q in range(pieces):
                row = (left % 2) * width + q * depth
                column = (right % 2) * width
                block = gram_ref[quadrant, row : row + depth, column : column + width]
                out_ref[q, 0, index * depth : (index + 1) * depth, :] = block * scale[0:1]
        for q in range(pieces):
            base = len(BLOCKS) * depth
            out_ref[q, 0, base : base + 8, :] = power
            out_ref[q, 0, base + 8 : base + TAIL, :] = power


def partial_grams(slabs):
    count, list_width, owners, width, rows = slabs.shape
    pieces = 4
    depth = len(BLOCKS) * (width // pieces) + TAIL
    steps = 2
    return pl.pallas_call(
        gram_kernel,
        out_shape=jax.ShapeDtypeStruct((pieces, owners, depth, width), F32),
        grid=(owners, steps),
        in_specs=[
            pl.BlockSpec(
                (count // steps, list_width, 1, width, rows), lambda j, h: (h, 0, j, 0, 0)
            )
        ],
        out_specs=pl.BlockSpec((pieces, 1, depth, width), lambda j, h: (0, j, 0, 0)),
        scratch_shapes=[pltpu.VMEM((3, list_width * width // 2, list_width * width // 2), F32)],
        compiler_params=pltpu.CompilerParams(vmem_limit_bytes=VMEM_LIMIT),
        name="partial_grams",
    )(slabs)


def split(value):
    high = value.astype(jnp.bfloat16).astype(F32)
    middle = (value - high).astype(jnp.bfloat16).astype(F32)
    return [high, middle, value - high - middle]


def pair_kernel(
    packed,
    occupied,
    place,
    block_ref,
    level_ref,
    out_ref,
    ratio_ref,
    column_ref,
    place_ref,
    acc_ref,
    weight_table,
    energy_table,
):
    list_width, width = level_ref.shape
    depth = block_ref.shape[0] // len(BLOCKS)
    pairs = packed.shape[0]
    piece, target = place[0], place[1]
    rows = pl.ds(pl.multiple_of(piece * depth, depth), depth)
    for k in range(list_width * list_width):
        weight_table[k] = 0
    for pair in range(pairs):
        weight_table[packed[pair, 0] * list_width + packed[pair, 1]] = packed[pair, 2]
    for s in range(list_width):
        column_ref[s] = jnp.broadcast_to(level_ref[s : s + 1, :], (width, width)).T
    acc_ref[...] = jnp.zeros_like(acc_ref)
    place_ref[...] = jnp.zeros_like(place_ref)
    row_squares = [jnp.zeros((depth, width), F32) for _ in range(list_width)]
    for index, (left, right) in enumerate(BLOCKS):
        block = block_ref[index * depth : (index + 1) * depth, :]
        denominator = (
            column_ref[left, rows, :]
            + level_ref[right : right + 1, :]
            - occupied[left]
            - occupied[right]
        )
        ratio = block / denominator
        ratio_ref[index] = ratio
        energy_table[index] = jnp.sum(block * ratio)
        weight = weight_table[left * list_width + right]
        if left != right:
            weight = weight + weight_table[right * list_width + left]
        squares = (weight.astype(F32) / width) * (ratio * ratio)
        row_squares[left] = row_squares[left] + squares
        acc_ref[right : right + 1, :] += jnp.sum(squares, axis=0, keepdims=True)
    for s in range(list_width):
        place_ref[rows, :] = row_squares[s]
        acc_ref[s : s + 1, :] += jnp.sum(place_ref[...].T, axis=0, keepdims=True)

    def block_of(pair):
        low = jnp.minimum(packed[pair, 0], packed[pair, 1])
        high = jnp.maximum(packed[pair, 0], packed[pair, 1])
        return jnp.where(low == 0, 0, jnp.where(low == 1, 3, jnp.where(low == 2, 5, 6))) + high

    lane = lax.broadcasted_iota(jnp.int32, (1, width), 1)
    energies = jnp.zeros((1, width), F32)
    for pair in range(pairs):
        energy = -packed[pair, 2].astype(F32) * energy_table[block_of(pair)] / (width * width)
        energies = jnp.where(lane == pair, energy, energies)
    share = pairs // list_width
    for quarter in range(list_width):
        lines = split(acc_ref[quarter : quarter + 1, :]) + split(energies)
        lines.append(jnp.zeros((TAIL - len(lines), width), F32))
        tail = jnp.concatenate(lines, axis=0).astype(jnp.bfloat16)
        for zone in range(out_ref.shape[0] // list_width):
            out_ref[zone * list_width + quarter, : share * depth, :] = jnp.zeros(
                (share * depth, width), jnp.bfloat16
            )
            out_ref[zone * list_width + quarter, share * depth :, :] = tail
    for pair in range(pairs):
        quarter, k = pair // share, pair % share
        live = (packed[pair, 2] > 0).astype(F32)
        value = (-ratio_ref[block_of(pair)] * live).astype(jnp.bfloat16)
        out_ref[target * list_width + quarter, k * depth : (k + 1) * depth, :] = value


def pair_terms(blocks, levels, packed, occupied, place):
    height, width = blocks.shape
    depth = height // len(BLOCKS)
    list_width = levels.shape[0]
    whole = pl.BlockSpec(memory_space=pltpu.VMEM)
    scalar = pl.BlockSpec(memory_space=pltpu.SMEM)
    rows = packed.shape[0] // list_width * depth + TAIL
    return pl.pallas_call(
        pair_kernel,
        out_shape=jax.ShapeDtypeStruct((4 * list_width, rows, width), jnp.bfloat16),
        in_specs=[scalar, scalar, scalar, whole, whole],
        out_specs=whole,
        scratch_shapes=[
            pltpu.VMEM((len(BLOCKS), depth, width), F32),
            pltpu.VMEM((list_width, width, width), F32),
            pltpu.VMEM((width, width), F32),
            pltpu.VMEM((list_width, width), F32),
            pltpu.SMEM((list_width * list_width,), jnp.int32),
            pltpu.SMEM((len(BLOCKS),), F32),
        ],
        compiler_params=pltpu.CompilerParams(vmem_limit_bytes=VMEM_LIMIT),
        name="pair_terms",
    )(packed, occupied, place, blocks, levels)


def owner_kernel(place, parts_ref, terms_ref, energy_ref):
    sources, height, width = parts_ref.shape
    zones = sources // 4
    share = energy_ref.shape[0]

    def tail(source):
        lines = parts_ref[source, height - TAIL :, :].astype(F32)
        return lines[0:1] + (lines[1:2] + lines[2:3]), lines[3:4] + (lines[4:5] + lines[5:6])

    vectors = []
    for s in range(4):
        vector = tail(s)[0]
        for q in range(1, zones):
            vector = vector + tail(q * 4 + s)[0]
        vectors.append(vector)
    tile = jnp.concatenate(vectors + vectors, axis=0)
    for k in range(terms_ref.shape[0] // 8):
        terms_ref[8 * k : 8 * k + 8, :] = tile
    energies = tail(place[0])[1]
    for q in range(1, zones):
        energies = energies + tail(q * 4 + place[0])[1]
    lane = lax.broadcasted_iota(jnp.int32, (1, width), 1)
    for k in range(share):
        energy_ref[k] = jnp.sum(jnp.where(lane == place[1] * share + k, energies, 0.0))


def owner_terms(parts, place, lines, share):
    whole = pl.BlockSpec(memory_space=pltpu.VMEM)
    scalar = pl.BlockSpec(memory_space=pltpu.SMEM)
    return pl.pallas_call(
        owner_kernel,
        out_shape=(
            jax.ShapeDtypeStruct((lines, parts.shape[2]), F32),
            jax.ShapeDtypeStruct((share,), F32),
        ),
        in_specs=[scalar, whole],
        out_specs=(whole, scalar),
        compiler_params=pltpu.CompilerParams(vmem_limit_bytes=VMEM_LIMIT),
        name="owner_terms",
    )(place, parts)


def join_kernel(slots, place, parts_ref, out_ref):
    share, width, _ = out_ref.shape
    sources, height, _ = parts_ref.shape
    depth = (height - TAIL) // share
    for k in range(share):
        block = jnp.concatenate(
            [
                parts_ref[q * 4 + place[0], k * depth : (k + 1) * depth, :].astype(F32)
                for q in range(sources // 4)
            ],
            axis=0,
        )
        pair = place[1] * share + k
        swapped = slots[pair, 0] > slots[pair, 1]
        out_ref[k] = jnp.where(swapped, block.T, block).astype(jnp.bfloat16)


def join_amplitudes(parts, pair_slots, place, share):
    whole = pl.BlockSpec(memory_space=pltpu.VMEM)
    scalar = pl.BlockSpec(memory_space=pltpu.SMEM)
    width = parts.shape[2]
    return pl.pallas_call(
        join_kernel,
        out_shape=jax.ShapeDtypeStruct((share, width, width), jnp.bfloat16),
        in_specs=[scalar, scalar, whole],
        out_specs=whole,
        compiler_params=pltpu.CompilerParams(vmem_limit_bytes=VMEM_LIMIT),
        name="join_amplitudes",
    )(pair_slots, place, parts)


def grad_kernel(owner_ref, terms_ref, out_ref):
    occ_local = out_ref.shape[0]
    lines = owner_ref.shape[1]
    chosen = (
        lax.broadcasted_iota(jnp.int32, (occ_local, lines), 0) == owner_ref[...]
    ).astype(F32)
    out_ref[...] = jnp.dot(
        chosen, terms_ref[...], preferred_element_type=F32, precision=lax.Precision.HIGHEST
    )


def sum_grads(terms, line_owner, occ_local):
    whole = pl.BlockSpec(memory_space=pltpu.VMEM)
    return pl.pallas_call(
        grad_kernel,
        out_shape=jax.ShapeDtypeStruct((occ_local, terms.shape[1]), F32),
        in_specs=[whole, whole],
        out_specs=whole,
        compiler_params=pltpu.CompilerParams(vmem_limit_bytes=VMEM_LIMIT),
        name="sum_grads",
    )(line_owner, terms)


def on_device(
    half_integrals,
    domain_map,
    domain_index,
    owner_orbitals,
    pair_slots,
    pair_weight,
    virtual_energy,
    occupied_energy,
):
    position = {name: lax.axis_index(name) for name in AXES}
    size = {name: lax.axis_size(name) for name in AXES}
    x = position["x"]

    def aux_rank(zh):
        rank = zh
        for name in AXES[1:-1]:
            rank = rank * size[name] + position[name]
        return rank

    occ_local, rows, width = half_integrals.shape
    owners, list_width = owner_orbitals.shape
    share = pair_slots.shape[0] // size["x"]
    cross = [(q * 4 + s, s * 4 + q) for q in range(4) for s in range(4)]

    packed = lax.ppermute(
        jnp.concatenate([pair_slots, pair_weight[:, None]], axis=1), ("zh", "x"), cross
    )
    own = lax.dynamic_slice_in_dim(owner_orbitals, x, 1, 1)[:, 0] - x * occ_local
    grid = own.reshape([size[name] for name in AXES[:-1]])
    order = grid.transpose(1, 3, 4, 0, 2).reshape(-1)
    line_owner = grid.transpose(1, 2, 3, 4, 0).reshape(1, -1)

    my_orbitals = lax.dynamic_slice_in_dim(owner_orbitals, aux_rank(x), 1, 0)[0]
    my_index = domain_index[my_orbitals]
    virt_count = virtual_energy.shape[0]
    levels = jnp.where(
        my_index >= 0, virtual_energy[jnp.clip(my_index, 0, virt_count - 1)], jnp.float32(1.0)
    )
    occupied = occupied_energy[my_orbitals]

    outgoing = make_slabs(half_integrals, domain_map, domain_index, order, x)
    inner = ("zl", "yl", "c", "x")
    members = size["zl"] * size["yl"] * size["c"] * size["x"]
    per_member = owners // members
    received = lax.all_to_all(
        outgoing.reshape(members, per_member * width, rows),
        inner,
        split_axis=0,
        concat_axis=0,
        tiled=True,
    )
    scaled = partial_grams(
        received.reshape(members // size["x"], list_width, per_member, width, rows)
    )
    depth = scaled.shape[2]
    sent = scaled.astype(jnp.float16).reshape(-1, depth, width)
    arrived = lax.all_to_all(sent, ("zh", "yh"), split_axis=0, concat_axis=0, tiled=True)
    power = arrived[:, depth - TAIL : depth - TAIL + 1, :].astype(F32) - TOP_POWER
    blocks = jnp.sum(arrived[:, : depth - TAIL, :].astype(F32) * jnp.exp2(power), axis=0)

    place = jnp.stack([position["zh"], x]).astype(jnp.int32)
    sent_terms = pair_terms(blocks, levels, packed, occupied, place)
    parts = lax.all_to_all(sent_terms, ("zh", "x"), split_axis=0, concat_axis=0, tiled=True)
    lines, pair_energy = owner_terms(parts, place, owners, share)
    all_lines = lax.all_to_all(
        lines, ("zl", "yh", "yl", "c"), split_axis=0, concat_axis=0, tiled=True
    )
    amplitude = join_amplitudes(parts, pair_slots, place, share)
    domain_grad = sum_grads(all_lines, line_owner, occ_local)
    return (amplitude, pair_energy, domain_grad)


def solution(mesh):
    fine = jax.sharding.Mesh(mesh.devices.reshape(4, 2, 4, 2, 2, 4), AXES)
    aux, orb = AXES[:-1], "x"
    placed = (
        P(orb, aux, None),
        P(orb, None, None),
        P(),
        P(),
        P(aux, None),
        P(aux),
        P(),
        P(),
    )
    return jax.shard_map(
        on_device,
        mesh=fine,
        in_specs=placed,
        out_specs=(P(AXES, None, None), P(AXES), P(orb, None)),
        check_vma=False,
    )
```

time: 233 us -> 232 us (level)
  blocking collectives: 106 us -> 131 us
  starting transfers between devices: 53.2 us -> 30.8 us
  local copies, waits for them, and re-layouts: 10.4 us -> 6.38 us
    all_to_all x1 -> x2, blocking collectives: 106 us -> 131 us  [the longest x1 106 us: on_device(): lax.all_to_all(outgoing.reshape(members, per_member * width, rows), inner...]
    ppermute x4 -> x0, starting transfers between devices: 19 us -> none  [on_device(): lax.ppermute(piece, ('zh', 'x'), [(q * 4 + s, s * 4 + (q + k) % 4) for q...]
    all_to_all x1, waiting for transfers between devices: 0.01 us -> 6.23 us  [on_device(): lax.all_to_all(lines, ('zl', 'yh', 'yl', 'c'), split_axis=0, concat_axis=...]
    unnamed x17 -> x11, local copies, waits for them, and re-layouts: 3.78 us -> 0.12 us
    ppermute x4 -> x0, waiting for transfers between devices: 3.63 us -> none  [on_device(): lax.ppermute(piece, ('zh', 'x'), [(q * 4 + s, s * 4 + (q + k) % 4) for q...]
    all_to_all x1, waiting for transfers between devices: 31.1 us -> 27.5 us  [on_device(): lax.all_to_all(sent, ('zh', 'yh'), split_axis=0, concat_axis=0, tiled=True)]
    all_to_all x1, starting transfers between devices: 22.6 us -> 19.2 us  [on_device(): lax.all_to_all(lines, ('zl', 'yh', 'yl', 'c'), split_axis=0, concat_axis=...]
    pallas_call x3 -> x4, Pallas kernels: 11.7 us -> 14.1 us  [the longest x1 11 us: make_slabs(): pl.pallas_call(slab_kernel, out_shape=jax.ShapeDtypeStruct((owners, width...]
  transfers between devices with their start and end apart: 7 -> 3, of which waited for: 3 -> 2; matrix products, arithmetic and copies ran while one was open for 3% -> 3% of each run, Pallas kernels for 1% -> 1%
where the time goes in v3:
time: 232 us; the launch traced here: 231 us
  blocking collectives  131 us (56%)
  waiting for transfers between devices  33.7 us (15%)
  starting transfers between devices  30.8 us (13%)
  Pallas kernels  24.9 us (11%)
  local copies, waits for them, and re-layouts  6.38 us (3%)
  other arithmetic  3.07 us (1%)
    all_to_all x1, blocking collectives, on_device(): lax.all_to_all(outgoing.reshape(members, per_member * width, rows), inner...  106 us
    all_to_all x1, waiting for transfers between devices, on_device(): lax.all_to_all(sent, ('zh', 'yh'), split_axis=0, concat_axis=0, tiled=True)  27.5 us
    all_to_all x1, blocking collectives, on_device(): lax.all_to_all(sent_terms, ('zh', 'x'), split_axis=0, concat_axis=0, tile...  25.1 us
    all_to_all x1, starting transfers between devices, on_device(): lax.all_to_all(lines, ('zl', 'yh', 'yl', 'c'), split_axis=0, concat_axis=...  19.2 us
    pallas_call x1, Pallas kernels, make_slabs(): pl.pallas_call(slab_kernel, out_shape=jax.ShapeDtypeStruct((owners, width...  11 us
    all_to_all x1, starting transfers between devices, on_device(): lax.all_to_all(sent, ('zh', 'yh'), split_axis=0, concat_axis=0, tiled=True)  10.9 us
    pallas_call x1, Pallas kernels, partial_grams(): pl.pallas_call(gram_kernel, out_shape=jax.ShapeDtypeStruct((pieces, owner...  9.37 us
    all_to_all x1, waiting for transfers between devices, on_device(): lax.all_to_all(lines, ('zl', 'yh', 'yl', 'c'), split_axis=0, concat_axis=...  6.23 us
  transfers between devices with their start and end apart: 3, of which 2 were waited for; matrix products, arithmetic and copies ran while one was open for 3% of the time, Pallas kernels for 1%

profile of v3, /device:TPU:1, one launch (start us, length us, event | category | flops | bytes accessed | tf_op | source)
XLA Modules:
  0.0 230.9 jit_solution(2277675683081540622)
XLA Ops:
  0.7 0.7 subtract_reduce_fusion
  1.4 0.2 sub.16
  1.6 0.2 copy.31
  1.9 0.6 pad_add_fusion.1.scalars
  2.5 11.0 %slabs.1 = bf16[128,128,256]{2,1,0:T(8,128)(2,1)} custom-call(s32[129]{0:T(256)} %pad_add_fusion.1.scalars, bf16[32,256,128]{2,1,0:T(8,128)(2,1)} %integral_ref.1, bf16[32,128,128]{2,1,0:T(8,128)(2,1)} %map_ref.1, s32[128,128]{1,0:T(8,128)} %index_ref.1), custom_call_target="tpu_custom_call" | custom-call | tf_op jit(solution)/shard_map/slabs/pallas_call | solution.py:49
  13.6 106.1 %all_to_all.26 = bf16[32,512,256]{2,1,0:T(8,128)(2,1)} all-to-all(bf16[32,512,256]{2,1,0:T(8,128)(2,1)} %bitcast.23), channel_id=1, replica_groups=mesh['zh'=4,'zl'=2,'yh'=4,'yl'=2,'c'=2,'x'=4] {'zl','yl','c','x'}, dimensions={0} | all-to-all | bytes 16777216 | tf_op jit(solution)/shard_map/all_to_all | solution.py:389
  119.7 9.4 %partial_grams.1 = f32[4,4,336,128]{3,2,1,0:T(8,128)S(1)} custom-call(bf16[8,4,4,128,256]{4,3,2,1,0:T(8,128)(2,1)} %bitcast.24), custom_call_target="tpu_custom_call" | custom-call | tf_op jit(solution)/shard_map/partial_grams/pallas_call | solution.py:125
  129.1 1.3 convert_element_type.9
  130.4 10.9 %all-to-all-start.1 = ((f16[16,336,128]{2,1,0:T(8,128)(2,1)}), f16[16,336,128]{2,1,0:T(8,128)(2,1)S(1)}, u32[]{:S(2)}, u32[]{:S(2)}) async-start(f16[16,336,128]{2,1,0:T(8,128)(2,1)} %bitcast.7), calls=%async_computation.1 | async-start | bytes 2752512 | tf_op jit(solution)/shard_map/all_to_all | solution.py:401
  141.5 0.7 collective-permute-start
  142.2 0.2 dynamic-slice_reduce_fusion
  142.4 1.4 gather_fusion.1
  143.8 0.6 gather_fusion
  144.4 3.1 %gather_fusion.2 = f32[512]{0:T(512)S(1)} fusion(f32[25000]{0:T(1024)S(1)} %copy-done, s32[1024]{0:T(1024)S(1)} %pad_clamp_fusion), kind=kCustom, calls=%fused_computation.2 | custom fusion | bytes 6144 | tf_op jit(solution)/shard_map/gather | solution.py:381
  147.7 27.5 %all-to-all-done.1 = f16[16,336,128]{2,1,0:T(8,128)(2,1)S(1)} async-done(((f16[16,336,128]{2,1,0:T(8,128)(2,1)}), f16[16,336,128]{2,1,0:T(8,128)(2,1)S(1)}, u32[]{:S(2)}, u32[]{:S(2)}) %all-to-all-start.1) | async-done | bytes 1376288 | tf_op jit(solution)/shard_map/all_to_all | solution.py:401
  175.2 0.3 multiply_reduce_fusion.block_ref
  175.4 1.1 pair_terms.1
  176.6 25.1 %all_to_all.27.parts_ref = bf16[16,144,128]{2,1,0:T(8,128)(2,1)S(1)} all-to-all(bf16[16,144,128]{2,1,0:T(8,128)(2,1)S(1)} %pair_terms.1), channel_id=1, replica_groups=mesh['zh'=4,'zl'=2,'yh'=4,'yl'=2,'c'=2,'x'=4] {'zh','x'}, dimensions={0} | all-to-all | bytes 1179648 | tf_op jit(solution)/shard_map/all_to_all | solution.py:407
  201.6 1.2 owner_terms.1
  202.8 19.2 %all-to-all-start.3 = ((f32[32,4,128]{2,1,0:T(4,128)}), f32[32,4,128]{2,1,0:T(4,128)S(1)}, u32[]{:S(2)}, u32[]{:S(2)}) async-start(f32[32,4,128]{2,1,0:T(4,128)} %bitcast.13), calls=%async_computation.3 | async-start | bytes 131072 | tf_op jit(solution)/shard_map/all_to_all | solution.py:409
  222.1 0.2 copy.34
  222.5 1.4 join_amplitudes.1
  223.9 6.2 %all-to-all-done.3 = f32[32,4,128]{2,1,0:T(4,128)S(1)} async-done(((f32[32,4,128]{2,1,0:T(4,128)}), f32[32,4,128]{2,1,0:T(4,128)S(1)}, u32[]{:S(2)}, u32[]{:S(2)}) %all-to-all-start.3) | async-done | bytes 65568 | tf_op jit(solution)/shard_map/all_to_all | solution.py:409
  230.1 0.8 sum_grads.1
  (24 shorter events, 0.6 us)
Async XLA Ops:
  0.6 143.8 %copy-start = (f32[25000]{0:T(1024)S(1)}, f32[25000]{0:T(1024)}, u32[]{:S(2)}) copy-start(f32[25000]{0:T(1024)} %param.14) | copy-start | bytes 300004
  129.1 12.3 %copy-start.2 = (s32[16,2]{0,1:T(2,128)S(1)}, s32[16,2]{0,1:T(2,128)}, u32[]{:S(2)}) copy-start(s32[16,2]{0,1:T(2,128)} %param.12) | copy-start | bytes 388
  129.1 12.3 %copy-start.4 = (s32[16]{0:T(128)S(1)}, s32[16]{0:T(128)}, u32[]{:S(2)}) copy-start(s32[16]{0:T(128)} %param.13) | copy-start | bytes 196
  129.1 13.0 %copy-start.3 = (s32[128,4]{0,1:T(4,128)S(1)}, s32[128,4]{0,1:T(4,128)}, u32[]{:S(2)}) copy-start(s32[128,4]{0,1:T(4,128)} %param.11) | copy-start | bytes 6148
  129.1 14.6 %copy-start.1 = (f32[128]{0:T(128)S(1)}, f32[128]{0:T(128)}, u32[]{:S(2)}) copy-start(f32[128]{0:T(128)} %param.15) | copy-start | bytes 1540
  130.4 44.7 %all-to-all-start.1 = ((f16[16,336,128]{2,1,0:T(8,128)(2,1)}), f16[16,336,128]{2,1,0:T(8,128)(2,1)S(1)}, u32[]{:S(2)}, u32[]{:S(2)}) async-start(f16[16,336,128]{2,1,0:T(8,128)(2,1)} %bitcast.7), calls=%async_computation.1 | async-start | bytes 2752512 | tf_op jit(solution)/shard_map/all_to_all | solution.py:401
  141.5 34.0 %collective-permute-start = (s32[16,3]{1,0:T(8,128)S(1)}, s32[16,3]{1,0:T(8,128)S(1)}, u32[]{:S(2)}, u32[]{:S(2)}) collective-permute-start(s32[16,3]{1,0:T(8,128)S(1)} %copy.30), channel_id=1, source_target_pairs={{0,0},{1,128},{2,256},{3,384},{128,1},{129,129},{130,257},{131,385... | collective-permute-start | bytes 584 | tf_op jit(solution)/shard_map/ppermute | solution.py:369
  202.8 27.3 %all-to-all-start.3 = ((f32[32,4,128]{2,1,0:T(4,128)}), f32[32,4,128]{2,1,0:T(4,128)S(1)}, u32[]{:S(2)}, u32[]{:S(2)}) async-start(f32[32,4,128]{2,1,0:T(4,128)} %bitcast.13), calls=%async_computation.3 | async-start | bytes 131072 | tf_op jit(solution)/shard_map/all_to_all | solution.py:409

commit v4 on v3

--- a/solution.py
+++ b/solution.py
@@ -10,25 +10,28 @@
 F32 = jnp.float32
 VMEM_LIMIT = 48 * 1024 * 1024
 SLAB_VMEM_LIMIT = 62 * 1024 * 1024
-OWNERS_PER_STEP = 8
-ORBS_PER_STEP = 8
+OWNERS_PER_STEP = 32
+ORBS_PER_STEP = 16
+GRAMS_PER_STEP = 2
 AXES = ("zh", "zl", "yh", "yl", "c", "x")
 BLOCKS = tuple((s, t) for s in range(4) for t in range(s, 4))
 TAIL = 16
 TOP_POWER = 14.0
 
 
-def slab_kernel(scalars, integral_ref, map_ref, index_ref, out_ref, slab_ref):
+def slab_kernel(owner_list, group, integral_ref, map_ref, index_ref, out_ref, slab_ref):
     orbs = integral_ref.shape[0]
+    occ_local = slab_ref.shape[0]
     per_step = out_ref.shape[0]
     step = pl.program_id(0)
-    first_write = slab_ref.shape[0] // orbs
+    first_write = occ_local // orbs
+    first_orb = group[0] * occ_local
 
     @pl.when(step < first_write)
     def _():
         for k in range(orbs):
             orb = step * orbs + k
-            live = index_ref[pl.ds(scalars[0] * slab_ref.shape[0] + orb, 1), :] >= 0
+            live = index_ref[pl.ds(first_orb + orb, 1), :] >= 0
             masked = map_ref[k] * live.astype(F32).astype(jnp.bfloat16)
             slab_ref[orb] = lax.dot_general(
                 masked.T, integral_ref[k], (((1,), (1,)), ((), ())), preferred_element_type=F32
@@ -36,103 +39,104 @@
 
     @pl.when(step >= first_write)
     def _():
+        part = step - first_write
+        base = jnp.right_shift(part, 1) * 16 + jnp.bitwise_and(part, 1) * 2
         for k in range(per_step):
-            out_ref[k] = slab_ref[scalars[1 + (step - first_write) * per_step + k]]
-
-
-def make_slabs(half_integrals, domain_map, domain_index, own_local, orb_group):
+            owner = base + (k // 4 % 4) * 32 + (k % 4) * 4 + k // 16
+            out_ref[k] = slab_ref[owner_list[group[0], owner] - first_orb]
+
+
+def make_slabs(half_integrals, domain_map, domain_index, owner_orbitals, orb_group):
     occ_local, rows, width = half_integrals.shape
-    owners = own_local.shape[0]
-    scalars = jnp.concatenate([orb_group[None].astype(jnp.int32), own_local])
+    owners = owner_orbitals.shape[0]
     parts = occ_local // ORBS_PER_STEP
-    read = lambda i, s: (jnp.minimum(i, parts - 1), 0, 0)
+    read = lambda i, s, t: (jnp.minimum(i, parts - 1), 0, 0)
     return pl.pallas_call(
         slab_kernel,
         out_shape=jax.ShapeDtypeStruct((owners, width, rows), jnp.bfloat16),
         grid_spec=pltpu.PrefetchScalarGridSpec(
-            num_scalar_prefetch=1,
+            num_scalar_prefetch=2,
             grid=(parts + owners // OWNERS_PER_STEP,),
             in_specs=[
                 pl.BlockSpec((ORBS_PER_STEP, rows, width), read),
                 pl.BlockSpec((ORBS_PER_STEP, width, width), read),
-                pl.BlockSpec(domain_index.shape, lambda i, s: (0, 0)),
+                pl.BlockSpec(domain_index.shape, lambda i, s, t: (0, 0)),
             ],
             out_specs=pl.BlockSpec(
-                (OWNERS_PER_STEP, width, rows), lambda i, s: (jnp.maximum(i - parts, 0), 0, 0)
+                (OWNERS_PER_STEP, width, rows), lambda i, s, t: (jnp.maximum(i - parts, 0), 0, 0)
             ),
             scratch_shapes=[pltpu.VMEM((occ_local, width, rows), jnp.bfloat16)],
         ),
         compiler_params=pltpu.CompilerParams(vmem_limit_bytes=SLAB_VMEM_LIMIT),
         name="slabs",
-    )(scalars, half_integrals, domain_map, domain_index)
-
-
-def gram_kernel(slab_ref, out_ref, gram_ref):
-    step = pl.program_id(1)
-    count, list_width, _, width, rows = slab_ref.shape
+    )(
+        owner_orbitals.T,
+        orb_group[None].astype(jnp.int32),
+        half_integrals,
+        domain_map,
+        domain_index,
+    )
+
+
+def gram_kernel(slab_ref, out_ref):
+    count, list_width, owners, width, rows = slab_ref.shape
     half = list_width * width // 2
     middle = list_width // 2
-    low = jnp.concatenate(
-        [slab_ref[k, :middle, 0].reshape(half, rows) for k in range(count)], axis=1
-    )
-    high = jnp.concatenate(
-        [slab_ref[k, middle:, 0].reshape(half, rows) for k in range(count)], axis=1
-    )
     product = functools.partial(
         lax.dot_general,
         dimension_numbers=(((1,), (1,)), ((), ())),
         preferred_element_type=F32,
     )
-    parts = (product(low, low), product(low, high), product(high, high))
-
-    @pl.when(step == 0)
-    def _():
-        for k in range(3):
-            gram_ref[k] = parts[k]
-
-    @pl.when(step > 0)
-    def _():
-        for k in range(3):
-            gram_ref[k] += parts[k]
-
-    @pl.when(step == pl.num_programs(1) - 1)
-    def _():
-        top = jnp.max(jnp.max(jnp.abs(gram_ref[...]), axis=0), axis=0, keepdims=True)
-        top = jnp.max(top, axis=1, keepdims=True)
+    pieces = out_ref.shape[0]
+    depth = width // pieces
+    base = len(BLOCKS) * depth
+    for j in range(owners):
+        low = jnp.concatenate(
+            [slab_ref[k, :middle, j].reshape(half, rows) for k in range(count)], axis=1
+        )
+        high = jnp.concatenate(
+            [slab_ref[k, middle:, j].reshape(half, rows) for k in range(count)], axis=1
+        )
+        parts = (product(low, low), product(low, high), product(high, high))
+
+        def block_at(left, right):
+            row, column = left % 2 * width, right % 2 * width
+            return parts[left // 2 + right // 2][row : row + width, column : column + width]
+
+        top = jnp.zeros((8, width), F32)
+        for s in range(list_width):
+            top = jnp.maximum(
+                top, jnp.max(jnp.abs(block_at(s, s)).reshape(width // 8, 8, width), axis=0)
+            )
+        top = jnp.max(jnp.max(top, axis=0, keepdims=True), axis=1, keepdims=True)
         power = jnp.clip(jnp.ceil(jnp.log2(jnp.maximum(top, 1e-35))), -100.0, 100.0)
         power = jnp.broadcast_to(power, (8, width))
-        scale = jnp.exp2(TOP_POWER - power)
-        pieces = out_ref.shape[0]
-        depth = width // pieces
+        scale = jnp.exp2(TOP_POWER - power)[0:1]
         for index, (left, right) in enumerate(BLOCKS):
-            quadrant = left // 2 + right // 2
+            block = block_at(left, right) * scale
             for q in range(pieces):
-                row = (left % 2) * width + q * depth
-                column = (right % 2) * width
-                block = gram_ref[quadrant, row : row + depth, column : column + width]
-                out_ref[q, 0, index * depth : (index + 1) * depth, :] = block * scale[0:1]
+                out_ref[q, j, index * depth : (index + 1) * depth, :] = block[
+                    q * depth : (q + 1) * depth
+                ]
         for q in range(pieces):
-            base = len(BLOCKS) * depth
-            out_ref[q, 0, base : base + 8, :] = power
-            out_ref[q, 0, base + 8 : base + TAIL, :] = power
+            out_ref[q, j, base : base + 8, :] = power
+            out_ref[q, j, base + 8 : base + TAIL, :] = power
 
 
 def partial_grams(slabs):
     count, list_width, owners, width, rows = slabs.shape
     pieces = 4
     depth = len(BLOCKS) * (width // pieces) + TAIL
-    steps = 2
     return pl.pallas_call(
         gram_kernel,
         out_shape=jax.ShapeDtypeStruct((pieces, owners, depth, width), F32),
-        grid=(owners, steps),
+        grid=(owners // GRAMS_PER_STEP,),
         in_specs=[
             pl.BlockSpec(
-                (count // steps, list_width, 1, width, rows), lambda j, h: (h, 0, j, 0, 0)
+                (count, list_width, GRAMS_PER_STEP, width, rows), lambda j: (0, 0, j, 0, 0)
             )
         ],
-        out_specs=pl.BlockSpec((pieces, 1, depth, width), lambda j, h: (0, j, 0, 0)),
-        scratch_shapes=[pltpu.VMEM((3, list_width * width // 2, list_width * width // 2), F32)],
+        out_specs=pl.BlockSpec((pieces, GRAMS_PER_STEP, depth, width), lambda j: (0, j, 0, 0)),
         compiler_params=pltpu.CompilerParams(vmem_limit_bytes=VMEM_LIMIT),
         name="partial_grams",
     )(slabs)
@@ -161,7 +165,7 @@
     list_width, width = level_ref.shape
     depth = block_ref.shape[0] // len(BLOCKS)
     pairs = packed.shape[0]
-    piece, target = place[0], place[1]
+    piece = place[0]
     rows = pl.ds(pl.multiple_of(piece * depth, depth), depth)
     for k in range(list_width * list_width):
         weight_table[k] = 0
@@ -208,16 +212,12 @@
         lines = split(acc_ref[quarter : quarter + 1, :]) + split(energies)
         lines.append(jnp.zeros((TAIL - len(lines), width), F32))
         tail = jnp.concatenate(lines, axis=0).astype(jnp.bfloat16)
-        for zone in range(out_ref.shape[0] // list_width):
-            out_ref[zone * list_width + quarter, : share * depth, :] = jnp.zeros(
-                (share * depth, width), jnp.bfloat16
-            )
-            out_ref[zone * list_width + quarter, share * depth :, :] = tail
+        out_ref[quarter, share * depth :, :] = tail
     for pair in range(pairs):
         quarter, k = pair // share, pair % share
         live = (packed[pair, 2] > 0).astype(F32)
         value = (-ratio_ref[block_of(pair)] * live).astype(jnp.bfloat16)
-        out_ref[target * list_width + quarter, k * depth : (k + 1) * depth, :] = value
+        out_ref[quarter, k * depth : (k + 1) * depth, :] = value
 
 
 def pair_terms(blocks, levels, packed, occupied, place):
@@ -229,7 +229,7 @@
     rows = packed.shape[0] // list_width * depth + TAIL
     return pl.pallas_call(
         pair_kernel,
-        out_shape=jax.ShapeDtypeStruct((4 * list_width, rows, width), jnp.bfloat16),
+        out_shape=jax.ShapeDtypeStruct((list_width, rows, width), jnp.bfloat16),
         in_specs=[scalar, scalar, scalar, whole, whole],
         out_specs=whole,
         scratch_shapes=[
@@ -245,30 +245,54 @@
     )(packed, occupied, place, blocks, levels)
 
 
+def plane_kernel(parts_ref, out_ref):
+    owners, height, width = parts_ref.shape
+    body = height - TAIL
+    tails = [parts_ref[s, body:, :].astype(F32) for s in range(owners)]
+    vectors = [tails[s][k : k + 1] for k in range(3) for s in range(owners)]
+    per_zone = out_ref.shape[0] // owners
+    for s in range(owners):
+        lines = vectors + [tails[s][3:6], jnp.zeros((TAIL - 3 * owners - 3, width), F32)]
+        tail = jnp.concatenate(lines, axis=0).astype(jnp.bfloat16)
+        for k in range(per_zone):
+            out_ref[s * per_zone + k, :body, :] = parts_ref[s, :body, :]
+            out_ref[s * per_zone + k, body:, :] = tail
+
+
+def plane_terms(parts, planes):
+    whole = pl.BlockSpec(memory_space=pltpu.VMEM)
+    return pl.pallas_call(
+        plane_kernel,
+        out_shape=jax.ShapeDtypeStruct((planes,) + parts.shape[1:], parts.dtype),
+        in_specs=[whole],
+        out_specs=whole,
+        compiler_params=pltpu.CompilerParams(vmem_limit_bytes=VMEM_LIMIT),
+        name="plane_terms",
+    )(parts)
+
+
 def owner_kernel(place, parts_ref, terms_ref, energy_ref):
-    sources, height, width = parts_ref.shape
-    zones = sources // 4
+    planes, height, width = parts_ref.shape
     share = energy_ref.shape[0]
-
-    def tail(source):
-        lines = parts_ref[source, height - TAIL :, :].astype(F32)
-        return lines[0:1] + (lines[1:2] + lines[2:3]), lines[3:4] + (lines[4:5] + lines[5:6])
-
-    vectors = []
-    for s in range(4):
-        vector = tail(s)[0]
-        for q in range(1, zones):
-            vector = vector + tail(q * 4 + s)[0]
-        vectors.append(vector)
-    tile = jnp.concatenate(vectors + vectors, axis=0)
+    body = height - TAIL
+    sums = []
+    for low in range(2):
+        total = None
+        for q in range(planes // 2):
+            tail = parts_ref[q * 2 + low, body:, :].astype(F32)
+            vectors = tail[0:4] + (tail[4:8] + tail[8:12])
+            total = vectors if total is None else total + vectors
+        sums.append(total)
+    tile = jnp.concatenate(sums, axis=0)
     for k in range(terms_ref.shape[0] // 8):
         terms_ref[8 * k : 8 * k + 8, :] = tile
-    energies = tail(place[0])[1]
-    for q in range(1, zones):
-        energies = energies + tail(q * 4 + place[0])[1]
+    energies = jnp.zeros((1, width), F32)
+    for q in range(planes // 2):
+        tail = parts_ref[q * 2 + place[1], body:, :].astype(F32)
+        energies = energies + (tail[12:13] + (tail[13:14] + tail[14:15]))
     lane = lax.broadcasted_iota(jnp.int32, (1, width), 1)
     for k in range(share):
-        energy_ref[k] = jnp.sum(jnp.where(lane == place[1] * share + k, energies, 0.0))
+        energy_ref[k] = jnp.sum(jnp.where(lane == place[2] * share + k, energies, 0.0))
 
 
 def owner_terms(parts, place, lines, share):
@@ -294,12 +318,12 @@
     for k in range(share):
         block = jnp.concatenate(
             [
-                parts_ref[q * 4 + place[0], k * depth : (k + 1) * depth, :].astype(F32)
-                for q in range(sources // 4)
+                parts_ref[q * 2 + place[1], k * depth : (k + 1) * depth, :].astype(F32)
+                for q in range(sources // 2)
             ],
             axis=0,
         )
-        pair = place[1] * share + k
+        pair = place[2] * share + k
         swapped = slots[pair, 0] > slots[pair, 1]
         out_ref[k] = jnp.where(swapped, block.T, block).astype(jnp.bfloat16)
 
@@ -371,8 +395,7 @@
     )
     own = lax.dynamic_slice_in_dim(owner_orbitals, x, 1, 1)[:, 0] - x * occ_local
     grid = own.reshape([size[name] for name in AXES[:-1]])
-    order = grid.transpose(1, 3, 4, 0, 2).reshape(-1)
-    line_owner = grid.transpose(1, 2, 3, 4, 0).reshape(1, -1)
+    line_owner = grid.transpose(2, 3, 4, 1, 0).reshape(1, -1)
 
     my_orbitals = lax.dynamic_slice_in_dim(owner_orbitals, aux_rank(x), 1, 0)[0]
     my_index = domain_index[my_orbitals]
@@ -382,7 +405,7 @@
     )
     occupied = occupied_energy[my_orbitals]
 
-    outgoing = make_slabs(half_integrals, domain_map, domain_index, order, x)
+    outgoing = make_slabs(half_integrals, domain_map, domain_index, owner_orbitals, x)
     inner = ("zl", "yl", "c", "x")
     members = size["zl"] * size["yl"] * size["c"] * size["x"]
     per_member = owners // members
@@ -402,13 +425,13 @@
     power = arrived[:, depth - TAIL : depth - TAIL + 1, :].astype(F32) - TOP_POWER
     blocks = jnp.sum(arrived[:, : depth - TAIL, :].astype(F32) * jnp.exp2(power), axis=0)
 
-    place = jnp.stack([position["zh"], x]).astype(jnp.int32)
-    sent_terms = pair_terms(blocks, levels, packed, occupied, place)
-    parts = lax.all_to_all(sent_terms, ("zh", "x"), split_axis=0, concat_axis=0, tiled=True)
+    place = jnp.stack([position["zh"], position["zl"], x]).astype(jnp.int32)
+    slices = pair_terms(blocks, levels, packed, occupied, place)
+    slices = lax.all_to_all(slices, "x", split_axis=0, concat_axis=0, tiled=True)
+    planes = plane_terms(slices, size["zh"] * size["zl"])
+    parts = lax.all_to_all(planes, ("zh", "zl"), split_axis=0, concat_axis=0, tiled=True)
     lines, pair_energy = owner_terms(parts, place, owners, share)
-    all_lines = lax.all_to_all(
-        lines, ("zl", "yh", "yl", "c"), split_axis=0, concat_axis=0, tiled=True
-    )
+    all_lines = lax.all_to_all(lines, ("yh", "yl", "c"), split_axis=0, concat_axis=0, tiled=True)
     amplitude = join_amplitudes(parts, pair_slots, place, share)
     domain_grad = sum_grads(all_lines, line_owner, occ_local)
     return (amplitude, pair_energy, domain_grad)

time: 232 us -> 220 us (0.948)
  Pallas kernels: 24.9 us -> 17.7 us
  starting transfers between devices: 30.8 us -> 25.4 us
  waiting for transfers between devices: 33.7 us -> 36.2 us
    all_to_all x1, starting transfers between devices: 19.2 us -> 13.8 us  [on_device(): lax.all_to_all(lines, ('yh', 'yl', 'c'), split_axis=0, concat_axis=0, til...]
    pallas_call x1, Pallas kernels: 11 us -> 6.83 us  [make_slabs(): pl.pallas_call(slab_kernel, out_shape=jax.ShapeDtypeStruct((owners, width...]
    pallas_call x1, Pallas kernels: 9.37 us -> 6.36 us  [partial_grams(): pl.pallas_call(gram_kernel, out_shape=jax.ShapeDtypeStruct((pieces, owner...]
    all_to_all x1, waiting for transfers between devices: 27.5 us -> 30.4 us  [on_device(): lax.all_to_all(sent, ('zh', 'yh'), split_axis=0, concat_axis=0, tiled=True)]
    all_to_all x1 -> x2, blocking collectives: 25.1 us -> 25.7 us  [the longest x1 15 us: on_device(): lax.all_to_all(planes, ('zh', 'zl'), split_axis=0, concat_axis=0, tiled=T...]
where the time goes in v4:
time: 220 us
  blocking collectives  132 us (60%)
  waiting for transfers between devices  36.2 us (16%)
  starting transfers between devices  25.4 us (12%)
  Pallas kernels  17.7 us (8%)
  local copies, waits for them, and re-layouts  6.06 us (3%)
    all_to_all x1, blocking collectives, on_device(): lax.all_to_all(outgoing.reshape(members, per_member * width, rows), inner...  106 us
    all_to_all x1, waiting for transfers between devices, on_device(): lax.all_to_all(sent, ('zh', 'yh'), split_axis=0, concat_axis=0, tiled=True)  30.4 us
    all_to_all x1, blocking collectives, on_device(): lax.all_to_all(planes, ('zh', 'zl'), split_axis=0, concat_axis=0, tiled=T...  15 us
    all_to_all x1, starting transfers between devices, on_device(): lax.all_to_all(lines, ('yh', 'yl', 'c'), split_axis=0, concat_axis=0, til...  13.8 us
    all_to_all x1, starting transfers between devices, on_device(): lax.all_to_all(sent, ('zh', 'yh'), split_axis=0, concat_axis=0, tiled=True)  10.9 us
    all_to_all x1, blocking collectives, on_device(): lax.all_to_all(slices, 'x', split_axis=0, concat_axis=0, tiled=True)  10.7 us
    pallas_call x1, Pallas kernels, make_slabs(): pl.pallas_call(slab_kernel, out_shape=jax.ShapeDtypeStruct((owners, width...  6.83 us
    pallas_call x1, Pallas kernels, partial_grams(): pl.pallas_call(gram_kernel, out_shape=jax.ShapeDtypeStruct((pieces, owner...  6.36 us
  transfers between devices with their start and end apart: 3, of which 2 were waited for; matrix products, arithmetic and copies ran while one was open for 3% of the time, Pallas kernels for 1%

profile of v4, /device:TPU:1, one launch (start us, length us, event | category | flops | bytes accessed | tf_op | source)
XLA Modules:
  0.0 219.8 jit_solution(5576599609274058957)
XLA Ops:
  0.7 6.8 %slabs.1 = bf16[128,128,256]{2,1,0:T(8,128)(2,1)} custom-call(s32[4,128]{1,0:T(4,128)} %bitcast.27, s32[1]{0:T(128)} %bitcast.2.group, bf16[32,256,128]{2,1,0:T(8,128)(2,1)} %integral_ref.1, bf16[32,128,128]{2,1,0:T(8,128)(2,1)} %map_ref.1, s32[128,128]{1,0:T(8,128)} %index_ref.1), custom_call_target="tpu_custom_call" | custom-call | tf_op jit(solution)/shard_map/slabs/pallas_call | solution.py:54
  7.5 106.1 %all_to_all.31 = bf16[32,512,256]{2,1,0:T(8,128)(2,1)} all-to-all(bf16[32,512,256]{2,1,0:T(8,128)(2,1)} %bitcast.25), channel_id=1, replica_groups=mesh['zh'=4,'zl'=2,'yh'=4,'yl'=2,'c'=2,'x'=4] {'zl','yl','c','x'}, dimensions={0} | all-to-all | bytes 16777216 | tf_op jit(solution)/shard_map/all_to_all | solution.py:412
  113.6 6.4 %partial_grams.1 = f32[4,4,336,128]{3,2,1,0:T(8,128)S(1)} custom-call(bf16[8,4,4,128,256]{4,3,2,1,0:T(8,128)(2,1)} %bitcast.24), custom_call_target="tpu_custom_call" | custom-call | tf_op jit(solution)/shard_map/partial_grams/pallas_call | solution.py:130
  120.0 1.3 convert_element_type.9
  121.3 10.9 %all-to-all-start.1 = ((f16[16,336,128]{2,1,0:T(8,128)(2,1)}), f16[16,336,128]{2,1,0:T(8,128)(2,1)S(1)}, u32[]{:S(2)}, u32[]{:S(2)}) async-start(f16[16,336,128]{2,1,0:T(8,128)(2,1)} %bitcast.8), calls=%async_computation.1 | async-start | bytes 2752512 | tf_op jit(solution)/shard_map/all_to_all | solution.py:424
  132.3 0.1 copy.26
  132.4 0.7 collective-permute-start
  133.1 0.2 dynamic-slice_reduce_fusion
  133.3 1.4 gather_fusion.1
  134.7 0.6 gather_fusion
  135.4 3.1 %gather_fusion.2 = f32[512]{0:T(512)S(1)} fusion(f32[25000]{0:T(1024)S(1)} %copy-done, s32[1024]{0:T(1024)S(1)} %pad_clamp_fusion), kind=kCustom, calls=%fused_computation.2 | custom fusion | bytes 6144 | tf_op jit(solution)/shard_map/gather | solution.py:404
  138.6 30.4 %all-to-all-done.1 = f16[16,336,128]{2,1,0:T(8,128)(2,1)S(1)} async-done(((f16[16,336,128]{2,1,0:T(8,128)(2,1)}), f16[16,336,128]{2,1,0:T(8,128)(2,1)S(1)}, u32[]{:S(2)}, u32[]{:S(2)}) %all-to-all-start.1) | async-done | bytes 1376288 | tf_op jit(solution)/shard_map/all_to_all | solution.py:424
  169.0 0.3 multiply_reduce_fusion.block_ref
  169.3 1.1 pair_terms.1
  170.4 10.7 %all_to_all.32.parts_ref = bf16[4,144,128]{2,1,0:T(8,128)(2,1)S(1)} all-to-all(bf16[4,144,128]{2,1,0:T(8,128)(2,1)S(1)} %pair_terms.1), channel_id=1, replica_groups=mesh['zh'=4,'zl'=2,'yh'=4,'yl'=2,'c'=2,'x'=4] {'x'}, dimensions={0} | all-to-all | bytes 294912 | tf_op jit(solution)/shard_map/all_to_all | solution.py:430
  181.1 15.0 %all_to_all.33.parts_ref = bf16[8,144,128]{2,1,0:T(8,128)(2,1)S(1)} all-to-all(bf16[8,144,128]{2,1,0:T(8,128)(2,1)S(1)} %plane_terms.1), channel_id=1, replica_groups=mesh['zh'=4,'zl'=2,'yh'=4,'yl'=2,'c'=2,'x'=4] {'zh','zl'}, dimensions={0} | all-to-all | bytes 589824 | tf_op jit(solution)/shard_map/all_to_all | solution.py:432
  196.2 1.2 owner_terms.1
  197.3 13.8 %all-to-all-start.4 = ((f32[16,8,128]{2,1,0:T(8,128)}), f32[16,8,128]{2,1,0:T(8,128)S(1)}, u32[]{:S(2)}, u32[]{:S(2)}) async-start(f32[16,8,128]{2,1,0:T(8,128)} %bitcast.14), calls=%async_computation.4 | async-start | bytes 131072 | tf_op jit(solution)/shard_map/all_to_all | solution.py:434
  211.3 0.2 sub.17
  211.5 0.2 copy.29
  211.7 0.1 reshape.74.owner_ref
  211.8 1.4 join_amplitudes.1
  213.2 5.8 %all-to-all-done.4 = f32[16,8,128]{2,1,0:T(8,128)S(1)} async-done(((f32[16,8,128]{2,1,0:T(8,128)}), f32[16,8,128]{2,1,0:T(8,128)S(1)}, u32[]{:S(2)}, u32[]{:S(2)}) %all-to-all-start.4) | async-done | bytes 65568 | tf_op jit(solution)/shard_map/all_to_all | solution.py:434
  219.0 0.8 sum_grads.1
  (23 shorter events, 0.3 us)
Async XLA Ops:
  0.6 134.7 %copy-start = (f32[25000]{0:T(1024)S(1)}, f32[25000]{0:T(1024)}, u32[]{:S(2)}) copy-start(f32[25000]{0:T(1024)} %param.14) | copy-start | bytes 300004
  120.0 12.3 %copy-start.3 = (s32[16,2]{0,1:T(2,128)S(1)}, s32[16,2]{0,1:T(2,128)}, u32[]{:S(2)}) copy-start(s32[16,2]{0,1:T(2,128)} %param.12) | copy-start | bytes 388
  120.0 12.3 %copy-start.4 = (s32[16]{0:T(128)S(1)}, s32[16]{0:T(128)}, u32[]{:S(2)}) copy-start(s32[16]{0:T(128)} %param.13) | copy-start | bytes 196
  120.0 13.1 %copy-start.2 = (s32[128,4]{0,1:T(4,128)S(1)}, s32[128,4]{0,1:T(4,128)}, u32[]{:S(2)}) copy-start(s32[128,4]{0,1:T(4,128)} %param.11) | copy-start | bytes 6148
  120.0 14.7 %copy-start.1 = (f32[128]{0:T(128)S(1)}, f32[128]{0:T(128)}, u32[]{:S(2)}) copy-start(f32[128]{0:T(128)} %param.15) | copy-start | bytes 1540
  121.3 47.7 %all-to-all-start.1 = ((f16[16,336,128]{2,1,0:T(8,128)(2,1)}), f16[16,336,128]{2,1,0:T(8,128)(2,1)S(1)}, u32[]{:S(2)}, u32[]{:S(2)}) async-start(f16[16,336,128]{2,1,0:T(8,128)(2,1)} %bitcast.8), calls=%async_computation.1 | async-start | bytes 2752512 | tf_op jit(solution)/shard_map/all_to_all | solution.py:424
  132.4 36.9 %collective-permute-start = (s32[16,3]{1,0:T(8,128)S(1)}, s32[16,3]{1,0:T(8,128)S(1)}, u32[]{:S(2)}, u32[]{:S(2)}) collective-permute-start(s32[16,3]{1,0:T(8,128)S(1)} %copy.26), channel_id=1, source_target_pairs={{0,0},{1,128},{2,256},{3,384},{128,1},{129,129},{130,257},{131,385... | collective-permute-start | bytes 584 | tf_op jit(solution)/shard_map/ppermute | solution.py:393
  197.3 21.6 %all-to-all-start.4 = ((f32[16,8,128]{2,1,0:T(8,128)}), f32[16,8,128]{2,1,0:T(8,128)S(1)}, u32[]{:S(2)}, u32[]{:S(2)}) async-start(f32[16,8,128]{2,1,0:T(8,128)} %bitcast.14), calls=%async_computation.4 | async-start | bytes 131072 | tf_op jit(solution)/shard_map/all_to_all | solution.py:434

commit v5 on v4

--- a/solution.py
+++ b/solution.py
@@ -15,6 +15,8 @@
 GRAMS_PER_STEP = 2
 AXES = ("zh", "zl", "yh", "yl", "c", "x")
 BLOCKS = tuple((s, t) for s in range(4) for t in range(s, 4))
+CROSS = tuple((s, t) for s, t in BLOCKS if s < t)
+SENT = len(CROSS) + 2
 TAIL = 16
 TOP_POWER = 14.0
 
@@ -89,7 +91,9 @@
     )
     pieces = out_ref.shape[0]
     depth = width // pieces
-    base = len(BLOCKS) * depth
+    base = SENT * depth
+    line = lax.broadcasted_iota(jnp.int32, (width, width), 0)
+    lane = lax.broadcasted_iota(jnp.int32, (width, width), 1)
     for j in range(owners):
         low = jnp.concatenate(
             [slab_ref[k, :middle, j].reshape(half, rows) for k in range(count)], axis=1
@@ -112,21 +116,30 @@
         power = jnp.clip(jnp.ceil(jnp.log2(jnp.maximum(top, 1e-35))), -100.0, 100.0)
         power = jnp.broadcast_to(power, (8, width))
         scale = jnp.exp2(TOP_POWER - power)[0:1]
-        for index, (left, right) in enumerate(BLOCKS):
-            block = block_at(left, right) * scale
+        blocks = [block_at(left, right) for left, right in CROSS]
+        diagonals = []
+        for s in range(0, list_width, 2):
+            lower = block_at(s + 1, s + 1)
+            blocks.append(jnp.where(lane >= line, block_at(s, s), lower))
+            diagonals.append(
+                jnp.sum(jnp.where(lane == line, lower, 0.0), axis=0, keepdims=True) * scale
+            )
+        tail = jnp.concatenate(diagonals + [power[: 8 - len(diagonals)]], axis=0)
+        for index, block in enumerate(blocks):
+            block = block * scale
             for q in range(pieces):
                 out_ref[q, j, index * depth : (index + 1) * depth, :] = block[
                     q * depth : (q + 1) * depth
                 ]
         for q in range(pieces):
-            out_ref[q, j, base : base + 8, :] = power
+            out_ref[q, j, base : base + 8, :] = tail
             out_ref[q, j, base + 8 : base + TAIL, :] = power
 
 
 def partial_grams(slabs):
     count, list_width, owners, width, rows = slabs.shape
     pieces = 4
-    depth = len(BLOCKS) * (width // pieces) + TAIL
+    depth = SENT * (width // pieces) + TAIL
     return pl.pallas_call(
         gram_kernel,
         out_shape=jax.ShapeDtypeStruct((pieces, owners, depth, width), F32),
@@ -163,7 +176,7 @@
     energy_table,
 ):
     list_width, width = level_ref.shape
-    depth = block_ref.shape[0] // len(BLOCKS)
+    depth = (block_ref.shape[0] - 8) // SENT
     pairs = packed.shape[0]
     piece = place[0]
     rows = pl.ds(pl.multiple_of(piece * depth, depth), depth)
@@ -176,8 +189,23 @@
     acc_ref[...] = jnp.zeros_like(acc_ref)
     place_ref[...] = jnp.zeros_like(place_ref)
     row_squares = [jnp.zeros((depth, width), F32) for _ in range(list_width)]
+    line = lax.broadcasted_iota(jnp.int32, (depth, width), 0) + piece * depth
+    column = lax.broadcasted_iota(jnp.int32, (depth, width), 1)
+
+    def block_at(index):
+        return block_ref[index * depth : (index + 1) * depth, :]
+
     for index, (left, right) in enumerate(BLOCKS):
-        block = block_ref[index * depth : (index + 1) * depth, :]
+        if left != right:
+            block = block_at(CROSS.index((left, right)))
+        else:
+            block = block_at(len(CROSS) + left // 2)
+            if left % 2 == 0:
+                block = jnp.where(column >= line, block, 0.0)
+            else:
+                row = SENT * depth + left // 2
+                inner = jnp.where(column == line, block_ref[row : row + 1, :], 0.0)
+                block = jnp.where(column < line, block, inner)
         denominator = (
             column_ref[left, rows, :]
             + level_ref[right : right + 1, :]
@@ -186,11 +214,12 @@
         )
         ratio = block / denominator
         ratio_ref[index] = ratio
-        energy_table[index] = jnp.sum(block * ratio)
+        times = jnp.where(column == line, 1.0, 2.0) if left == right else 1.0
+        energy_table[index] = jnp.sum(times * block * ratio)
         weight = weight_table[left * list_width + right]
         if left != right:
             weight = weight + weight_table[right * list_width + left]
-        squares = (weight.astype(F32) / width) * (ratio * ratio)
+        squares = times * (weight.astype(F32) / width) * (ratio * ratio)
         row_squares[left] = row_squares[left] + squares
         acc_ref[right : right + 1, :] += jnp.sum(squares, axis=0, keepdims=True)
     for s in range(list_width):
@@ -222,7 +251,7 @@
 
 def pair_terms(blocks, levels, packed, occupied, place):
     height, width = blocks.shape
-    depth = height // len(BLOCKS)
+    depth = (height - 8) // SENT
     list_width = levels.shape[0]
     whole = pl.BlockSpec(memory_space=pltpu.VMEM)
     scalar = pl.BlockSpec(memory_space=pltpu.SMEM)
@@ -315,6 +344,8 @@
     share, width, _ = out_ref.shape
     sources, height, _ = parts_ref.shape
     depth = (height - TAIL) // share
+    line = lax.broadcasted_iota(jnp.int32, (width, width), 0)
+    column = lax.broadcasted_iota(jnp.int32, (width, width), 1)
     for k in range(share):
         block = jnp.concatenate(
             [
@@ -325,7 +356,11 @@
         )
         pair = place[2] * share + k
         swapped = slots[pair, 0] > slots[pair, 1]
-        out_ref[k] = jnp.where(swapped, block.T, block).astype(jnp.bfloat16)
+        same = slots[pair, 0] == slots[pair, 1]
+        other = block.T
+        both = jnp.where(line == column, block, block + other)
+        value = jnp.where(same, both, jnp.where(swapped, other, block))
+        out_ref[k] = value.astype(jnp.bfloat16)
 
 
 def join_amplitudes(parts, pair_slots, place, share):
@@ -422,8 +457,8 @@
     depth = scaled.shape[2]
     sent = scaled.astype(jnp.float16).reshape(-1, depth, width)
     arrived = lax.all_to_all(sent, ("zh", "yh"), split_axis=0, concat_axis=0, tiled=True)
-    power = arrived[:, depth - TAIL : depth - TAIL + 1, :].astype(F32) - TOP_POWER
-    blocks = jnp.sum(arrived[:, : depth - TAIL, :].astype(F32) * jnp.exp2(power), axis=0)
+    power = arrived[:, depth - 1 :, :].astype(F32) - TOP_POWER
+    blocks = jnp.sum(arrived[:, : depth - 8, :].astype(F32) * jnp.exp2(power), axis=0)
 
     place = jnp.stack([position["zh"], position["zl"], x]).astype(jnp.int32)
     slices = pair_terms(blocks, levels, packed, occupied, place)

time: 220 us -> 213 us (0.968)
  waiting for transfers between devices: 36.2 us -> 30.6 us
  starting transfers between devices: 25.4 us -> 20.7 us
  blocking collectives: 132 us -> 136 us
    all_to_all x1, blocking collectives: 15 us -> 21.9 us  [on_device(): lax.all_to_all(planes, ('zh', 'zl'), split_axis=0, concat_axis=0, tiled=T...]
    all_to_all x1, waiting for transfers between devices: 30.4 us -> 24.9 us  [on_device(): lax.all_to_all(sent, ('zh', 'yh'), split_axis=0, concat_axis=0, tiled=True)]
    all_to_all x1, starting transfers between devices: 13.8 us -> 9.12 us  [on_device(): lax.all_to_all(lines, ('yh', 'yl', 'c'), split_axis=0, concat_axis=0, til...]
    all_to_all x1, blocking collectives: 10.7 us -> 7.5 us  [on_device(): lax.all_to_all(slices, 'x', split_axis=0, concat_axis=0, tiled=True)]
where the time goes in v5:
time: 213 us
  blocking collectives  136 us (64%)
  waiting for transfers between devices  30.6 us (14%)
  starting transfers between devices  20.7 us (10%)
  Pallas kernels  17.7 us (8%)
  local copies, waits for them, and re-layouts  6.07 us (3%)
    all_to_all x1, blocking collectives, on_device(): lax.all_to_all(outgoing.reshape(members, per_member * width, rows), inner...  106 us
    all_to_all x1, waiting for transfers between devices, on_device(): lax.all_to_all(sent, ('zh', 'yh'), split_axis=0, concat_axis=0, tiled=True)  24.9 us
    all_to_all x1, blocking collectives, on_device(): lax.all_to_all(planes, ('zh', 'zl'), split_axis=0, concat_axis=0, tiled=T...  21.9 us
    all_to_all x1, starting transfers between devices, on_device(): lax.all_to_all(sent, ('zh', 'yh'), split_axis=0, concat_axis=0, tiled=True)  10.9 us
    all_to_all x1, starting transfers between devices, on_device(): lax.all_to_all(lines, ('yh', 'yl', 'c'), split_axis=0, concat_axis=0, til...  9.12 us
    all_to_all x1, blocking collectives, on_device(): lax.all_to_all(slices, 'x', split_axis=0, concat_axis=0, tiled=True)  7.5 us
    pallas_call x1, Pallas kernels, make_slabs(): pl.pallas_call(slab_kernel, out_shape=jax.ShapeDtypeStruct((owners, width...  6.83 us
    pallas_call x1, Pallas kernels, partial_grams(): pl.pallas_call(gram_kernel, out_shape=jax.ShapeDtypeStruct((pieces, owner...  6.33 us
  transfers between devices with their start and end apart: 3, of which 2 were waited for; matrix products, arithmetic and copies ran while one was open for 3% of the time, Pallas kernels for 1%

profile of v5, /device:TPU:1, one launch (start us, length us, event | category | flops | bytes accessed | tf_op | source)
XLA Modules:
  0.0 213.0 jit_solution(15566368953088705437)
XLA Ops:
  0.7 6.8 %slabs.1 = bf16[128,128,256]{2,1,0:T(8,128)(2,1)} custom-call(s32[4,128]{1,0:T(4,128)} %bitcast.27, s32[1]{0:T(128)} %bitcast.2.group, bf16[32,256,128]{2,1,0:T(8,128)(2,1)} %integral_ref.1, bf16[32,128,128]{2,1,0:T(8,128)(2,1)} %map_ref.1, s32[128,128]{1,0:T(8,128)} %index_ref.1), custom_call_target="tpu_custom_call" | custom-call | tf_op jit(solution)/shard_map/slabs/pallas_call | solution.py:56
  7.5 106.1 %all_to_all.31 = bf16[32,512,256]{2,1,0:T(8,128)(2,1)} all-to-all(bf16[32,512,256]{2,1,0:T(8,128)(2,1)} %bitcast.25), channel_id=1, replica_groups=mesh['zh'=4,'zl'=2,'yh'=4,'yl'=2,'c'=2,'x'=4] {'zl','yl','c','x'}, dimensions={0} | all-to-all | bytes 16777216 | tf_op jit(solution)/shard_map/all_to_all | solution.py:447
  113.6 6.3 %partial_grams.1 = f32[4,4,272,128]{3,2,1,0:T(8,128)S(1)} custom-call(bf16[8,4,4,128,256]{4,3,2,1,0:T(8,128)(2,1)} %bitcast.24), custom_call_target="tpu_custom_call" | custom-call | tf_op jit(solution)/shard_map/partial_grams/pallas_call | solution.py:143
  120.0 1.1 convert_element_type.9
  121.1 10.9 %all-to-all-start.1 = ((f16[16,272,128]{2,1,0:T(8,128)(2,1)}), f16[16,272,128]{2,1,0:T(8,128)(2,1)S(1)}, u32[]{:S(2)}, u32[]{:S(2)}) async-start(f16[16,272,128]{2,1,0:T(8,128)(2,1)} %bitcast.8), calls=%async_computation.1 | async-start | bytes 2228224 | tf_op jit(solution)/shard_map/all_to_all | solution.py:459
  132.1 0.1 copy.26
  132.2 0.7 collective-permute-start
  132.9 0.2 dynamic-slice_reduce_fusion
  133.1 1.4 gather_fusion.1
  134.5 0.6 gather_fusion
  135.2 3.1 %gather_fusion.2 = f32[512]{0:T(512)S(1)} fusion(f32[25000]{0:T(1024)S(1)} %copy-done, s32[1024]{0:T(1024)S(1)} %pad_clamp_fusion), kind=kCustom, calls=%fused_computation.2 | custom fusion | bytes 6144 | tf_op jit(solution)/shard_map/gather | solution.py:439
  138.4 24.9 %all-to-all-done.1 = f16[16,272,128]{2,1,0:T(8,128)(2,1)S(1)} async-done(((f16[16,272,128]{2,1,0:T(8,128)(2,1)}), f16[16,272,128]{2,1,0:T(8,128)(2,1)S(1)}, u32[]{:S(2)}, u32[]{:S(2)}) %all-to-all-start.1) | async-done | bytes 1114144 | tf_op jit(solution)/shard_map/all_to_all | solution.py:459
  163.3 0.2 multiply_reduce_fusion.block_ref
  163.5 1.1 pair_terms.1
  164.6 7.5 %all_to_all.32.parts_ref = bf16[4,144,128]{2,1,0:T(8,128)(2,1)S(1)} all-to-all(bf16[4,144,128]{2,1,0:T(8,128)(2,1)S(1)} %pair_terms.1), channel_id=1, replica_groups=mesh['zh'=4,'zl'=2,'yh'=4,'yl'=2,'c'=2,'x'=4] {'x'}, dimensions={0} | all-to-all | bytes 294912 | tf_op jit(solution)/shard_map/all_to_all | solution.py:465
  172.2 21.9 %all_to_all.33.parts_ref = bf16[8,144,128]{2,1,0:T(8,128)(2,1)S(1)} all-to-all(bf16[8,144,128]{2,1,0:T(8,128)(2,1)S(1)} %plane_terms.1), channel_id=1, replica_groups=mesh['zh'=4,'zl'=2,'yh'=4,'yl'=2,'c'=2,'x'=4] {'zh','zl'}, dimensions={0} | all-to-all | bytes 589824 | tf_op jit(solution)/shard_map/all_to_all | solution.py:467
  194.1 1.2 owner_terms.1
  195.3 9.1 %all-to-all-start.4 = ((f32[16,8,128]{2,1,0:T(8,128)}), f32[16,8,128]{2,1,0:T(8,128)S(1)}, u32[]{:S(2)}, u32[]{:S(2)}) async-start(f32[16,8,128]{2,1,0:T(8,128)} %bitcast.14), calls=%async_computation.4 | async-start | bytes 131072 | tf_op jit(solution)/shard_map/all_to_all | solution.py:469
  204.5 0.2 sub.17
  204.7 0.2 copy.29
  204.9 0.1 reshape.74.owner_ref
  205.0 1.5 join_amplitudes.1
  206.4 5.8 %all-to-all-done.4 = f32[16,8,128]{2,1,0:T(8,128)S(1)} async-done(((f32[16,8,128]{2,1,0:T(8,128)}), f32[16,8,128]{2,1,0:T(8,128)S(1)}, u32[]{:S(2)}, u32[]{:S(2)}) %all-to-all-start.4) | async-done | bytes 65568 | tf_op jit(solution)/shard_map/all_to_all | solution.py:469
  212.2 0.8 sum_grads.1
  (23 shorter events, 0.3 us)
Async XLA Ops:
  0.6 134.5 %copy-start = (f32[25000]{0:T(1024)S(1)}, f32[25000]{0:T(1024)}, u32[]{:S(2)}) copy-start(f32[25000]{0:T(1024)} %param.14) | copy-start | bytes 300004
  120.0 12.1 %copy-start.3 = (s32[16,2]{0,1:T(2,128)S(1)}, s32[16,2]{0,1:T(2,128)}, u32[]{:S(2)}) copy-start(s32[16,2]{0,1:T(2,128)} %param.12) | copy-start | bytes 388
  120.0 12.1 %copy-start.4 = (s32[16]{0:T(128)S(1)}, s32[16]{0:T(128)}, u32[]{:S(2)}) copy-start(s32[16]{0:T(128)} %param.13) | copy-start | bytes 196
  120.0 12.9 %copy-start.2 = (s32[128,4]{0,1:T(4,128)S(1)}, s32[128,4]{0,1:T(4,128)}, u32[]{:S(2)}) copy-start(s32[128,4]{0,1:T(4,128)} %param.11) | copy-start | bytes 6148
  120.0 14.5 %copy-start.1 = (f32[128]{0:T(128)S(1)}, f32[128]{0:T(128)}, u32[]{:S(2)}) copy-start(f32[128]{0:T(128)} %param.15) | copy-start | bytes 1540
  121.1 42.1 %all-to-all-start.1 = ((f16[16,272,128]{2,1,0:T(8,128)(2,1)}), f16[16,272,128]{2,1,0:T(8,128)(2,1)S(1)}, u32[]{:S(2)}, u32[]{:S(2)}) async-start(f16[16,272,128]{2,1,0:T(8,128)(2,1)} %bitcast.8), calls=%async_computation.1 | async-start | bytes 2228224 | tf_op jit(solution)/shard_map/all_to_all | solution.py:459
  132.2 31.3 %collective-permute-start = (s32[16,3]{1,0:T(8,128)S(1)}, s32[16,3]{1,0:T(8,128)S(1)}, u32[]{:S(2)}, u32[]{:S(2)}) collective-permute-start(s32[16,3]{1,0:T(8,128)S(1)} %copy.26), channel_id=1, source_target_pairs={{0,0},{1,128},{2,256},{3,384},{128,1},{129,129},{130,257},{131,385... | collective-permute-start | bytes 584 | tf_op jit(solution)/shard_map/ppermute | solution.py:428
  195.3 16.9 %all-to-all-start.4 = ((f32[16,8,128]{2,1,0:T(8,128)}), f32[16,8,128]{2,1,0:T(8,128)S(1)}, u32[]{:S(2)}, u32[]{:S(2)}) async-start(f32[16,8,128]{2,1,0:T(8,128)} %bitcast.14), calls=%async_computation.4 | async-start | bytes 131072 | tf_op jit(solution)/shard_map/all_to_all | solution.py:469

commit v6 on v5

--- a/solution.py
+++ b/solution.py
@@ -44,7 +44,7 @@
         part = step - first_write
         base = jnp.right_shift(part, 1) * 16 + jnp.bitwise_and(part, 1) * 2
         for k in range(per_step):
-            owner = base + (k // 4 % 4) * 32 + (k % 4) * 4 + k // 16
+            owner = base + (k % 4) * 32 + (k // 4 % 4) * 4 + k // 16
             out_ref[k] = slab_ref[owner_list[group[0], owner] - first_orb]
 
 
@@ -89,7 +89,7 @@
         dimension_numbers=(((1,), (1,)), ((), ())),
         preferred_element_type=F32,
     )
-    pieces = out_ref.shape[0]
+    pieces = out_ref.shape[1]
     depth = width // pieces
     base = SENT * depth
     line = lax.broadcasted_iota(jnp.int32, (width, width), 0)
@@ -128,12 +128,12 @@
         for index, block in enumerate(blocks):
             block = block * scale
             for q in range(pieces):
-                out_ref[q, j, index * depth : (index + 1) * depth, :] = block[
+                out_ref[j, q, index * depth : (index + 1) * depth, :] = block[
                     q * depth : (q + 1) * depth
                 ]
         for q in range(pieces):
-            out_ref[q, j, base : base + 8, :] = tail
-            out_ref[q, j, base + 8 : base + TAIL, :] = power
+            out_ref[j, q, base : base + 8, :] = tail
+            out_ref[j, q, base + 8 : base + TAIL, :] = power
 
 
 def partial_grams(slabs):
@@ -142,14 +142,14 @@
     depth = SENT * (width // pieces) + TAIL
     return pl.pallas_call(
         gram_kernel,
-        out_shape=jax.ShapeDtypeStruct((pieces, owners, depth, width), F32),
+        out_shape=jax.ShapeDtypeStruct((owners, pieces, depth, width), F32),
         grid=(owners // GRAMS_PER_STEP,),
         in_specs=[
             pl.BlockSpec(
                 (count, list_width, GRAMS_PER_STEP, width, rows), lambda j: (0, 0, j, 0, 0)
             )
         ],
-        out_specs=pl.BlockSpec((pieces, GRAMS_PER_STEP, depth, width), lambda j: (0, j, 0, 0)),
+        out_specs=pl.BlockSpec((GRAMS_PER_STEP, pieces, depth, width), lambda j: (j, 0, 0, 0)),
         compiler_params=pltpu.CompilerParams(vmem_limit_bytes=VMEM_LIMIT),
         name="partial_grams",
     )(slabs)
@@ -300,9 +300,8 @@
     )(parts)
 
 
-def owner_kernel(place, parts_ref, terms_ref, energy_ref):
+def owner_kernel(parts_ref, terms_ref):
     planes, height, width = parts_ref.shape
-    share = energy_ref.shape[0]
     body = height - TAIL
     sums = []
     for low in range(2):
@@ -315,37 +314,30 @@
     tile = jnp.concatenate(sums, axis=0)
     for k in range(terms_ref.shape[0] // 8):
         terms_ref[8 * k : 8 * k + 8, :] = tile
-    energies = jnp.zeros((1, width), F32)
-    for q in range(planes // 2):
-        tail = parts_ref[q * 2 + place[1], body:, :].astype(F32)
-        energies = energies + (tail[12:13] + (tail[13:14] + tail[14:15]))
-    lane = lax.broadcasted_iota(jnp.int32, (1, width), 1)
-    for k in range(share):
-        energy_ref[k] = jnp.sum(jnp.where(lane == place[2] * share + k, energies, 0.0))
-
-
-def owner_terms(parts, place, lines, share):
+
+
+def owner_terms(parts, lines):
     whole = pl.BlockSpec(memory_space=pltpu.VMEM)
-    scalar = pl.BlockSpec(memory_space=pltpu.SMEM)
     return pl.pallas_call(
         owner_kernel,
-        out_shape=(
-            jax.ShapeDtypeStruct((lines, parts.shape[2]), F32),
-            jax.ShapeDtypeStruct((share,), F32),
-        ),
-        in_specs=[scalar, whole],
-        out_specs=(whole, scalar),
+        out_shape=jax.ShapeDtypeStruct((lines, parts.shape[2]), F32),
+        in_specs=[whole],
+        out_specs=whole,
         compiler_params=pltpu.CompilerParams(vmem_limit_bytes=VMEM_LIMIT),
         name="owner_terms",
-    )(place, parts)
-
-
-def join_kernel(slots, place, parts_ref, out_ref):
+    )(parts)
+
+
+def join_kernel(slots, place, parts_ref, out_ref, energy_ref):
     share, width, _ = out_ref.shape
     sources, height, _ = parts_ref.shape
     depth = (height - TAIL) // share
     line = lax.broadcasted_iota(jnp.int32, (width, width), 0)
     column = lax.broadcasted_iota(jnp.int32, (width, width), 1)
+    energies = jnp.zeros((1, width), F32)
+    for q in range(sources // 2):
+        tail = parts_ref[q * 2 + place[1], height - TAIL :, :].astype(F32)
+        energies = energies + (tail[12:13] + (tail[13:14] + tail[14:15]))
     for k in range(share):
         block = jnp.concatenate(
             [
@@ -361,6 +353,7 @@
         both = jnp.where(line == column, block, block + other)
         value = jnp.where(same, both, jnp.where(swapped, other, block))
         out_ref[k] = value.astype(jnp.bfloat16)
+        energy_ref[k] = jnp.sum(jnp.where(column[0:1] == pair, energies, 0.0))
 
 
 def join_amplitudes(parts, pair_slots, place, share):
@@ -369,9 +362,12 @@
     width = parts.shape[2]
     return pl.pallas_call(
         join_kernel,
-        out_shape=jax.ShapeDtypeStruct((share, width, width), jnp.bfloat16),
+        out_shape=(
+            jax.ShapeDtypeStruct((share, width, width), jnp.bfloat16),
+            jax.ShapeDtypeStruct((share,), F32),
+        ),
         in_specs=[scalar, scalar, whole],
-        out_specs=whole,
+        out_specs=(whole, scalar),
         compiler_params=pltpu.CompilerParams(vmem_limit_bytes=VMEM_LIMIT),
         name="join_amplitudes",
     )(pair_slots, place, parts)
@@ -414,10 +410,10 @@
     size = {name: lax.axis_size(name) for name in AXES}
     x = position["x"]
 
-    def aux_rank(zh):
-        rank = zh
-        for name in AXES[1:-1]:
-            rank = rank * size[name] + position[name]
+    def aux_rank(yh):
+        rank = 0
+        for name in AXES[:-1]:
+            rank = rank * size[name] + (yh if name == "yh" else position[name])
         return rank
 
     occ_local, rows, width = half_integrals.shape
@@ -426,11 +422,11 @@
     cross = [(q * 4 + s, s * 4 + q) for q in range(4) for s in range(4)]
 
     packed = lax.ppermute(
-        jnp.concatenate([pair_slots, pair_weight[:, None]], axis=1), ("zh", "x"), cross
+        jnp.concatenate([pair_slots, pair_weight[:, None]], axis=1), ("yh", "x"), cross
     )
     own = lax.dynamic_slice_in_dim(owner_orbitals, x, 1, 1)[:, 0] - x * occ_local
     grid = own.reshape([size[name] for name in AXES[:-1]])
-    line_owner = grid.transpose(2, 3, 4, 1, 0).reshape(1, -1)
+    line_owner = grid.transpose(0, 1, 4, 3, 2).reshape(1, -1)
 
     my_orbitals = lax.dynamic_slice_in_dim(owner_orbitals, aux_rank(x), 1, 0)[0]
     my_index = domain_index[my_orbitals]
@@ -460,14 +456,14 @@
     power = arrived[:, depth - 1 :, :].astype(F32) - TOP_POWER
     blocks = jnp.sum(arrived[:, : depth - 8, :].astype(F32) * jnp.exp2(power), axis=0)
 
-    place = jnp.stack([position["zh"], position["zl"], x]).astype(jnp.int32)
+    place = jnp.stack([position["yh"], position["yl"], x]).astype(jnp.int32)
     slices = pair_terms(blocks, levels, packed, occupied, place)
     slices = lax.all_to_all(slices, "x", split_axis=0, concat_axis=0, tiled=True)
-    planes = plane_terms(slices, size["zh"] * size["zl"])
-    parts = lax.all_to_all(planes, ("zh", "zl"), split_axis=0, concat_axis=0, tiled=True)
-    lines, pair_energy = owner_terms(parts, place, owners, share)
-    all_lines = lax.all_to_all(lines, ("yh", "yl", "c"), split_axis=0, concat_axis=0, tiled=True)
-    amplitude = join_amplitudes(parts, pair_slots, place, share)
+    planes = plane_terms(slices, size["yh"] * size["yl"])
+    parts = lax.all_to_all(planes, ("yh", "yl"), split_axis=0, concat_axis=0, tiled=True)
+    lines = owner_terms(parts, owners)
+    all_lines = lax.all_to_all(lines, ("zh", "zl", "c"), split_axis=0, concat_axis=0, tiled=True)
+    amplitude, pair_energy = join_amplitudes(parts, pair_slots, place, share)
     domain_grad = sum_grads(all_lines, line_owner, occ_local)
     return (amplitude, pair_energy, domain_grad)
 

time: 213 us -> 213 us (level)
  no operation moved by 1% of the time
where the time goes in v6:
time: 213 us; the launch traced here: 212 us
  blocking collectives  135 us (63%)
  waiting for transfers between devices  30.4 us (14%)
  starting transfers between devices  21 us (10%)
  Pallas kernels  17.1 us (8%)
  local copies, waits for them, and re-layouts  6.07 us (3%)
    all_to_all x1, blocking collectives, on_device(): lax.all_to_all(outgoing.reshape(members, per_member * width, rows), inner...  106 us
    all_to_all x1, waiting for transfers between devices, on_device(): lax.all_to_all(sent, ('zh', 'yh'), split_axis=0, concat_axis=0, tiled=True)  24.7 us
    all_to_all x1, blocking collectives, on_device(): lax.all_to_all(planes, ('yh', 'yl'), split_axis=0, concat_axis=0, tiled=T...  21.6 us
    all_to_all x1, starting transfers between devices, on_device(): lax.all_to_all(sent, ('zh', 'yh'), split_axis=0, concat_axis=0, tiled=True)  10.9 us
    all_to_all x1, starting transfers between devices, on_device(): lax.all_to_all(lines, ('zh', 'zl', 'c'), split_axis=0, concat_axis=0, til...  9.39 us
    all_to_all x1, blocking collectives, on_device(): lax.all_to_all(slices, 'x', split_axis=0, concat_axis=0, tiled=True)  7.54 us
    pallas_call x1, Pallas kernels, make_slabs(): pl.pallas_call(slab_kernel, out_shape=jax.ShapeDtypeStruct((owners, width...  6.83 us
    pallas_call x1, Pallas kernels, partial_grams(): pl.pallas_call(gram_kernel, out_shape=jax.ShapeDtypeStruct((owners, piece...  6.19 us
  transfers between devices with their start and end apart: 3, of which 2 were waited for; matrix products, arithmetic and copies ran while one was open for 3% of the time, Pallas kernels for 1%

profile of v6, /device:TPU:1, one launch (start us, length us, event | category | flops | bytes accessed | tf_op | source)
XLA Modules:
  0.0 212.1 jit_solution(11467932297427912558)
XLA Ops:
  0.7 6.8 %slabs.1 = bf16[128,128,256]{2,1,0:T(8,128)(2,1)} custom-call(s32[4,128]{1,0:T(4,128)} %bitcast.27, s32[1]{0:T(128)} %bitcast.2.group, bf16[32,256,128]{2,1,0:T(8,128)(2,1)} %integral_ref.1, bf16[32,128,128]{2,1,0:T(8,128)(2,1)} %map_ref.1, s32[128,128]{1,0:T(8,128)} %index_ref.1), custom_call_target="tpu_custom_call" | custom-call | tf_op jit(solution)/shard_map/slabs/pallas_call | solution.py:56
  7.5 106.1 %all_to_all.31 = bf16[32,512,256]{2,1,0:T(8,128)(2,1)} all-to-all(bf16[32,512,256]{2,1,0:T(8,128)(2,1)} %bitcast.25), channel_id=1, replica_groups=mesh['zh'=4,'zl'=2,'yh'=4,'yl'=2,'c'=2,'x'=4] {'zl','yl','c','x'}, dimensions={0} | all-to-all | bytes 16777216 | tf_op jit(solution)/shard_map/all_to_all | solution.py:443
  113.6 6.2 %partial_grams.1 = f32[4,4,272,128]{3,2,1,0:T(8,128)S(1)} custom-call(bf16[8,4,4,128,256]{4,3,2,1,0:T(8,128)(2,1)} %bitcast.24), custom_call_target="tpu_custom_call" | custom-call | tf_op jit(solution)/shard_map/partial_grams/pallas_call | solution.py:143
  119.9 1.1 convert_element_type.9
  121.0 10.9 %all-to-all-start.1 = ((f16[16,272,128]{2,1,0:T(8,128)(2,1)}), f16[16,272,128]{2,1,0:T(8,128)(2,1)S(1)}, u32[]{:S(2)}, u32[]{:S(2)}) async-start(f16[16,272,128]{2,1,0:T(8,128)(2,1)} %bitcast.8), calls=%async_computation.1 | async-start | bytes 2228224 | tf_op jit(solution)/shard_map/all_to_all | solution.py:455
  132.0 0.1 copy.26
  132.1 0.7 collective-permute-start
  132.8 0.2 dynamic-slice_reduce_fusion
  133.0 1.4 gather_fusion.1
  134.4 0.6 gather_fusion
  135.0 3.1 %gather_fusion.2 = f32[512]{0:T(512)S(1)} fusion(f32[25000]{0:T(1024)S(1)} %copy-done, s32[1024]{0:T(1024)S(1)} %pad_clamp_fusion), kind=kCustom, calls=%fused_computation.2 | custom fusion | bytes 6144 | tf_op jit(solution)/shard_map/gather | solution.py:435
  138.3 24.7 %all-to-all-done.1 = f16[16,272,128]{2,1,0:T(8,128)(2,1)S(1)} async-done(((f16[16,272,128]{2,1,0:T(8,128)(2,1)}), f16[16,272,128]{2,1,0:T(8,128)(2,1)S(1)}, u32[]{:S(2)}, u32[]{:S(2)}) %all-to-all-start.1) | async-done | bytes 1114144 | tf_op jit(solution)/shard_map/all_to_all | solution.py:455
  163.0 0.2 multiply_reduce_fusion.block_ref
  163.2 1.1 pair_terms.1
  164.3 7.5 %all_to_all.32.parts_ref = bf16[4,144,128]{2,1,0:T(8,128)(2,1)S(1)} all-to-all(bf16[4,144,128]{2,1,0:T(8,128)(2,1)S(1)} %pair_terms.1), channel_id=1, replica_groups=mesh['zh'=4,'zl'=2,'yh'=4,'yl'=2,'c'=2,'x'=4] {'x'}, dimensions={0} | all-to-all | bytes 294912 | tf_op jit(solution)/shard_map/all_to_all | solution.py:461
  171.9 21.6 %all_to_all.33.parts_ref = bf16[8,144,128]{2,1,0:T(8,128)(2,1)S(1)} all-to-all(bf16[8,144,128]{2,1,0:T(8,128)(2,1)S(1)} %plane_terms.1), channel_id=1, replica_groups=mesh['zh'=4,'zl'=2,'yh'=4,'yl'=2,'c'=2,'x'=4] {'yh','yl'}, dimensions={0} | all-to-all | bytes 589824 | tf_op jit(solution)/shard_map/all_to_all | solution.py:463
  193.5 0.6 owner_terms.1
  194.1 9.4 %all-to-all-start.4 = ((f32[16,8,128]{2,1,0:T(8,128)}), f32[16,8,128]{2,1,0:T(8,128)S(1)}, u32[]{:S(2)}, u32[]{:S(2)}) async-start(f32[16,8,128]{2,1,0:T(8,128)} %bitcast.14), calls=%async_computation.4 | async-start | bytes 131072 | tf_op jit(solution)/shard_map/all_to_all | solution.py:465
  203.6 0.2 sub.17
  203.8 0.2 copy.29
  204.0 0.1 reshape.74.owner_ref
  204.1 1.5 join_amplitudes.1
  205.6 5.7 %all-to-all-done.4 = f32[16,8,128]{2,1,0:T(8,128)S(1)} async-done(((f32[16,8,128]{2,1,0:T(8,128)}), f32[16,8,128]{2,1,0:T(8,128)S(1)}, u32[]{:S(2)}, u32[]{:S(2)}) %all-to-all-start.4) | async-done | bytes 65568 | tf_op jit(solution)/shard_map/all_to_all | solution.py:465
  211.3 0.8 sum_grads.1
  (23 shorter events, 0.3 us)
Async XLA Ops:
  0.6 134.4 %copy-start = (f32[25000]{0:T(1024)S(1)}, f32[25000]{0:T(1024)}, u32[]{:S(2)}) copy-start(f32[25000]{0:T(1024)} %param.14) | copy-start | bytes 300004
  119.8 12.1 %copy-start.3 = (s32[16,2]{0,1:T(2,128)S(1)}, s32[16,2]{0,1:T(2,128)}, u32[]{:S(2)}) copy-start(s32[16,2]{0,1:T(2,128)} %param.12) | copy-start | bytes 388
  119.8 12.1 %copy-start.4 = (s32[16]{0:T(128)S(1)}, s32[16]{0:T(128)}, u32[]{:S(2)}) copy-start(s32[16]{0:T(128)} %param.13) | copy-start | bytes 196
  119.8 12.9 %copy-start.2 = (s32[128,4]{0,1:T(4,128)S(1)}, s32[128,4]{0,1:T(4,128)}, u32[]{:S(2)}) copy-start(s32[128,4]{0,1:T(4,128)} %param.11) | copy-start | bytes 6148
  119.9 14.5 %copy-start.1 = (f32[128]{0:T(128)S(1)}, f32[128]{0:T(128)}, u32[]{:S(2)}) copy-start(f32[128]{0:T(128)} %param.15) | copy-start | bytes 1540
  121.0 41.9 %all-to-all-start.1 = ((f16[16,272,128]{2,1,0:T(8,128)(2,1)}), f16[16,272,128]{2,1,0:T(8,128)(2,1)S(1)}, u32[]{:S(2)}, u32[]{:S(2)}) async-start(f16[16,272,128]{2,1,0:T(8,128)(2,1)} %bitcast.8), calls=%async_computation.1 | async-start | bytes 2228224 | tf_op jit(solution)/shard_map/all_to_all | solution.py:455
  132.1 31.1 %collective-permute-start = (s32[16,3]{1,0:T(8,128)S(1)}, s32[16,3]{1,0:T(8,128)S(1)}, u32[]{:S(2)}, u32[]{:S(2)}) collective-permute-start(s32[16,3]{1,0:T(8,128)S(1)} %copy.26), channel_id=1, source_target_pairs={{0,0},{1,16},{2,32},{3,48},{16,1},{17,17},{18,33},{19,49},{32,2},{... | collective-permute-start | bytes 584 | tf_op jit(solution)/shard_map/ppermute | solution.py:424
  194.1 17.2 %all-to-all-start.4 = ((f32[16,8,128]{2,1,0:T(8,128)}), f32[16,8,128]{2,1,0:T(8,128)S(1)}, u32[]{:S(2)}, u32[]{:S(2)}) async-start(f32[16,8,128]{2,1,0:T(8,128)} %bitcast.14), calls=%async_computation.4 | async-start | bytes 131072 | tf_op jit(solution)/shard_map/all_to_all | solution.py:465

commit v7 on v6

--- a/solution.py
+++ b/solution.py
@@ -279,20 +279,18 @@
     body = height - TAIL
     tails = [parts_ref[s, body:, :].astype(F32) for s in range(owners)]
     vectors = [tails[s][k : k + 1] for k in range(3) for s in range(owners)]
-    per_zone = out_ref.shape[0] // owners
     for s in range(owners):
         lines = vectors + [tails[s][3:6], jnp.zeros((TAIL - 3 * owners - 3, width), F32)]
         tail = jnp.concatenate(lines, axis=0).astype(jnp.bfloat16)
-        for k in range(per_zone):
-            out_ref[s * per_zone + k, :body, :] = parts_ref[s, :body, :]
-            out_ref[s * per_zone + k, body:, :] = tail
-
-
-def plane_terms(parts, planes):
+        out_ref[s, :body, :] = parts_ref[s, :body, :]
+        out_ref[s, body:, :] = tail
+
+
+def plane_terms(parts):
     whole = pl.BlockSpec(memory_space=pltpu.VMEM)
     return pl.pallas_call(
         plane_kernel,
-        out_shape=jax.ShapeDtypeStruct((planes,) + parts.shape[1:], parts.dtype),
+        out_shape=jax.ShapeDtypeStruct(parts.shape, parts.dtype),
         in_specs=[whole],
         out_specs=whole,
         compiler_params=pltpu.CompilerParams(vmem_limit_bytes=VMEM_LIMIT),
@@ -301,17 +299,13 @@
 
 
 def owner_kernel(parts_ref, terms_ref):
-    planes, height, width = parts_ref.shape
-    body = height - TAIL
-    sums = []
-    for low in range(2):
-        total = None
-        for q in range(planes // 2):
-            tail = parts_ref[q * 2 + low, body:, :].astype(F32)
-            vectors = tail[0:4] + (tail[4:8] + tail[8:12])
-            total = vectors if total is None else total + vectors
-        sums.append(total)
-    tile = jnp.concatenate(sums, axis=0)
+    pieces, height, width = parts_ref.shape
+    total = None
+    for q in range(pieces):
+        tail = parts_ref[q, height - TAIL :, :].astype(F32)
+        vectors = tail[0:4] + (tail[4:8] + tail[8:12])
+        total = vectors if total is None else total + vectors
+    tile = jnp.concatenate([total, total], axis=0)
     for k in range(terms_ref.shape[0] // 8):
         terms_ref[8 * k : 8 * k + 8, :] = tile
 
@@ -335,18 +329,18 @@
     line = lax.broadcasted_iota(jnp.int32, (width, width), 0)
     column = lax.broadcasted_iota(jnp.int32, (width, width), 1)
     energies = jnp.zeros((1, width), F32)
-    for q in range(sources // 2):
-        tail = parts_ref[q * 2 + place[1], height - TAIL :, :].astype(F32)
+    for q in range(sources):
+        tail = parts_ref[q, height - TAIL :, :].astype(F32)
         energies = energies + (tail[12:13] + (tail[13:14] + tail[14:15]))
     for k in range(share):
         block = jnp.concatenate(
             [
-                parts_ref[q * 2 + place[1], k * depth : (k + 1) * depth, :].astype(F32)
-                for q in range(sources // 2)
+                parts_ref[q, k * depth : (k + 1) * depth, :].astype(F32)
+                for q in range(sources)
             ],
             axis=0,
         )
-        pair = place[2] * share + k
+        pair = place[1] * share + k
         swapped = slots[pair, 0] > slots[pair, 1]
         same = slots[pair, 0] == slots[pair, 1]
         other = block.T
@@ -426,7 +420,7 @@
     )
     own = lax.dynamic_slice_in_dim(owner_orbitals, x, 1, 1)[:, 0] - x * occ_local
     grid = own.reshape([size[name] for name in AXES[:-1]])
-    line_owner = grid.transpose(0, 1, 4, 3, 2).reshape(1, -1)
+    line_owner = grid.transpose(0, 1, 3, 4, 2).reshape(1, -1)
 
     my_orbitals = lax.dynamic_slice_in_dim(owner_orbitals, aux_rank(x), 1, 0)[0]
     my_index = domain_index[my_orbitals]
@@ -456,13 +450,15 @@
     power = arrived[:, depth - 1 :, :].astype(F32) - TOP_POWER
     blocks = jnp.sum(arrived[:, : depth - 8, :].astype(F32) * jnp.exp2(power), axis=0)
 
-    place = jnp.stack([position["yh"], position["yl"], x]).astype(jnp.int32)
+    place = jnp.stack([position["yh"], x]).astype(jnp.int32)
     slices = pair_terms(blocks, levels, packed, occupied, place)
     slices = lax.all_to_all(slices, "x", split_axis=0, concat_axis=0, tiled=True)
-    planes = plane_terms(slices, size["yh"] * size["yl"])
-    parts = lax.all_to_all(planes, ("yh", "yl"), split_axis=0, concat_axis=0, tiled=True)
+    planes = plane_terms(slices)
+    parts = lax.all_to_all(planes, "yh", split_axis=0, concat_axis=0, tiled=True)
     lines = owner_terms(parts, owners)
-    all_lines = lax.all_to_all(lines, ("zh", "zl", "c"), split_axis=0, concat_axis=0, tiled=True)
+    all_lines = lax.all_to_all(
+        lines, ("zh", "zl", "yl", "c"), split_axis=0, concat_axis=0, tiled=True
+    )
     amplitude, pair_energy = join_amplitudes(parts, pair_slots, place, share)
     domain_grad = sum_grads(all_lines, line_owner, occ_local)
     return (amplitude, pair_energy, domain_grad)

time: 213 us -> 210 us (0.986)
  blocking collectives: 135 us -> 129 us
  starting transfers between devices: 21 us -> 24.8 us
    all_to_all x1, blocking collectives: 21.6 us -> 15.2 us  [on_device(): lax.all_to_all(planes, 'yh', split_axis=0, concat_axis=0, tiled=True)]
    all_to_all x1, starting transfers between devices: 9.39 us -> 13.2 us  [on_device(): lax.all_to_all(lines, ('zh', 'zl', 'yl', 'c'), split_axis=0, concat_axis=...]
where the time goes in v7:
time: 210 us
  blocking collectives  129 us (61%)
  waiting for transfers between devices  30.7 us (15%)
  starting transfers between devices  24.8 us (12%)
  Pallas kernels  17 us (8%)
  local copies, waits for them, and re-layouts  6.07 us (3%)
    all_to_all x1, blocking collectives, on_device(): lax.all_to_all(outgoing.reshape(members, per_member * width, rows), inner...  106 us
    all_to_all x1, waiting for transfers between devices, on_device(): lax.all_to_all(sent, ('zh', 'yh'), split_axis=0, concat_axis=0, tiled=True)  24.7 us
    all_to_all x1, blocking collectives, on_device(): lax.all_to_all(planes, 'yh', split_axis=0, concat_axis=0, tiled=True)  15.2 us
    all_to_all x1, starting transfers between devices, on_device(): lax.all_to_all(lines, ('zh', 'zl', 'yl', 'c'), split_axis=0, concat_axis=...  13.2 us
    all_to_all x1, starting transfers between devices, on_device(): lax.all_to_all(sent, ('zh', 'yh'), split_axis=0, concat_axis=0, tiled=True)  10.9 us
    all_to_all x1, blocking collectives, on_device(): lax.all_to_all(slices, 'x', split_axis=0, concat_axis=0, tiled=True)  7.54 us
    pallas_call x1, Pallas kernels, make_slabs(): pl.pallas_call(slab_kernel, out_shape=jax.ShapeDtypeStruct((owners, width...  6.83 us
    pallas_call x1, Pallas kernels, partial_grams(): pl.pallas_call(gram_kernel, out_shape=jax.ShapeDtypeStruct((owners, piece...  6.19 us
  transfers between devices with their start and end apart: 3, of which 2 were waited for; matrix products, arithmetic and copies ran while one was open for 3% of the time, Pallas kernels for 1%

profile of v7, /device:TPU:1, one launch (start us, length us, event | category | flops | bytes accessed | tf_op | source)
XLA Modules:
  0.0 209.8 jit_solution(7219181413295640553)
XLA Ops:
  0.7 6.8 %slabs.1 = bf16[128,128,256]{2,1,0:T(8,128)(2,1)} custom-call(s32[4,128]{1,0:T(4,128)} %bitcast.26, s32[1]{0:T(128)} %bitcast.1.group, bf16[32,256,128]{2,1,0:T(8,128)(2,1)} %integral_ref.1, bf16[32,128,128]{2,1,0:T(8,128)(2,1)} %map_ref.1, s32[128,128]{1,0:T(8,128)} %index_ref.1), custom_call_target="tpu_custom_call" | custom-call | tf_op jit(solution)/shard_map/slabs/pallas_call | solution.py:56
  7.5 106.1 %all_to_all.31 = bf16[32,512,256]{2,1,0:T(8,128)(2,1)} all-to-all(bf16[32,512,256]{2,1,0:T(8,128)(2,1)} %bitcast.24), channel_id=1, replica_groups=mesh['zh'=4,'zl'=2,'yh'=4,'yl'=2,'c'=2,'x'=4] {'zl','yl','c','x'}, dimensions={0} | all-to-all | bytes 16777216 | tf_op jit(solution)/shard_map/all_to_all | solution.py:437
  113.6 6.2 %partial_grams.1 = f32[4,4,272,128]{3,2,1,0:T(8,128)S(1)} custom-call(bf16[8,4,4,128,256]{4,3,2,1,0:T(8,128)(2,1)} %bitcast.23), custom_call_target="tpu_custom_call" | custom-call | tf_op jit(solution)/shard_map/partial_grams/pallas_call | solution.py:143
  119.9 1.1 convert_element_type.9
  121.0 10.9 %all-to-all-start.1 = ((f16[16,272,128]{2,1,0:T(8,128)(2,1)}), f16[16,272,128]{2,1,0:T(8,128)(2,1)S(1)}, u32[]{:S(2)}, u32[]{:S(2)}) async-start(f16[16,272,128]{2,1,0:T(8,128)(2,1)} %bitcast.7), calls=%async_computation.1 | async-start | bytes 2228224 | tf_op jit(solution)/shard_map/all_to_all | solution.py:449
  132.0 0.1 copy.26
  132.1 0.7 collective-permute-start
  132.8 0.2 dynamic-slice_reduce_fusion
  133.0 1.4 gather_fusion.1
  134.4 0.6 gather_fusion
  135.0 3.1 %gather_fusion.2 = f32[512]{0:T(512)S(1)} fusion(f32[25000]{0:T(1024)S(1)} %copy-done, s32[1024]{0:T(1024)S(1)} %pad_clamp_fusion), kind=kCustom, calls=%fused_computation.2 | custom fusion | bytes 6144 | tf_op jit(solution)/shard_map/gather | solution.py:429
  138.3 24.7 %all-to-all-done.1 = f16[16,272,128]{2,1,0:T(8,128)(2,1)S(1)} async-done(((f16[16,272,128]{2,1,0:T(8,128)(2,1)}), f16[16,272,128]{2,1,0:T(8,128)(2,1)S(1)}, u32[]{:S(2)}, u32[]{:S(2)}) %all-to-all-start.1) | async-done | bytes 1114144 | tf_op jit(solution)/shard_map/all_to_all | solution.py:449
  163.0 0.2 multiply_reduce_fusion.block_ref
  163.2 1.1 pair_terms.1
  164.3 7.5 %all_to_all.32.parts_ref = bf16[4,144,128]{2,1,0:T(8,128)(2,1)S(1)} all-to-all(bf16[4,144,128]{2,1,0:T(8,128)(2,1)S(1)} %pair_terms.1), channel_id=1, replica_groups=mesh['zh'=4,'zl'=2,'yh'=4,'yl'=2,'c'=2,'x'=4] {'x'}, dimensions={0} | all-to-all | bytes 294912 | tf_op jit(solution)/shard_map/all_to_all | solution.py:455
  171.8 15.2 %all_to_all.33.parts_ref = bf16[4,144,128]{2,1,0:T(8,128)(2,1)S(1)} all-to-all(bf16[4,144,128]{2,1,0:T(8,128)(2,1)S(1)} %plane_terms.1), channel_id=1, replica_groups=mesh['zh'=4,'zl'=2,'yh'=4,'yl'=2,'c'=2,'x'=4] {'yh'}, dimensions={0} | all-to-all | bytes 294912 | tf_op jit(solution)/shard_map/all_to_all | solution.py:457
  187.0 0.6 owner_terms.1
  187.7 13.2 %all-to-all-start.4 = ((f32[32,4,128]{2,1,0:T(4,128)}), f32[32,4,128]{2,1,0:T(4,128)S(1)}, u32[]{:S(2)}, u32[]{:S(2)}) async-start(f32[32,4,128]{2,1,0:T(4,128)} %bitcast.13), calls=%async_computation.4 | async-start | bytes 131072 | tf_op jit(solution)/shard_map/all_to_all | solution.py:459
  200.9 0.2 sub.17
  201.1 0.2 copy.29
  201.3 0.1 reshape.74.owner_ref
  201.4 1.5 join_amplitudes.1
  202.9 6.1 %all-to-all-done.4 = f32[32,4,128]{2,1,0:T(4,128)S(1)} async-done(((f32[32,4,128]{2,1,0:T(4,128)}), f32[32,4,128]{2,1,0:T(4,128)S(1)}, u32[]{:S(2)}, u32[]{:S(2)}) %all-to-all-start.4) | async-done | bytes 65568 | tf_op jit(solution)/shard_map/all_to_all | solution.py:459
  209.0 0.8 sum_grads.1
  (23 shorter events, 0.3 us)
Async XLA Ops:
  0.6 134.4 %copy-start = (f32[25000]{0:T(1024)S(1)}, f32[25000]{0:T(1024)}, u32[]{:S(2)}) copy-start(f32[25000]{0:T(1024)} %param.14) | copy-start | bytes 300004
  119.8 12.1 %copy-start.3 = (s32[16,2]{0,1:T(2,128)S(1)}, s32[16,2]{0,1:T(2,128)}, u32[]{:S(2)}) copy-start(s32[16,2]{0,1:T(2,128)} %param.12) | copy-start | bytes 388
  119.8 12.1 %copy-start.4 = (s32[16]{0:T(128)S(1)}, s32[16]{0:T(128)}, u32[]{:S(2)}) copy-start(s32[16]{0:T(128)} %param.13) | copy-start | bytes 196
  119.8 12.9 %copy-start.2 = (s32[128,4]{0,1:T(4,128)S(1)}, s32[128,4]{0,1:T(4,128)}, u32[]{:S(2)}) copy-start(s32[128,4]{0,1:T(4,128)} %param.11) | copy-start | bytes 6148
  119.9 14.5 %copy-start.1 = (f32[128]{0:T(128)S(1)}, f32[128]{0:T(128)}, u32[]{:S(2)}) copy-start(f32[128]{0:T(128)} %param.15) | copy-start | bytes 1540
  121.0 41.9 %all-to-all-start.1 = ((f16[16,272,128]{2,1,0:T(8,128)(2,1)}), f16[16,272,128]{2,1,0:T(8,128)(2,1)S(1)}, u32[]{:S(2)}, u32[]{:S(2)}) async-start(f16[16,272,128]{2,1,0:T(8,128)(2,1)} %bitcast.7), calls=%async_computation.1 | async-start | bytes 2228224 | tf_op jit(solution)/shard_map/all_to_all | solution.py:449
  132.1 31.1 %collective-permute-start = (s32[16,3]{1,0:T(8,128)S(1)}, s32[16,3]{1,0:T(8,128)S(1)}, u32[]{:S(2)}, u32[]{:S(2)}) collective-permute-start(s32[16,3]{1,0:T(8,128)S(1)} %copy.26), channel_id=1, source_target_pairs={{0,0},{1,16},{2,32},{3,48},{16,1},{17,17},{18,33},{19,49},{32,2},{... | collective-permute-start | bytes 584 | tf_op jit(solution)/shard_map/ppermute | solution.py:418
  187.7 21.3 %all-to-all-start.4 = ((f32[32,4,128]{2,1,0:T(4,128)}), f32[32,4,128]{2,1,0:T(4,128)S(1)}, u32[]{:S(2)}, u32[]{:S(2)}) async-start(f32[32,4,128]{2,1,0:T(4,128)} %bitcast.13), calls=%async_computation.4 | async-start | bytes 131072 | tf_op jit(solution)/shard_map/all_to_all | solution.py:459

commit v8 on v7

--- a/solution.py
+++ b/solution.py
@@ -341,8 +341,8 @@
             axis=0,
         )
         pair = place[1] * share + k
-        swapped = slots[pair, 0] > slots[pair, 1]
-        same = slots[pair, 0] == slots[pair, 1]
+        swapped = slots[0, pair] > slots[1, pair]
+        same = slots[0, pair] == slots[1, pair]
         other = block.T
         both = jnp.where(line == column, block, block + other)
         value = jnp.where(same, both, jnp.where(swapped, other, block))
@@ -429,6 +429,7 @@
         my_index >= 0, virtual_energy[jnp.clip(my_index, 0, virt_count - 1)], jnp.float32(1.0)
     )
     occupied = occupied_energy[my_orbitals]
+    levels, line_owner = lax.optimization_barrier((levels, line_owner))
 
     outgoing = make_slabs(half_integrals, domain_map, domain_index, owner_orbitals, x)
     inner = ("zl", "yl", "c", "x")
@@ -456,10 +457,11 @@
     planes = plane_terms(slices)
     parts = lax.all_to_all(planes, "yh", split_axis=0, concat_axis=0, tiled=True)
     lines = owner_terms(parts, owners)
+    amplitude, pair_energy = join_amplitudes(parts, pair_slots.T, place, share)
+    lines, amplitude = lax.optimization_barrier((lines, amplitude))
     all_lines = lax.all_to_all(
         lines, ("zh", "zl", "yl", "c"), split_axis=0, concat_axis=0, tiled=True
     )
-    amplitude, pair_energy = join_amplitudes(parts, pair_slots, place, share)
     domain_grad = sum_grads(all_lines, line_owner, occ_local)
     return (amplitude, pair_energy, domain_grad)
 

time: 210 us -> 212 us (level)
  blocking collectives: 129 us -> 152 us
  starting transfers between devices: 24.8 us -> 11.7 us
  waiting for transfers between devices: 30.7 us -> 23.8 us
    all_to_all x0 -> x1, blocking collectives: none -> 22.8 us  [on_device(): lax.all_to_all(lines, ('zh', 'zl', 'yl', 'c'), split_axis=0, concat_axis=...]
    all_to_all x1 -> x0, starting transfers between devices: 13.2 us -> none  [on_device(): lax.all_to_all(lines, ('zh', 'zl', 'yl', 'c'), split_axis=0, concat_axis=...]
    all_to_all x1 -> x0, waiting for transfers between devices: 6.07 us -> none  [on_device(): lax.all_to_all(lines, ('zh', 'zl', 'yl', 'c'), split_axis=0, concat_axis=...]
  transfers between devices with their start and end apart: 3 -> 2, of which waited for: 2 -> 1; matrix products, arithmetic and copies ran while one was open for 3% -> 3% of each run, Pallas kernels for 1% -> 0%
where the time goes in v8:
time: 212 us
  blocking collectives  152 us (72%)
  waiting for transfers between devices  23.8 us (11%)
  Pallas kernels  16.3 us (8%)
  starting transfers between devices  11.7 us (6%)
  local copies, waits for them, and re-layouts  5.98 us (3%)
    all_to_all x1, blocking collectives, on_device(): lax.all_to_all(outgoing.reshape(members, per_member * width, rows), inner...  106 us
    all_to_all x1, waiting for transfers between devices, on_device(): lax.all_to_all(sent, ('zh', 'yh'), split_axis=0, concat_axis=0, tiled=True)  23.8 us
    all_to_all x1, blocking collectives, on_device(): lax.all_to_all(lines, ('zh', 'zl', 'yl', 'c'), split_axis=0, concat_axis=...  22.8 us
    all_to_all x1, blocking collectives, on_device(): lax.all_to_all(planes, 'yh', split_axis=0, concat_axis=0, tiled=True)  15.3 us
    all_to_all x1, starting transfers between devices, on_device(): lax.all_to_all(sent, ('zh', 'yh'), split_axis=0, concat_axis=0, tiled=True)  11.1 us
    all_to_all x1, blocking collectives, on_device(): lax.all_to_all(slices, 'x', split_axis=0, concat_axis=0, tiled=True)  7.69 us
    pallas_call x1, Pallas kernels, make_slabs(): pl.pallas_call(slab_kernel, out_shape=jax.ShapeDtypeStruct((owners, width...  6.83 us
    pallas_call x1, Pallas kernels, partial_grams(): pl.pallas_call(gram_kernel, out_shape=jax.ShapeDtypeStruct((owners, piece...  6.19 us
  transfers between devices with their start and end apart: 2, of which 1 were waited for; matrix products, arithmetic and copies ran while one was open for 3% of the time, Pallas kernels for 0%

profile of v8, /device:TPU:1, one launch (start us, length us, event | category | flops | bytes accessed | tf_op | source)
XLA Modules:
  0.0 212.0 jit_solution(1113367826154640194)
XLA Ops:
  0.6 0.0 copy-start
  0.7 6.8 %slabs.1 = bf16[128,128,256]{2,1,0:T(8,128)(2,1)} custom-call(s32[4,128]{1,0:T(4,128)} %bitcast.29, s32[1]{0:T(128)} %bitcast.3.group, bf16[32,256,128]{2,1,0:T(8,128)(2,1)} %integral_ref.1, bf16[32,128,128]{2,1,0:T(8,128)(2,1)} %map_ref.1, s32[128,128]{1,0:T(8,128)} %index_ref.1), custom_call_target="tpu_custom_call" | custom-call | tf_op jit(solution)/shard_map/slabs/pallas_call | solution.py:56
  7.5 106.2 %all_to_all.31 = bf16[32,512,256]{2,1,0:T(8,128)(2,1)} all-to-all(bf16[32,512,256]{2,1,0:T(8,128)(2,1)} %bitcast.27), channel_id=1, replica_groups=mesh['zh'=4,'zl'=2,'yh'=4,'yl'=2,'c'=2,'x'=4] {'zl','yl','c','x'}, dimensions={0} | all-to-all | bytes 16777216 | tf_op jit(solution)/shard_map/all_to_all | solution.py:438
  113.6 6.2 %partial_grams.1 = f32[4,4,272,128]{3,2,1,0:T(8,128)S(1)} custom-call(bf16[8,4,4,128,256]{4,3,2,1,0:T(8,128)(2,1)} %bitcast.26), custom_call_target="tpu_custom_call" | custom-call | tf_op jit(solution)/shard_map/partial_grams/pallas_call | solution.py:143
  119.9 1.1 convert_element_type.9
  121.0 11.1 %all-to-all-start.1 = ((f16[16,272,128]{2,1,0:T(8,128)(2,1)}), f16[16,272,128]{2,1,0:T(8,128)(2,1)S(1)}, u32[]{:S(2)}, u32[]{:S(2)}) async-start(f16[16,272,128]{2,1,0:T(8,128)(2,1)} %bitcast.7), calls=%async_computation.1 | async-start | bytes 2228224 | tf_op jit(solution)/shard_map/all_to_all | solution.py:450
  132.1 0.1 copy.22
  132.2 0.7 collective-permute-start
  132.9 0.2 dynamic-slice_reduce_fusion
  133.1 1.4 gather_fusion.1
  134.5 0.2 sub.17
  134.7 0.2 copy.24
  134.9 0.1 reshape.74.owner_ref
  135.0 3.1 %gather_fusion.2 = f32[512]{0:T(512)S(1)} fusion(f32[25000]{0:T(1024)S(1)} %copy-done, s32[1024]{0:T(1024)S(1)} %pad_clamp_fusion), kind=kCustom, calls=%fused_computation.2 | custom fusion | bytes 6144 | tf_op jit(solution)/shard_map/gather | solution.py:429
  138.2 0.6 gather_fusion
  138.9 0.1 pad_add_fusion.1.place
  138.9 23.8 %all-to-all-done.1 = f16[16,272,128]{2,1,0:T(8,128)(2,1)S(1)} async-done(((f16[16,272,128]{2,1,0:T(8,128)(2,1)}), f16[16,272,128]{2,1,0:T(8,128)(2,1)S(1)}, u32[]{:S(2)}, u32[]{:S(2)}) %all-to-all-start.1) | async-done | bytes 1114144 | tf_op jit(solution)/shard_map/all_to_all | solution.py:450
  162.8 0.2 multiply_reduce_fusion.block_ref
  163.0 1.1 pair_terms.1
  164.1 7.7 %all_to_all.32.parts_ref = bf16[4,144,128]{2,1,0:T(8,128)(2,1)S(1)} all-to-all(bf16[4,144,128]{2,1,0:T(8,128)(2,1)S(1)} %pair_terms.1), channel_id=1, replica_groups=mesh['zh'=4,'zl'=2,'yh'=4,'yl'=2,'c'=2,'x'=4] {'x'}, dimensions={0} | all-to-all | bytes 294912 | tf_op jit(solution)/shard_map/all_to_all | solution.py:456
  171.8 15.3 %all_to_all.33.parts_ref = bf16[4,144,128]{2,1,0:T(8,128)(2,1)S(1)} all-to-all(bf16[4,144,128]{2,1,0:T(8,128)(2,1)S(1)} %plane_terms.1), channel_id=1, replica_groups=mesh['zh'=4,'zl'=2,'yh'=4,'yl'=2,'c'=2,'x'=4] {'yh'}, dimensions={0} | all-to-all | bytes 294912 | tf_op jit(solution)/shard_map/all_to_all | solution.py:458
  187.1 1.4 join_amplitudes.1
  188.5 22.8 %all_to_all.34 = f32[32,4,128]{2,1,0:T(4,128)S(1)} all-to-all(f32[32,4,128]{2,1,0:T(4,128)S(1)} %bitcast.24), channel_id=1, replica_groups=mesh['zh'=4,'zl'=2,'yh'=4,'yl'=2,'c'=2,'x'=4] {'zh','zl','yl','c'}, dimensions={0} | all-to-all | bytes 131072 | tf_op jit(solution)/shard_map/all_to_all | solution.py:462
  211.3 0.8 sum_grads.1
  (21 shorter events, 0.1 us)
Async XLA Ops:
  0.6 134.4 %copy-start = (f32[25000]{0:T(1024)S(1)}, f32[25000]{0:T(1024)}, u32[]{:S(2)}) copy-start(f32[25000]{0:T(1024)} %param.14) | copy-start | bytes 300004
  119.8 12.2 %copy-start.1 = (s32[16,2]{0,1:T(2,128)S(1)}, s32[16,2]{0,1:T(2,128)}, u32[]{:S(2)}) copy-start(s32[16,2]{0,1:T(2,128)} %param.12) | copy-start | bytes 388
  119.8 12.2 %copy-start.4 = (s32[16]{0:T(128)S(1)}, s32[16]{0:T(128)}, u32[]{:S(2)}) copy-start(s32[16]{0:T(128)} %param.13) | copy-start | bytes 196
  119.9 13.0 %copy-start.3 = (s32[128,4]{0,1:T(4,128)S(1)}, s32[128,4]{0,1:T(4,128)}, u32[]{:S(2)}) copy-start(s32[128,4]{0,1:T(4,128)} %param.11) | copy-start | bytes 6148
  121.0 17.2 %copy-start.2 = (f32[128]{0:T(128)S(1)}, f32[128]{0:T(128)}, u32[]{:S(2)}) copy-start(f32[128]{0:T(128)} %param.15) | copy-start | bytes 1540
  121.0 41.7 %all-to-all-start.1 = ((f16[16,272,128]{2,1,0:T(8,128)(2,1)}), f16[16,272,128]{2,1,0:T(8,128)(2,1)S(1)}, u32[]{:S(2)}, u32[]{:S(2)}) async-start(f16[16,272,128]{2,1,0:T(8,128)(2,1)} %bitcast.7), calls=%async_computation.1 | async-start | bytes 2228224 | tf_op jit(solution)/shard_map/all_to_all | solution.py:450
  132.2 30.8 %collective-permute-start = (s32[16,3]{1,0:T(8,128)S(1)}, s32[16,3]{1,0:T(8,128)S(1)}, u32[]{:S(2)}, u32[]{:S(2)}) collective-permute-start(s32[16,3]{1,0:T(8,128)S(1)} %copy.22), channel_id=1, source_target_pairs={{0,0},{1,16},{2,32},{3,48},{16,1},{17,17},{18,33},{19,49},{32,2},{... | collective-permute-start | bytes 584 | tf_op jit(solution)/shard_map/ppermute | solution.py:418

commit v9 on v8

--- a/solution.py
+++ b/solution.py
@@ -458,7 +458,6 @@
     parts = lax.all_to_all(planes, "yh", split_axis=0, concat_axis=0, tiled=True)
     lines = owner_terms(parts, owners)
     amplitude, pair_energy = join_amplitudes(parts, pair_slots.T, place, share)
-    lines, amplitude = lax.optimization_barrier((lines, amplitude))
     all_lines = lax.all_to_all(
         lines, ("zh", "zl", "yl", "c"), split_axis=0, concat_axis=0, tiled=True
     )

time: 212 us -> 210 us (level)
  blocking collectives: 152 us -> 129 us
  starting transfers between devices: 11.7 us -> 24.9 us
  waiting for transfers between devices: 23.8 us -> 30.9 us
    all_to_all x1 -> x0, blocking collectives: 22.8 us -> none  [on_device(): lax.all_to_all(lines, ('zh', 'zl', 'yl', 'c'), split_axis=0, concat_axis=...]
    all_to_all x0 -> x1, starting transfers between devices: none -> 13.2 us  [on_device(): lax.all_to_all(lines, ('zh', 'zl', 'yl', 'c'), split_axis=0, concat_axis=...]
    all_to_all x0 -> x1, waiting for transfers between devices: none -> 6.79 us  [on_device(): lax.all_to_all(lines, ('zh', 'zl', 'yl', 'c'), split_axis=0, concat_axis=...]
  transfers between devices with their start and end apart: 2 -> 3, of which waited for: 1 -> 2; matrix products, arithmetic and copies ran while one was open for 3% -> 3% of each run, Pallas kernels for 0% -> 1%
where the time goes in v9:
time: 210 us
  blocking collectives  129 us (61%)
  waiting for transfers between devices  30.9 us (15%)
  starting transfers between devices  24.9 us (12%)
  Pallas kernels  16.9 us (8%)
  local copies, waits for them, and re-layouts  5.98 us (3%)
    all_to_all x1, blocking collectives, on_device(): lax.all_to_all(outgoing.reshape(members, per_member * width, rows), inner...  106 us
    all_to_all x1, waiting for transfers between devices, on_device(): lax.all_to_all(sent, ('zh', 'yh'), split_axis=0, concat_axis=0, tiled=True)  24.1 us
    all_to_all x1, blocking collectives, on_device(): lax.all_to_all(planes, 'yh', split_axis=0, concat_axis=0, tiled=True)  15.2 us
    all_to_all x1, starting transfers between devices, on_device(): lax.all_to_all(lines, ('zh', 'zl', 'yl', 'c'), split_axis=0, concat_axis=...  13.2 us
    all_to_all x1, starting transfers between devices, on_device(): lax.all_to_all(sent, ('zh', 'yh'), split_axis=0, concat_axis=0, tiled=True)  11.1 us
    all_to_all x1, blocking collectives, on_device(): lax.all_to_all(slices, 'x', split_axis=0, concat_axis=0, tiled=True)  7.54 us
    pallas_call x1, Pallas kernels, make_slabs(): pl.pallas_call(slab_kernel, out_shape=jax.ShapeDtypeStruct((owners, width...  6.83 us
    all_to_all x1, waiting for transfers between devices, on_device(): lax.all_to_all(lines, ('zh', 'zl', 'yl', 'c'), split_axis=0, concat_axis=...  6.79 us
  transfers between devices with their start and end apart: 3, of which 2 were waited for; matrix products, arithmetic and copies ran while one was open for 3% of the time, Pallas kernels for 1%

profile of v9, /device:TPU:1, one launch (start us, length us, event | category | flops | bytes accessed | tf_op | source)
XLA Modules:
  0.0 209.9 jit_solution(2327231255854922953)
XLA Ops:
  0.7 6.8 %slabs.1 = bf16[128,128,256]{2,1,0:T(8,128)(2,1)} custom-call(s32[4,128]{1,0:T(4,128)} %bitcast.28, s32[1]{0:T(128)} %bitcast.2.group, bf16[32,256,128]{2,1,0:T(8,128)(2,1)} %integral_ref.1, bf16[32,128,128]{2,1,0:T(8,128)(2,1)} %map_ref.1, s32[128,128]{1,0:T(8,128)} %index_ref.1), custom_call_target="tpu_custom_call" | custom-call | tf_op jit(solution)/shard_map/slabs/pallas_call | solution.py:56
  7.5 106.1 %all_to_all.31 = bf16[32,512,256]{2,1,0:T(8,128)(2,1)} all-to-all(bf16[32,512,256]{2,1,0:T(8,128)(2,1)} %bitcast.26), channel_id=1, replica_groups=mesh['zh'=4,'zl'=2,'yh'=4,'yl'=2,'c'=2,'x'=4] {'zl','yl','c','x'}, dimensions={0} | all-to-all | bytes 16777216 | tf_op jit(solution)/shard_map/all_to_all | solution.py:438
  113.6 6.2 %partial_grams.1 = f32[4,4,272,128]{3,2,1,0:T(8,128)S(1)} custom-call(bf16[8,4,4,128,256]{4,3,2,1,0:T(8,128)(2,1)} %bitcast.25), custom_call_target="tpu_custom_call" | custom-call | tf_op jit(solution)/shard_map/partial_grams/pallas_call | solution.py:143
  119.9 1.1 convert_element_type.9
  121.0 11.1 %all-to-all-start.1 = ((f16[16,272,128]{2,1,0:T(8,128)(2,1)}), f16[16,272,128]{2,1,0:T(8,128)(2,1)S(1)}, u32[]{:S(2)}, u32[]{:S(2)}) async-start(f16[16,272,128]{2,1,0:T(8,128)(2,1)} %bitcast.8), calls=%async_computation.1 | async-start | bytes 2228224 | tf_op jit(solution)/shard_map/all_to_all | solution.py:450
  132.1 0.1 copy.22
  132.2 0.7 collective-permute-start
  132.9 0.2 dynamic-slice_reduce_fusion
  133.1 1.4 gather_fusion.1
  134.5 0.2 sub.17
  134.7 0.2 copy.24
  134.9 0.1 reshape.74.owner_ref
  135.0 3.1 %gather_fusion.2 = f32[512]{0:T(512)S(1)} fusion(f32[25000]{0:T(1024)S(1)} %copy-done, s32[1024]{0:T(1024)S(1)} %pad_clamp_fusion), kind=kCustom, calls=%fused_computation.2 | custom fusion | bytes 6144 | tf_op jit(solution)/shard_map/gather | solution.py:429
  138.2 0.6 gather_fusion
  138.9 24.1 %all-to-all-done.1 = f16[16,272,128]{2,1,0:T(8,128)(2,1)S(1)} async-done(((f16[16,272,128]{2,1,0:T(8,128)(2,1)}), f16[16,272,128]{2,1,0:T(8,128)(2,1)S(1)}, u32[]{:S(2)}, u32[]{:S(2)}) %all-to-all-start.1) | async-done | bytes 1114144 | tf_op jit(solution)/shard_map/all_to_all | solution.py:450
  163.1 0.2 multiply_reduce_fusion.block_ref
  163.3 1.1 pair_terms.1
  164.4 7.5 %all_to_all.32.parts_ref = bf16[4,144,128]{2,1,0:T(8,128)(2,1)S(1)} all-to-all(bf16[4,144,128]{2,1,0:T(8,128)(2,1)S(1)} %pair_terms.1), channel_id=1, replica_groups=mesh['zh'=4,'zl'=2,'yh'=4,'yl'=2,'c'=2,'x'=4] {'x'}, dimensions={0} | all-to-all | bytes 294912 | tf_op jit(solution)/shard_map/all_to_all | solution.py:456
  172.0 15.2 %all_to_all.33.parts_ref = bf16[4,144,128]{2,1,0:T(8,128)(2,1)S(1)} all-to-all(bf16[4,144,128]{2,1,0:T(8,128)(2,1)S(1)} %plane_terms.1), channel_id=1, replica_groups=mesh['zh'=4,'zl'=2,'yh'=4,'yl'=2,'c'=2,'x'=4] {'yh'}, dimensions={0} | all-to-all | bytes 294912 | tf_op jit(solution)/shard_map/all_to_all | solution.py:458
  187.2 0.6 owner_terms.1
  187.8 13.2 %all-to-all-start.4 = ((f32[32,4,128]{2,1,0:T(4,128)}), f32[32,4,128]{2,1,0:T(4,128)S(1)}, u32[]{:S(2)}, u32[]{:S(2)}) async-start(f32[32,4,128]{2,1,0:T(4,128)} %bitcast.14), calls=%async_computation.4 | async-start | bytes 131072 | tf_op jit(solution)/shard_map/all_to_all | solution.py:461
  201.0 1.4 join_amplitudes.1
  202.3 6.8 %all-to-all-done.4 = f32[32,4,128]{2,1,0:T(4,128)S(1)} async-done(((f32[32,4,128]{2,1,0:T(4,128)}), f32[32,4,128]{2,1,0:T(4,128)S(1)}, u32[]{:S(2)}, u32[]{:S(2)}) %all-to-all-start.4) | async-done | bytes 65568 | tf_op jit(solution)/shard_map/all_to_all | solution.py:461
  209.1 0.8 sum_grads.1
  (22 shorter events, 0.2 us)
Async XLA Ops:
  0.6 134.4 %copy-start = (f32[25000]{0:T(1024)S(1)}, f32[25000]{0:T(1024)}, u32[]{:S(2)}) copy-start(f32[25000]{0:T(1024)} %param.14) | copy-start | bytes 300004
  119.8 12.3 %copy-start.1 = (s32[16,2]{0,1:T(2,128)S(1)}, s32[16,2]{0,1:T(2,128)}, u32[]{:S(2)}) copy-start(s32[16,2]{0,1:T(2,128)} %param.12) | copy-start | bytes 388
  119.8 12.3 %copy-start.4 = (s32[16]{0:T(128)S(1)}, s32[16]{0:T(128)}, u32[]{:S(2)}) copy-start(s32[16]{0:T(128)} %param.13) | copy-start | bytes 196
  119.8 13.0 %copy-start.3 = (s32[128,4]{0,1:T(4,128)S(1)}, s32[128,4]{0,1:T(4,128)}, u32[]{:S(2)}) copy-start(s32[128,4]{0,1:T(4,128)} %param.11) | copy-start | bytes 6148
  121.0 17.2 %copy-start.2 = (f32[128]{0:T(128)S(1)}, f32[128]{0:T(128)}, u32[]{:S(2)}) copy-start(f32[128]{0:T(128)} %param.15) | copy-start | bytes 1540
  121.0 42.1 %all-to-all-start.1 = ((f16[16,272,128]{2,1,0:T(8,128)(2,1)}), f16[16,272,128]{2,1,0:T(8,128)(2,1)S(1)}, u32[]{:S(2)}, u32[]{:S(2)}) async-start(f16[16,272,128]{2,1,0:T(8,128)(2,1)} %bitcast.8), calls=%async_computation.1 | async-start | bytes 2228224 | tf_op jit(solution)/shard_map/all_to_all | solution.py:450
  132.2 31.1 %collective-permute-start = (s32[16,3]{1,0:T(8,128)S(1)}, s32[16,3]{1,0:T(8,128)S(1)}, u32[]{:S(2)}, u32[]{:S(2)}) collective-permute-start(s32[16,3]{1,0:T(8,128)S(1)} %copy.22), channel_id=1, source_target_pairs={{0,0},{1,16},{2,32},{3,48},{16,1},{17,17},{18,33},{19,49},{32,2},{... | collective-permute-start | bytes 584 | tf_op jit(solution)/shard_map/ppermute | solution.py:418
  187.8 21.3 %all-to-all-start.4 = ((f32[32,4,128]{2,1,0:T(4,128)}), f32[32,4,128]{2,1,0:T(4,128)S(1)}, u32[]{:S(2)}, u32[]{:S(2)}) async-start(f32[32,4,128]{2,1,0:T(4,128)} %bitcast.14), calls=%async_computation.4 | async-start | bytes 131072 | tf_op jit(solution)/shard_map/all_to_all | solution.py:461
